TPU v7x, 32 devices: a whole 2x2x4 slice. The times are simulated.
32 devices in a mesh: freq: 8 (over z, x), tile: 4 (over y, core).
Axes of the slice: x: 2, y: 2, z: 4, core: 2. Of those that a mesh axis runs over, the one named last changes fastest.
Arguments:
- sky_cube: float32 [32, 64, 128], P(('freq', 'tile')), may hold values from -6 to 6
- kernel_one: bfloat16 [8, 1, 3, 3, 3], replicated, may hold values from -1.25 to 1.25
- bias_one: float32 [8], replicated, may hold values from -2 to 2
- kernel_two: bfloat16 [8, 8, 3, 3, 3], replicated, may hold values from -0.4375 to 0.4375
- bias_two: float32 [8], replicated, may hold values from -2 to 2
- kernel_three: bfloat16 [16, 8, 3, 3, 3], replicated, may hold values from -0.4375 to 0.4375
- bias_three: float32 [16], replicated, may hold values from -2 to 2
Outputs:
- features: bfloat16 [16, 16, 32, 64], P(None, 'freq', 'tile')
All inputs are finite; a program needn't handle non-finite values.
Results may differ from a plain program's by a relative error of at most 0.0066.
Values may be sent and summed in bfloat16 or wider, within the bound.
No kernel may reach another device: no remote copies, remote signals or barrier semaphores. Data moves between devices by JAX's collectives and lax.ppermute only.
A program may use at most 64 MiB of HBM per device.

v0:
```python
import jax
import jax.numpy as jnp
from jax import lax
from jax.sharding import PartitionSpec as P


def extended_2(cells, sides, width):
    for axis, dim in sides:
        count = lax.axis_size(axis)
        ends = count - 1
        head = lax.slice_in_dim(cells, 0, width, axis=dim)
        tail = lax.slice_in_dim(cells, cells.shape[dim] - width, cells.shape[dim], axis=dim)
        cells = jnp.concatenate(
            [
                lax.ppermute(tail, axis, [(i, (i + 1) % count) for i in range(ends)]),
                cells,
                lax.ppermute(head, axis, [((i + 1) % count, i) for i in range(ends)]),
            ],
            axis=dim,
        )
    return cells


def shortened(shard):

    def short(part):
        return part.astype(jnp.bfloat16) if part.dtype == jnp.float32 else part

    return jax.tree.map(short, shard)


def from_behind(shard, axis, by):
    devices = lax.axis_size(axis)
    pairs = [(i, i + by) for i in range(devices) if 0 <= i + by < devices]
    return lax.ppermute(shard, axis, pairs)


def leaky_relu(values):
    return jnp.maximum(values, 0.1 * values)


def conv_layer(volume, kernel, bias_term):
    depth = volume.shape[1] - 2
    blocks = []
    for begin_at in range(0, depth, 4):
        count = min(4, depth - begin_at)
        section = volume[:, begin_at : begin_at + count + 2]
        values = lax.conv_general_dilated(
            section[None],
            kernel,
            (1, 1, 1),
            ((0, 0), (0, 0), (1, 1)),
            dimension_numbers=("NCDHW", "OIDHW", "NCDHW"),
            preferred_element_type=jnp.float32,
        )[0]
        values = leaky_relu(values + bias_term[:, None, None, None])
        blocks.append(values.astype(jnp.bfloat16))
    return jnp.concatenate(blocks, axis=1)


def body(sky_cube, kernel_one, bias_one, kernel_two, bias_two, kernel_three, bias_three):
    slab = lax.all_to_all(
        sky_cube.astype(jnp.bfloat16), "tile", split_axis=1, concat_axis=0, tiled=True
    )
    widened = extended_2(slab, (("freq", 0), ("tile", 1)), 1)
    layer_one = conv_layer(widened[None], kernel_one, bias_one)
    widened = extended_2(layer_one, (("freq", 1), ("tile", 2)), 1)
    layer_two = conv_layer(widened, kernel_two, bias_two)
    lower_rows = from_behind(shortened(layer_two[:, :, -1:, :]), "tile", 1)
    extended = jnp.concatenate([lower_rows, layer_two], axis=2)
    lower_planes = from_behind(shortened(extended[:, -1:]), "freq", 1)
    extended = jnp.concatenate([lower_planes, extended], axis=1)
    values = lax.conv_general_dilated(
        extended[None],
        kernel_three,
        (2, 2, 2),
        ((0, 0), (0, 0), (1, 1)),
        dimension_numbers=("NCDHW", "OIDHW", "NCDHW"),
        preferred_element_type=jnp.float32,
    )[0]
    return leaky_relu(values + bias_three[:, None, None, None]).astype(jnp.bfloat16)


def solution(mesh):
    return jax.shard_map(
        body,
        mesh=mesh,
        in_specs=(P(("freq", "tile"), None, None), P(), P(), P(), P(), P(), P()),
        out_specs=P(None, "freq", "tile", None),
        check_vma=False,
    )
```

profile of v0, /device:TPU:0, one launch (start us, length us, event | category | flops | bytes accessed | tf_op | source)
XLA Modules:
  0.0 107.5 jit_solution(10686314246774161173)
XLA Ops:
  0.0 0.8 convert_element_type.12
  0.8 0.5 broadcast.51
  1.3 0.7 reduce
  2.1 7.9 %all_to_all.15 = bf16[4,2,1024]{2,1,0:T(2,128)(2,1)S(1)} all-to-all(bf16[4,2,1024]{2,1,0:T(2,128)(2,1)S(1)} %reshape.44), channel_id=1, replica_groups=mesh['freq'=8,'tile'=4] {'tile'}, dimensions={0} | all-to-all | bytes 32768 | tf_op jit(solution)/shard_map/all_to_all | solution.py:62
  10.0 3.4 %collective-permute-start = (bf16[1,16,128]{2,1,0:T(8,128)(2,1)S(1)}, bf16[1,16,128]{2,1,0:T(8,128)(2,1)S(1)}, u32[]{:S(2)}, u32[]{:S(2)}) collective-permute-start(bf16[1,16,128]{2,1,0:T(8,128)(2,1)S(1)} %slice_bitcast_fusion.2), channel_id=1, source_target_pairs={{0,4},{4,8},{8,12},{12,16},{16,20},{20,24},{24,28},{1,5},{5,9},{9,... | collective-permute-start | bytes 12296 | tf_op jit(solution)/shard_map/ppermute | solution.py:15
  13.4 1.3 %collective-permute-start.1 = (bf16[1,16,128]{2,1,0:T(8,128)(2,1)S(1)}, bf16[1,16,128]{2,1,0:T(8,128)(2,1)S(1)}, u32[]{:S(2)}, u32[]{:S(2)}) collective-permute-start(bf16[1,16,128]{2,1,0:T(8,128)(2,1)S(1)} %copy.73), channel_id=1, source_target_pairs={{4,0},{8,4},{12,8},{16,12},{20,16},{24,20},{28,24},{5,1},{9,5},{13... | collective-permute-start | bytes 12296 | tf_op jit(solution)/shard_map/ppermute | solution.py:17
  14.7 0.0 collective-permute-done
  14.8 4.2 %collective-permute-done.1 = bf16[1,16,128]{2,1,0:T(8,128)(2,1)S(1)} collective-permute-done((bf16[1,16,128]{2,1,0:T(8,128)(2,1)S(1)}, bf16[1,16,128]{2,1,0:T(8,128)(2,1)S(1)}, u32[]{:S(2)}, u32[]{:S(2)}) %collective-permute-start.1) | collective-permute-done | bytes 4128 | tf_op jit(solution)/shard_map/ppermute | solution.py:17
  19.0 1.3 %collective-permute-start.2 = (bf16[6,1,128]{2,1,0:T(2,128)(2,1)S(1)}, bf16[6,1,128]{2,1,0:T(2,128)(2,1)S(1)}, u32[]{:S(2)}, u32[]{:S(2)}) collective-permute-start(bf16[6,1,128]{2,1,0:T(2,128)(2,1)S(1)} %get-tuple-element.9), channel_id=1, source_target_pairs={{0,1},{1,2},{2,3},{4,5},{5,6},{6,7},{8,9},{9,10},{10,11},{12,13},{... | collective-permute-start | bytes 4616 | tf_op jit(solution)/shard_map/ppermute | solution.py:15
  20.3 1.3 %collective-permute-start.3 = (bf16[6,1,128]{2,1,0:T(2,128)(2,1)S(1)}, bf16[6,1,128]{2,1,0:T(2,128)(2,1)S(1)}, u32[]{:S(2)}, u32[]{:S(2)}) collective-permute-start(bf16[6,1,128]{2,1,0:T(2,128)(2,1)S(1)} %get-tuple-element.10), channel_id=1, source_target_pairs={{1,0},{2,1},{3,2},{5,4},{6,5},{7,6},{9,8},{10,9},{11,10},{13,12},{... | collective-permute-start | bytes 4616 | tf_op jit(solution)/shard_map/ppermute | solution.py:17
  21.6 2.0 %collective-permute-done.3 = bf16[6,1,128]{2,1,0:T(2,128)(2,1)S(1)} collective-permute-done((bf16[6,1,128]{2,1,0:T(2,128)(2,1)S(1)}, bf16[6,1,128]{2,1,0:T(2,128)(2,1)S(1)}, u32[]{:S(2)}, u32[]{:S(2)}) %collective-permute-start.3) | collective-permute-done | bytes 1568 | tf_op jit(solution)/shard_map/ppermute | solution.py:17
  23.6 0.1 pad
  23.7 0.2 reshape.10
  23.9 0.1 slice.53
  23.9 0.2 fusion.26
  24.1 1.7 %copy.61 = bf16[1,6,18,8,19]{3,0,4,2,1:T(2,128)(2,1)S(1)} copy(bf16[1,6,18,8,19]{4,3,2,1,0:T(8,128)(2,1)S(1)} %fusion.26) | data formatting | bytes 65664 | tf_op jit(solution)/shard_map/conv_general_dilated | solution.py:48
  25.8 9.5 %broadcast_select_fusion.1 = f32[4,16,8,17,8]{4,2,3,1,0:T(8,128)} fusion(pred[8,17]{0,1:T(8,128)(4,1)} %constant.17, bf16[1,6,18,8,19]{3,0,4,2,1:T(2,128)(2,1)S(1)} %copy.61, bf16[8,1,3,3,3]{0,4,3,2,1:T(4,128)(2,1)} %param.8), kind=kOutput, calls=%fused_computation.14 | convolution fusion | flops 3829760 | bytes 311928 | tf_op jit(solution)/shard_map/conv_general_dilated | solution.py:48
  35.2 5.2 %copy.63 = f32[4,16,8,17,8]{3,2,4,1,0:T(8,128)S(1)} copy(f32[4,16,8,17,8]{4,2,3,1,0:T(8,128)} %broadcast_select_fusion.1) | data formatting | bytes 557056 | tf_op jit(solution)/shard_map/conv_general_dilated | solution.py:48
  40.4 0.6 reshape.14
  41.0 0.1 fusion.21
  41.2 4.4 %collective-permute-start.4 = (bf16[8,1,16,128]{3,0,2,1:T(8,128)(2,1)S(1)}, bf16[8,1,16,128]{3,0,2,1:T(8,128)(2,1)S(1)}, u32[]{:S(2)}, u32[]{:S(2)}) collective-permute-start(bf16[8,1,16,128]{3,0,2,1:T(8,128)(2,1)S(1)} %get-tuple-element.7), channel_id=1, source_target_pairs={{0,4},{4,8},{8,12},{12,16},{16,20},{20,24},{24,28},{1,5},{5,9},{9,... | collective-permute-start | bytes 98312 | tf_op jit(solution)/shard_map/ppermute | solution.py:15
  45.5 1.3 %collective-permute-start.5 = (bf16[8,1,16,128]{3,0,2,1:T(8,128)(2,1)S(1)}, bf16[8,1,16,128]{3,0,2,1:T(8,128)(2,1)S(1)}, u32[]{:S(2)}, u32[]{:S(2)}) collective-permute-start(bf16[8,1,16,128]{3,0,2,1:T(8,128)(2,1)S(1)} %get-tuple-element.8), channel_id=1, source_target_pairs={{4,0},{8,4},{12,8},{16,12},{20,16},{24,20},{28,24},{5,1},{9,5},{13... | collective-permute-start | bytes 98312 | tf_op jit(solution)/shard_map/ppermute | solution.py:17
  46.8 0.3 collective-permute-done.4
  47.1 4.2 %collective-permute-done.5 = bf16[8,1,16,128]{3,0,2,1:T(8,128)(2,1)S(1)} collective-permute-done((bf16[8,1,16,128]{3,0,2,1:T(8,128)(2,1)S(1)}, bf16[8,1,16,128]{3,0,2,1:T(8,128)(2,1)S(1)}, u32[]{:S(2)}, u32[]{:S(2)}) %collective-permute-start.5) | collective-permute-done | bytes 32800 | tf_op jit(solution)/shard_map/ppermute | solution.py:17
  51.3 2.8 %collective-permute-start.6 = (bf16[8,6,1,128]{3,0,2,1:T(8,128)(2,1)S(1)}, bf16[8,6,1,128]{3,0,2,1:T(8,128)(2,1)S(1)}, u32[]{:S(2)}, u32[]{:S(2)}) collective-permute-start(bf16[8,6,1,128]{3,0,2,1:T(8,128)(2,1)S(1)} %get-tuple-element.5), channel_id=1, source_target_pairs={{0,1},{1,2},{2,3},{4,5},{5,6},{6,7},{8,9},{9,10},{10,11},{12,13},{... | collective-permute-start | bytes 36872 | tf_op jit(solution)/shard_map/ppermute | solution.py:15
  54.2 1.5 %collective-permute-start.7 = (bf16[8,6,1,128]{3,0,2,1:T(8,128)(2,1)S(1)}, bf16[8,6,1,128]{3,0,2,1:T(8,128)(2,1)S(1)}, u32[]{:S(2)}, u32[]{:S(2)}) collective-permute-start(bf16[8,6,1,128]{3,0,2,1:T(8,128)(2,1)S(1)} %get-tuple-element.6), channel_id=1, source_target_pairs={{1,0},{2,1},{3,2},{5,4},{6,5},{7,6},{9,8},{10,9},{11,10},{13,12},{... | collective-permute-start | bytes 36872 | tf_op jit(solution)/shard_map/ppermute | solution.py:17
  55.7 2.6 %collective-permute-done.7 = bf16[8,6,1,128]{3,0,2,1:T(8,128)(2,1)S(1)} collective-permute-done((bf16[8,6,1,128]{3,0,2,1:T(8,128)(2,1)S(1)}, bf16[8,6,1,128]{3,0,2,1:T(8,128)(2,1)S(1)}, u32[]{:S(2)}, u32[]{:S(2)}) %collective-permute-start.7) | collective-permute-done | bytes 12320 | tf_op jit(solution)/shard_map/ppermute | solution.py:17
  58.3 0.2 pad.2
  58.5 0.0 copy-start.5
  58.5 1.3 %reshape.17 = bf16[8,6,18,1,8,17]{5,4,0,2,1,3:T(8,128)(2,1)S(1)} reshape(bf16[8,6,18,1,136]{4,0,2,1,3:T(8,128)(2,1)S(1)} %pad.2) | data formatting | bytes 470016 | tf_op jit(solution)/shard_map/conv_general_dilated | solution.py:48
  59.8 6.6 %copy.65 = bf16[8,6,18,1,8,17]{0,4,5,2,1,3:T(8,128)(2,1)} copy(bf16[8,6,18,1,8,17]{5,4,0,2,1,3:T(8,128)(2,1)S(1)} %reshape.17) | data formatting | bytes 470016 | tf_op jit(solution)/shard_map/conv_general_dilated | solution.py:48
  66.5 1.1 %slice.57 = bf16[8,6,18,1,7,2]{0,4,5,2,1,3:T(8,128)(2,1)S(1)} slice(bf16[8,6,18,1,8,17]{0,4,5,2,1,3:T(8,128)(2,1)} %copy.65), slice={[0:8], [0:6], [0:18], [0:1], [1:8], [0:2]} | slice | bytes 48384 | tf_op jit(solution)/shard_map/conv_general_dilated | solution.py:48
  67.6 9.7 %broadcast_select_fusion = f32[4,16,8,17,8]{4,2,3,1,0:T(8,128)} fusion(pred[8,17]{0,1:T(8,128)(4,1)S(1)} %copy-done.5, bf16[8,8,3,3,3]{1,0,4,3,2:T(8,128)(2,1)S(1)} %copy-done, bf16[8,6,18,1,7,2]{0,4,5,2,1,3:T(8,128)(2,1)S(1)} %slice.57, bf16[8,6,18,1,8,17]{0,4,5,2,1,3:T(8,128)(2,1)} %copy.65), kind=kOutput, calls=%fused_computation.13 | convolution fusion | flops 30938624 | bytes 541320 | tf_op jit(solution)/shard_map/conv_general_dilated | solution.py:48
  77.4 5.2 %copy.66 = f32[4,16,8,17,8]{3,2,4,1,0:T(8,128)S(1)} copy(f32[4,16,8,17,8]{4,2,3,1,0:T(8,128)} %broadcast_select_fusion) | data formatting | bytes 557056 | tf_op jit(solution)/shard_map/conv_general_dilated | solution.py:48
  82.6 0.6 reshape.21
  83.2 0.1 fusion.22
  83.3 4.3 %collective-permute-start.8 = (bf16[8,4,1,128]{3,0,2,1:T(8,128)(2,1)S(1)}, bf16[8,4,1,128]{3,0,2,1:T(8,128)(2,1)S(1)}, u32[]{:S(2)}, u32[]{:S(2)}) collective-permute-start(bf16[8,4,1,128]{3,0,2,1:T(8,128)(2,1)S(1)} %slice.59), channel_id=1, source_target_pairs={{0,1},{1,2},{2,3},{4,5},{5,6},{6,7},{8,9},{9,10},{10,11},{12,13},{... | collective-permute-start | bytes 24584 | tf_op jit(solution)/shard_map/ppermute | solution.py:35
  87.7 0.8 collective-permute-done.8
  88.5 3.4 %collective-permute-start.9 = (bf16[8,1,17,128]{3,0,2,1:T(8,128)(2,1)S(1)}, bf16[8,1,17,128]{3,0,2,1:T(8,128)(2,1)S(1)}, u32[]{:S(2)}, u32[]{:S(2)}) collective-permute-start(bf16[8,1,17,128]{3,0,2,1:T(8,128)(2,1)S(1)} %pad_maximum_fusion), channel_id=1, source_target_pairs={{0,4},{4,8},{8,12},{12,16},{16,20},{20,24},{24,28},{1,5},{5,9},{9,... | collective-permute-start | bytes 104456 | tf_op jit(solution)/shard_map/ppermute | solution.py:35
  91.9 1.6 %collective-permute-done.9 = bf16[8,1,17,128]{3,0,2,1:T(8,128)(2,1)S(1)} collective-permute-done((bf16[8,1,17,128]{3,0,2,1:T(8,128)(2,1)S(1)}, bf16[8,1,17,128]{3,0,2,1:T(8,128)(2,1)S(1)}, u32[]{:S(2)}, u32[]{:S(2)}) %collective-permute-start.9) | collective-permute-done | bytes 34848 | tf_op jit(solution)/shard_map/ppermute | solution.py:35
  93.5 0.2 pad.4
  93.7 1.0 reshape.24
  94.7 6.3 %copy.68 = bf16[8,5,17,1,8,18]{0,4,5,2,1,3:T(8,128)(2,1)} copy(bf16[8,5,17,1,8,18]{5,4,0,2,1,3:T(8,128)(2,1)S(1)} %reshape.24) | data formatting | bytes 391680 | tf_op jit(solution)/shard_map/conv_general_dilated | solution.py:73
  101.0 1.1 %slice.60 = bf16[8,5,17,1,7,2]{0,4,5,2,1,3:T(8,128)(2,1)S(1)} slice(bf16[8,5,17,1,8,18]{0,4,5,2,1,3:T(8,128)(2,1)} %copy.68), slice={[0:8], [0:5], [0:17], [0:1], [1:8], [0:2]} | slice | bytes 38080 | tf_op jit(solution)/shard_map/conv_general_dilated | solution.py:73
  102.1 4.3 %fusion.17 = f32[2,8,8,9,16]{4,2,3,1,0:T(8,128)S(1)} fusion(bf16[16,8,3,3,3]{0,1,4,3,2:T(8,128)(2,1)S(1)} %copy-done.4, bf16[8,5,17,1,7,2]{0,4,5,2,1,3:T(8,128)(2,1)S(1)} %slice.60, bf16[8,5,17,1,8,18]{0,4,5,2,1,3:T(8,128)(2,1)} %copy.68, pred[8,9]{0,1:T(8,128)(4,1)S(1)} %copy-done.6), kind=kOutput, calls=%fused_computation.17 | convolution fusion | flops 8633856 | bytes 295592 | tf_op jit(solution)/shard_map/conv_general_dilated | solution.py:73
  106.4 0.1 copy.69
  106.6 0.2 copy.74
  106.8 0.7 fusion.27
  (31 shorter events, 0.3 us)
Async XLA Ops:
  0.0 67.6 %copy-start = (bf16[8,8,3,3,3]{1,0,4,3,2:T(8,128)(2,1)S(1)}, bf16[8,8,3,3,3]{1,0,4,3,2:T(8,128)(2,1)}, u32[]{:S(2)}) copy-start(bf16[8,8,3,3,3]{1,0,4,3,2:T(8,128)(2,1)} %param.10) | copy-start | bytes 10372
  10.0 4.7 %collective-permute-start = (bf16[1,16,128]{2,1,0:T(8,128)(2,1)S(1)}, bf16[1,16,128]{2,1,0:T(8,128)(2,1)S(1)}, u32[]{:S(2)}, u32[]{:S(2)}) collective-permute-start(bf16[1,16,128]{2,1,0:T(8,128)(2,1)S(1)} %slice_bitcast_fusion.2), channel_id=1, source_target_pairs={{0,4},{4,8},{8,12},{12,16},{16,20},{20,24},{24,28},{1,5},{5,9},{9,... | collective-permute-start | bytes 12296 | tf_op jit(solution)/shard_map/ppermute | solution.py:15
  13.4 5.5 %collective-permute-start.1 = (bf16[1,16,128]{2,1,0:T(8,128)(2,1)S(1)}, bf16[1,16,128]{2,1,0:T(8,128)(2,1)S(1)}, u32[]{:S(2)}, u32[]{:S(2)}) collective-permute-start(bf16[1,16,128]{2,1,0:T(8,128)(2,1)S(1)} %copy.73), channel_id=1, source_target_pairs={{4,0},{8,4},{12,8},{16,12},{20,16},{24,20},{28,24},{5,1},{9,5},{13... | collective-permute-start | bytes 12296 | tf_op jit(solution)/shard_map/ppermute | solution.py:17
  19.0 2.6 %collective-permute-start.2 = (bf16[6,1,128]{2,1,0:T(2,128)(2,1)S(1)}, bf16[6,1,128]{2,1,0:T(2,128)(2,1)S(1)}, u32[]{:S(2)}, u32[]{:S(2)}) collective-permute-start(bf16[6,1,128]{2,1,0:T(2,128)(2,1)S(1)} %get-tuple-element.9), channel_id=1, source_target_pairs={{0,1},{1,2},{2,3},{4,5},{5,6},{6,7},{8,9},{9,10},{10,11},{12,13},{... | collective-permute-start | bytes 4616 | tf_op jit(solution)/shard_map/ppermute | solution.py:15
  20.3 3.3 %collective-permute-start.3 = (bf16[6,1,128]{2,1,0:T(2,128)(2,1)S(1)}, bf16[6,1,128]{2,1,0:T(2,128)(2,1)S(1)}, u32[]{:S(2)}, u32[]{:S(2)}) collective-permute-start(bf16[6,1,128]{2,1,0:T(2,128)(2,1)S(1)} %get-tuple-element.10), channel_id=1, source_target_pairs={{1,0},{2,1},{3,2},{5,4},{6,5},{7,6},{9,8},{10,9},{11,10},{13,12},{... | collective-permute-start | bytes 4616 | tf_op jit(solution)/shard_map/ppermute | solution.py:17
  35.2 5.8 %copy-start.1 = (f32[8]{0:T(128)S(1)}, f32[8]{0:T(128)}, u32[]{:S(2)}) copy-start(f32[8]{0:T(128)} %param.9) | copy-start | bytes 100
  41.2 5.9 %collective-permute-start.4 = (bf16[8,1,16,128]{3,0,2,1:T(8,128)(2,1)S(1)}, bf16[8,1,16,128]{3,0,2,1:T(8,128)(2,1)S(1)}, u32[]{:S(2)}, u32[]{:S(2)}) collective-permute-start(bf16[8,1,16,128]{3,0,2,1:T(8,128)(2,1)S(1)} %get-tuple-element.7), channel_id=1, source_target_pairs={{0,4},{4,8},{8,12},{12,16},{16,20},{20,24},{24,28},{1,5},{5,9},{9,... | collective-permute-start | bytes 98312 | tf_op jit(solution)/shard_map/ppermute | solution.py:15
  45.5 5.8 %collective-permute-start.5 = (bf16[8,1,16,128]{3,0,2,1:T(8,128)(2,1)S(1)}, bf16[8,1,16,128]{3,0,2,1:T(8,128)(2,1)S(1)}, u32[]{:S(2)}, u32[]{:S(2)}) collective-permute-start(bf16[8,1,16,128]{3,0,2,1:T(8,128)(2,1)S(1)} %get-tuple-element.8), channel_id=1, source_target_pairs={{4,0},{8,4},{12,8},{16,12},{20,16},{24,20},{28,24},{5,1},{9,5},{13... | collective-permute-start | bytes 98312 | tf_op jit(solution)/shard_map/ppermute | solution.py:17
  51.3 4.3 %collective-permute-start.6 = (bf16[8,6,1,128]{3,0,2,1:T(8,128)(2,1)S(1)}, bf16[8,6,1,128]{3,0,2,1:T(8,128)(2,1)S(1)}, u32[]{:S(2)}, u32[]{:S(2)}) collective-permute-start(bf16[8,6,1,128]{3,0,2,1:T(8,128)(2,1)S(1)} %get-tuple-element.5), channel_id=1, source_target_pairs={{0,1},{1,2},{2,3},{4,5},{5,6},{6,7},{8,9},{9,10},{10,11},{12,13},{... | collective-permute-start | bytes 36872 | tf_op jit(solution)/shard_map/ppermute | solution.py:15
  54.2 4.0 %collective-permute-start.7 = (bf16[8,6,1,128]{3,0,2,1:T(8,128)(2,1)S(1)}, bf16[8,6,1,128]{3,0,2,1:T(8,128)(2,1)S(1)}, u32[]{:S(2)}, u32[]{:S(2)}) collective-permute-start(bf16[8,6,1,128]{3,0,2,1:T(8,128)(2,1)S(1)} %get-tuple-element.6), channel_id=1, source_target_pairs={{1,0},{2,1},{3,2},{5,4},{6,5},{7,6},{9,8},{10,9},{11,10},{13,12},{... | collective-permute-start | bytes 36872 | tf_op jit(solution)/shard_map/ppermute | solution.py:17
  58.5 9.1 %copy-start.5 = (pred[8,17]{0,1:T(8,128)(4,1)S(1)}, pred[8,17]{0,1:T(8,128)(4,1)}, u32[]{:S(2)}) copy-start(pred[8,17]{0,1:T(8,128)(4,1)} %constant.17) | copy-start | bytes 412
  77.4 5.8 %copy-start.2 = (f32[8]{0:T(128)S(1)}, f32[8]{0:T(128)}, u32[]{:S(2)}) copy-start(f32[8]{0:T(128)} %param.11) | copy-start | bytes 100
  83.2 18.9 %copy-start.4 = (bf16[16,8,3,3,3]{0,1,4,3,2:T(8,128)(2,1)S(1)}, bf16[16,8,3,3,3]{0,1,4,3,2:T(8,128)(2,1)}, u32[]{:S(2)}) copy-start(bf16[16,8,3,3,3]{0,1,4,3,2:T(8,128)(2,1)} %param.12) | copy-start | bytes 20740
  83.2 18.9 %copy-start.6 = (pred[8,9]{0,1:T(8,128)(4,1)S(1)}, pred[8,9]{0,1:T(8,128)(4,1)}, u32[]{:S(2)}) copy-start(pred[8,9]{0,1:T(8,128)(4,1)} %constant.16) | copy-start | bytes 220
  83.3 5.2 %collective-permute-start.8 = (bf16[8,4,1,128]{3,0,2,1:T(8,128)(2,1)S(1)}, bf16[8,4,1,128]{3,0,2,1:T(8,128)(2,1)S(1)}, u32[]{:S(2)}, u32[]{:S(2)}) collective-permute-start(bf16[8,4,1,128]{3,0,2,1:T(8,128)(2,1)S(1)} %slice.59), channel_id=1, source_target_pairs={{0,1},{1,2},{2,3},{4,5},{5,6},{6,7},{8,9},{9,10},{10,11},{12,13},{... | collective-permute-start | bytes 24584 | tf_op jit(solution)/shard_map/ppermute | solution.py:35
  88.5 5.0 %collective-permute-start.9 = (bf16[8,1,17,128]{3,0,2,1:T(8,128)(2,1)S(1)}, bf16[8,1,17,128]{3,0,2,1:T(8,128)(2,1)S(1)}, u32[]{:S(2)}, u32[]{:S(2)}) collective-permute-start(bf16[8,1,17,128]{3,0,2,1:T(8,128)(2,1)S(1)} %pad_maximum_fusion), channel_id=1, source_target_pairs={{0,4},{4,8},{8,12},{12,16},{16,20},{20,24},{24,28},{1,5},{5,9},{9,... | collective-permute-start | bytes 104456 | tf_op jit(solution)/shard_map/ppermute | solution.py:35
  102.1 4.7 %copy-start.3 = (f32[16]{0:T(128)S(1)}, f32[16]{0:T(128)}, u32[]{:S(2)}) copy-start(f32[16]{0:T(128)} %param.13) | copy-start | bytes 196
where the time goes:
time: 109 us; the launch traced here: 108 us
  local copies, waits for them, and re-layouts  32.4 us (30%)
  starting transfers between devices  25 us (23%)
  matrix products  23.5 us (22%)
  waiting for transfers between devices  15.7 us (14%)
  blocking collectives  7.9 us (7%)
  other arithmetic  2.69 us (2%)
    conv_general_dilated x10, local copies, waits for them, and re-layouts, conv_layer(): lax.conv_general_dilated(section[None], kernel, (1, 1, 1), ((0, 0), (0, 0...  22.6 us
    conv_general_dilated x2, matrix products, conv_layer(): lax.conv_general_dilated(section[None], kernel, (1, 1, 1), ((0, 0), (0, 0...  19.2 us
    ppermute x4, waiting for transfers between devices, extended_2(): lax.ppermute(head, axis, [((i + 1) % count, i) for i in range(ends)])  13 us
    ppermute x4, starting transfers between devices, extended_2(): lax.ppermute(tail, axis, [(i, (i + 1) % count) for i in range(ends)])  11.9 us
    conv_general_dilated x5, local copies, waits for them, and re-layouts, body(): lax.conv_general_dilated(extended[None], kernel_three, (2, 2, 2), ((0, 0)...  8.55 us
    all_to_all x1, blocking collectives, body(): lax.all_to_all(sky_cube.astype(jnp.bfloat16), 'tile', split_axis=1, conca...  7.9 us
    ppermute x2, starting transfers between devices, from_behind(): return lax.ppermute(shard, axis, pairs)  7.73 us
    ppermute x4, starting transfers between devices, extended_2(): lax.ppermute(head, axis, [((i + 1) % count, i) for i in range(ends)])  5.35 us
  transfers between devices with their start and end apart: 10, of which 7 were waited for; matrix products, arithmetic and copies ran while one was open for 0% of the time, Pallas kernels for 0%

commit v1 on v0

v1 whole, which is shorter than its diff:
```python
import functools

import jax
import jax.numpy as jnp
from jax import lax
from jax.experimental import pallas as pl
from jax.experimental.pallas import tpu as pltpu
from jax.sharding import PartitionSpec as P

BF = jnp.bfloat16
F32 = jnp.float32
VM = pl.BlockSpec(memory_space=pltpu.VMEM)
SM = pl.BlockSpec(memory_space=pltpu.SMEM)


def even(n):
    return n + n % 2


def up_to(n, unit):
    return -(-n // unit) * unit


class Plan:
    def __init__(self, strip, c1, c2, c3):
        self.strip, self.c1, self.c2, self.c3 = strip, c1, c2, c3
        self.slots = strip + 8
        self.plane_k = up_to(3 * self.slots, 16)
        self.k1 = up_to(3 * self.plane_k, 256)
        self.r1 = even(strip + 3)
        self.r2 = even(strip + 1)
        self.r3 = strip // 2
        self.k2 = up_to(3 * self.r1 * c1, 256)
        self.k3 = up_to(3 * self.r2 * c2, 256)


def leaky_relu(values):
    return jnp.maximum(values, 0.1 * values)


def column_of(bias_ref, rows, lanes):
    at = lax.broadcasted_iota(jnp.int32, (rows, lanes), 0)
    out = jnp.zeros((rows, lanes), F32)
    for o in range(rows):
        out = jnp.where(at == o, bias_ref[o], out)
    return out


def bands_kernel(plan, bias1, bias2, bias3, base1, base2, base3, t1, t2, t3, b1, b2, b3):
    c1, c2, c3 = plan.c1, plan.c2, plan.c3
    slots = plan.slots
    b1[...] = column_of(bias1, c1, 128)
    b2[...] = column_of(bias2, c2, 128)
    lanes = lax.broadcasted_iota(jnp.int32, (c1, plan.k1), 1)
    slot = lax.rem(lax.rem(lanes, plan.plane_k), slots)
    taps = [jnp.where(slot == b, base1[...], 0.0) for b in range(3)]

    def rolled(x, by):
        return pltpu.roll(x, by, 1) if by else x

    def tap_at(b, to):
        return rolled(taps[b], (to - b) % plan.k1)

    for y in range(0, plan.r1, 2):
        rows = [sum(tap_at(b, (row - 3 + b) % slots) for b in range(3)) for row in (y, y + 1)]
        t1[y * c1 : (y + 2) * c1, :] = jnp.concatenate(rows, axis=0).astype(BF)
    for a in range(3):
        base = base2[a]
        for y in range(0, plan.r2, 2):
            rows = [rolled(base, (y + k) * c1) for k in range(2)]
            t2[a, y * c2 : (y + 2) * c2, :] = jnp.concatenate(rows, axis=0).astype(BF)
    n3 = plan.r3 * c3
    row = lax.broadcasted_iota(jnp.int32, (n3, n3), 0)
    col = lax.broadcasted_iota(jnp.int32, (n3, n3), 1)
    turn = ((row // plan.r3 == col % c3) & (row % plan.r3 == col // c3)).astype(F32).astype(BF)
    for a in range(3):
        base = base3[a]
        rows = [rolled(base, 2 * y * c2) for y in range(plan.r3)]
        stacked = jnp.concatenate(rows, axis=0).astype(BF)
        t3[a] = jnp.dot(turn, stacked, preferred_element_type=F32).astype(BF)
    for o in range(c3):
        b3[o * plan.r3 : (o + 1) * plan.r3, :] = jnp.full((plan.r3, 128), bias3[o], F32)


def layers_kernel(plan, depth, own, got, other, t1, t2, t3, b1, b2, b3, out, x2, x3):
    freq, tile = lax.axis_index("freq"), lax.axis_index("tile")
    last_group, last_strip = lax.axis_size("freq") - 1, lax.axis_size("tile") - 1
    strip, c1, c2 = plan.strip, plan.c1, plan.c2
    here = pl.multiple_of(tile * strip, 16)
    above = pl.multiple_of(jnp.maximum(tile - 1, 0) * strip + strip - 16, 16)
    below = pl.multiple_of(jnp.minimum(tile + 1, last_strip) * strip, 16)
    has_above, has_below = tile > 0, tile < last_strip
    has_lower, has_upper = freq > 0, freq < last_group
    upward = lax.rem(tile, 2) == 0

    sub = lax.broadcasted_iota(jnp.int32, (8, 128), 0)
    rim_keep = ((sub < 4) & has_below) | ((sub >= 4) & has_above)

    def lane_of(rows):
        return lax.broadcasted_iota(jnp.int32, (rows, 128), 1)

    def window(ref, plane):
        middle = ref[plane, pl.ds(here, strip), :].astype(F32)
        rim_above = ref[plane, pl.ds(above, 16), :].astype(F32)[8:]
        rim_below = ref[plane, pl.ds(below, 16), :].astype(F32)[:8]
        rim = jnp.where(rim_keep, jnp.where(sub < 4, rim_below, rim_above), 0.0)
        return jnp.concatenate([middle, rim], axis=0)

    def shifted(x):
        lane = lane_of(x.shape[0])
        return (
            jnp.where(lane == 0, 0.0, pltpu.roll(x, 1, 1)),
            x,
            jnp.where(lane == 127, 0.0, pltpu.roll(x, 127, 1)),
        )

    slab = []
    for p in range(depth - 3, depth):
        rows = jnp.where(upward, window(got, p), window(other, p))
        slab.append(jnp.where(has_lower, rows, 0.0))
    for p in range(depth):
        slab.append(window(own, p))
    for p in range(2):
        rows = jnp.where(upward, window(other, p), window(got, p))
        slab.append(jnp.where(has_upper, rows, 0.0))
    pad = jnp.zeros((plan.plane_k - 3 * plan.slots, 128), F32)
    pieces = [jnp.concatenate([*shifted(rows), pad], axis=0).astype(BF) for rows in slab]

    k1_pad = jnp.zeros((plan.k1 - 3 * plan.plane_k, 128), BF)
    n1, n2 = plan.r1 * c1, plan.r2 * c2
    planes1, planes2 = depth + 3, depth + 1
    x2[3 * n1 :, :] = jnp.zeros((plan.k2 - 3 * n1, planes1 * 128), BF)
    x3[3 * n2 :, :] = jnp.zeros((plan.k3 - 3 * n2, planes2 * 128), BF)

    def chunks(count):
        return [range(p, min(p + 2, count)) for p in range(0, count, 2)]

    for chunk in chunks(planes1):
        x1 = jnp.concatenate(
            [jnp.concatenate([*pieces[p : p + 3], k1_pad], axis=0) for p in chunk], axis=1
        )
        sums = jnp.dot(t1[...], x1, preferred_element_type=F32)
        for i, p in enumerate(chunk):
            v = sums[:, i * 128 : (i + 1) * 128].reshape(plan.r1, c1, 128)
            v = leaky_relu(v + b1[...])
            if p < 2:
                v = jnp.where(has_lower, v, 0.0)
            if p == planes1 - 1:
                v = jnp.where(has_upper, v, 0.0)
            v = jnp.concatenate(
                [
                    jnp.where(has_above, v[:2], 0.0),
                    v[2 : strip + 2],
                    jnp.where(has_below, v[strip + 2 :], 0.0),
                ],
                axis=0,
            ).reshape(n1, 128)
            for c, rows in enumerate(shifted(v)):
                x2[c * n1 : (c + 1) * n1, p * 128 : (p + 1) * 128] = rows.astype(BF)

    for chunk in chunks(planes2):
        sums = sum(
            jnp.dot(
                t2[a],
                x2[:, (chunk[0] + a) * 128 : (chunk[-1] + a + 1) * 128],
                preferred_element_type=F32,
            )
            for a in range(3)
        )
        for i, p in enumerate(chunk):
            v = sums[:, i * 128 : (i + 1) * 128].reshape(plan.r2, c2, 128)
            v = leaky_relu(v + b2[...])
            if p == 0:
                v = jnp.where(has_lower, v, 0.0)
            v = jnp.concatenate([jnp.where(has_above, v[:1], 0.0), v[1:]], axis=0).reshape(n2, 128)
            for c, rows in enumerate(shifted(v)):
                x3[c * n2 : (c + 1) * n2, p * 128 : (p + 1) * 128] = rows.astype(BF)

    pick = (
        lax.broadcasted_iota(jnp.int32, (128, 64), 0)
        == 2 * lax.broadcasted_iota(jnp.int32, (128, 64), 1)
    ).astype(F32).astype(BF)
    for f in range(0, depth // 2, 2):
        pair = range(f, min(f + 2, depth // 2))
        sums = 0.0
        for a in range(3):
            x = jnp.concatenate([x3[:, (2 * k + a) * 128 : (2 * k + a + 1) * 128] for k in pair], axis=1)
            sums = sums + jnp.dot(t3[a], x, preferred_element_type=F32)
        for i, k in enumerate(pair):
            v = leaky_relu(sums[:, i * 128 : (i + 1) * 128] + b3[...]).astype(BF)
            v = jnp.dot(v, pick, preferred_element_type=F32)
            out[:, k] = v.reshape(plan.c3, plan.r3, 64).astype(BF)


def band_base(kernel, rows, k):
    out_channels, in_channels = kernel.shape[:2]
    base = jnp.transpose(kernel.astype(F32), (2, 0, 4, 3, 1))
    base = jnp.pad(base, ((0, 0), (0, 0), (0, 0), (0, rows - 3), (0, 0)))
    base = base.reshape(3, out_channels, 3 * rows * in_channels)
    return jnp.pad(base, ((0, 0), (0, 0), (0, k - base.shape[2])))


def body(sky_cube, kernel_one, bias_one, kernel_two, bias_two, kernel_three, bias_three):
    tiles, groups = lax.axis_size("tile"), lax.axis_size("freq")
    strip = sky_cube.shape[1] // tiles
    depth = tiles * sky_cube.shape[0]
    c1, c2, c3 = (kernel.shape[0] for kernel in (kernel_one, kernel_two, kernel_three))
    plan = Plan(strip, c1, c2, c3)

    own = lax.all_gather(sky_cube.astype(BF), "tile", axis=0, tiled=True)
    pairs = []
    for g in range(groups):
        for t in range(tiles):
            to = g + 1 if t % 2 == 0 else g - 1
            target = to * tiles + t if 0 <= to < groups else g * tiles + (t ^ 1)
            pairs.append((g * tiles + t, target))
    got = lax.ppermute(own, ("freq", "tile"), pairs)
    other = lax.ppermute(got, "tile", [(t, t ^ 1) for t in range(tiles)])

    base1 = jnp.transpose(kernel_one[:, 0].astype(F32), (0, 1, 3, 2))
    base1 = jnp.pad(base1, ((0, 0), (0, 0), (0, 0), (0, plan.slots - 3)))
    base1 = base1.reshape(c1, 3, 3 * plan.slots)
    base1 = jnp.pad(base1, ((0, 0), (0, 0), (0, plan.plane_k - 3 * plan.slots)))
    base1 = base1.reshape(c1, 3 * plan.plane_k)
    base1 = jnp.pad(base1, ((0, 0), (0, plan.k1 - 3 * plan.plane_k)))
    base2 = band_base(kernel_two, plan.r1, plan.k2)
    base3 = band_base(kernel_three, plan.r2, plan.k3)

    bands = pl.pallas_call(
        functools.partial(bands_kernel, plan),
        name="bands",
        out_shape=[
            jax.ShapeDtypeStruct((plan.r1 * c1, plan.k1), BF),
            jax.ShapeDtypeStruct((3, plan.r2 * c2, plan.k2), BF),
            jax.ShapeDtypeStruct((3, plan.r3 * c3, plan.k3), BF),
            jax.ShapeDtypeStruct((c1, 128), F32),
            jax.ShapeDtypeStruct((c2, 128), F32),
            jax.ShapeDtypeStruct((plan.r3 * c3, 128), F32),
        ],
        in_specs=[SM] * 3 + [VM] * 3,
        out_specs=[VM] * 6,
        compiler_params=pltpu.CompilerParams(vmem_limit_bytes=32 * 2**20),
    )(bias_one, bias_two, bias_three, base1, base2, base3)

    return pl.pallas_call(
        functools.partial(layers_kernel, plan, depth),
        name="layers",
        out_shape=jax.ShapeDtypeStruct((c3, depth // 2, plan.r3, sky_cube.shape[2] // 2), BF),
        in_specs=[VM] * 9,
        out_specs=VM,
        scratch_shapes=[
            pltpu.VMEM((plan.k2, (depth + 3) * 128), BF),
            pltpu.VMEM((plan.k3, (depth + 1) * 128), BF),
        ],
        compiler_params=pltpu.CompilerParams(vmem_limit_bytes=32 * 2**20),
    )(own, got, other, *bands)


def solution(mesh):
    return jax.shard_map(
        body,
        mesh=mesh,
        in_specs=(P(("freq", "tile"), None, None), P(), P(), P(), P(), P(), P()),
        out_specs=P(None, "freq", "tile", None),
        check_vma=False,
    )
```

time: 109 us -> 15.3 us (0.14); the launches traced: 108 us -> 15.1 us
  local copies, waits for them, and re-layouts: 32.4 us -> 2.62 us
  matrix products: 23.5 us -> 0 us
  starting transfers between devices: 25 us -> 2 us
  waiting for transfers between devices: 15.7 us -> 0.22 us
  Pallas kernels: 0 us -> 3.14 us
  other arithmetic: 2.69 us -> 0.79 us
  blocking collectives: 7.9 us -> 6.17 us
    conv_general_dilated x15 -> x0, local copies, waits for them, and re-layouts: 31.1 us -> none  [the longest x10 22.6 us: conv_layer(): lax.conv_general_dilated(section[None], kernel, (1, 1, 1), ((0, 0), (0, 0...]
    conv_general_dilated x3 -> x0, matrix products: 23.5 us -> none  [the longest x2 19.2 us: conv_layer(): lax.conv_general_dilated(section[None], kernel, (1, 1, 1), ((0, 0), (0, 0...]
    ppermute x10 -> x2, starting transfers between devices: 25 us -> 2 us  [the longest x1 2 us: body(): got = lax.ppermute(own, ('freq', 'tile'), pairs)]
    ppermute x10 -> x2, waiting for transfers between devices: 15.7 us -> 0.22 us  [the longest x1 0.22 us: body(): got = lax.ppermute(own, ('freq', 'tile'), pairs)]
    all_to_all x1 -> x0, blocking collectives: 7.9 us -> none  [body(): lax.all_to_all(sky_cube.astype(jnp.bfloat16), 'tile', split_axis=1, conca...]
    all_gather x0 -> x1, blocking collectives: none -> 6.17 us  [body(): own = lax.all_gather(sky_cube.astype(BF), 'tile', axis=0, tiled=True)]
    pallas_call x0 -> x2, Pallas kernels: none -> 3.14 us  [the longest x1 2.06 us: body(): pl.pallas_call(functools.partial(layers_kernel, plan, depth), name='layer...]
  transfers between devices with their start and end apart: 10 -> 2, of which waited for: 7 -> 1; matrix products, arithmetic and copies ran while one was open for 0% -> 6% of each run, Pallas kernels for 0% -> 7%
where the time goes in v1:
time: 15.3 us; the launch traced here: 15.1 us
  blocking collectives  6.17 us (40%)
  Pallas kernels  3.14 us (21%)
  local copies, waits for them, and re-layouts  2.62 us (17%)
  starting transfers between devices  2 us (13%)
  other arithmetic  0.79 us (5%)
  waiting for transfers between devices  0.22 us (1%)
    all_gather x1, blocking collectives, body(): own = lax.all_gather(sky_cube.astype(BF), 'tile', axis=0, tiled=True)  6.17 us
    pallas_call x1, Pallas kernels, body(): pl.pallas_call(functools.partial(layers_kernel, plan, depth), name='layer...  2.06 us
    ppermute x1, starting transfers between devices, body(): got = lax.ppermute(own, ('freq', 'tile'), pairs)  2 us
    unnamed x16, local copies, waits for them, and re-layouts  1.89 us
    pallas_call x1, Pallas kernels, body(): pl.pallas_call(functools.partial(bands_kernel, plan), name='bands', out_s...  1.08 us
    convert_element_type x1, other arithmetic, body(): own = lax.all_gather(sky_cube.astype(BF), 'tile', axis=0, tiled=True)  0.77 us
    reshape x2, local copies, waits for them, and re-layouts, band_base(): base = base.reshape(3, out_channels, 3 * rows * in_channels)  0.4 us
  transfers between devices with their start and end apart: 2, of which 1 were waited for; matrix products, arithmetic and copies ran while one was open for 6% of the time, Pallas kernels for 7%

profile of v1, /device:TPU:0, one launch (start us, length us, event | category | flops | bytes accessed | tf_op | source)
XLA Modules:
  0.0 15.1 jit_solution(11903654728737475748)
XLA Ops:
  0.0 0.0 copy-start.4
  0.0 0.8 %convert_element_type.23 = bf16[1,64,128]{2,1,0:T(8,128)(2,1)S(1)} convert(f32[1,64,128]{2,1,0:T(8,128)} %param.7) | non-fusion elementwise | flops 8192 | bytes 49152 | tf_op jit(solution)/shard_map/convert_element_type | solution.py:210
  0.8 6.2 %all_gather.3.own = bf16[4,64,128]{2,1,0:T(8,128)(2,1)S(1)} all-gather(bf16[1,64,128]{2,1,0:T(8,128)(2,1)S(1)} %convert_element_type.23), channel_id=1, replica_groups=mesh['freq'=8,'tile'=4] {'tile'}, dimensions={0}, use_global_device_ids=true | all-gather | bytes 81920 | tf_op jit(solution)/shard_map/all_gather | solution.py:210
  6.9 2.0 %collective-permute-start = (bf16[4,64,128]{2,1,0:T(8,128)(2,1)S(1)}, bf16[4,64,128]{2,1,0:T(8,128)(2,1)S(1)}, u32[]{:S(2)}, u32[]{:S(2)}) collective-permute-start(bf16[4,64,128]{2,1,0:T(8,128)(2,1)S(1)} %all_gather.3.own), channel_id=1, source_target_pairs={{0,4},{1,0},{2,6},{3,2},{4,8},{5,1},{6,10},{7,3},{8,12},{9,5},{10,... | collective-permute-start | bytes 196616 | tf_op jit(solution)/shard_map/ppermute | solution.py:217
  8.9 0.0 copy-done.4
  9.0 0.1 pad.42.clone
  9.1 0.0 copy-start.3
  9.1 0.3 %reshape.20 = bf16[3,8,480]{2,1,0:T(8,128)(2,1)S(1)} reshape(bf16[3,8,3,20,8]{4,3,2,1,0:T(8,128)(2,1)S(1)} %pad.42.clone) | data formatting | bytes 46080 | tf_op jit(solution)/shard_map/reshape | solution.py:199
  9.3 0.6 %copy-done.3 = bf16[16,8,3,3,3]{0,1,4,3,2:T(8,128)(2,1)S(1)} copy-done((bf16[16,8,3,3,3]{0,1,4,3,2:T(8,128)(2,1)S(1)}, bf16[16,8,3,3,3]{0,1,4,3,2:T(8,128)(2,1)}, u32[]{:S(2)}) %copy-start.3) | copy-done | bytes 6936
  9.9 0.1 pad.45.clone
  10.0 0.1 copy.19
  10.1 0.0 copy-start.5
  10.1 0.7 %copy-done.5 = bf16[8,1,3,3,3]{0,4,3,2,1:T(4,128)(2,1)S(1)} copy-done((bf16[8,1,3,3,3]{0,4,3,2,1:T(4,128)(2,1)S(1)}, bf16[8,1,3,3,3]{0,4,3,2,1:T(4,128)(2,1)}, u32[]{:S(2)}) %copy-start.5) | copy-done | bytes 456
  10.8 0.2 %copy.20 = bf16[8,3,3,3]{3,2,0,1:T(4,128)(2,1)S(1)} copy(bf16[8,3,3,3]{0,2,3,1:T(4,128)(2,1)S(1)} %bitcast.11) | data formatting | bytes 864
  11.0 0.1 reshape.18
  11.1 0.1 reshape.19
  11.2 0.0 copy-start
  11.2 0.0 copy-start.1
  11.2 0.0 copy-start.2
  11.2 0.2 %collective-permute-done.got = bf16[4,64,128]{2,1,0:T(8,128)(2,1)S(1)} collective-permute-done((bf16[4,64,128]{2,1,0:T(8,128)(2,1)S(1)}, bf16[4,64,128]{2,1,0:T(8,128)(2,1)S(1)}, u32[]{:S(2)}, u32[]{:S(2)}) %collective-permute-start) | collective-permute-done | bytes 65568 | tf_op jit(solution)/shard_map/ppermute | solution.py:217
  11.5 0.0 collective-permute-start.1
  11.5 0.4 %copy-done = f32[8]{0:T(128)S(1)} copy-done((f32[8]{0:T(128)S(1)}, f32[8]{0:T(128)}, u32[]{:S(2)}) %copy-start) | copy-done | bytes 56
  11.9 0.0 copy-done.1
  11.9 0.0 copy-done.2
  11.9 1.1 %bands.1 = (bf16[160,256]{1,0:T(8,128)(2,1)S(1)}, bf16[3,144,512]{2,1,0:T(8,128)(2,1)S(1)}, bf16[3,128,512]{2,1,0:T(8,128)(2,1)S(1)}, f32[8,128]{1,0:T(8,128)S(1...) custom-call(f32[8]{0:T(128)S(1)} %copy-done, f32[8]{0:T(128)S(1)} %copy-done.1, f32[16]{0:T(128)S(1)} %copy-done.2, ...), custom_call_target="tpu_custom_call" | custom-call | tf_op jit(solution)/shard_map/bands/pallas_call | solution.py:229
  13.0 0.0 collective-permute-done.1.other
  13.0 2.1 %layers.1 = bf16[16,2,8,64]{3,2,1,0:T(8,128)(2,1)} custom-call(bf16[4,64,128]{2,1,0:T(8,128)(2,1)S(1)} %all_gather.3.own, bf16[4,64,128]{2,1,0:T(8,128)(2,1)S(1)} %collective-permute-done.got, bf16[4,64,128]{2,1,0:T(8,128)(2,1)S(1)} %collective-permute-done.1.other, bf16[160,256]{1,0:T(8,128)(2,1)S(1)} %get-tuple-element.11.t1, ...), custom_call_target="tpu_custom_call" | custom-call | tf_op jit(solution)/shard_map/layers/pallas_call | solution.py:245
  (8 shorter events, 0.1 us)
Async XLA Ops:
  0.0 8.9 %copy-start.4 = (bf16[8,8,3,3,3]{1,0,4,3,2:T(8,128)(2,1)S(1)}, bf16[8,8,3,3,3]{1,0,4,3,2:T(8,128)(2,1)}, u32[]{:S(2)}) copy-start(bf16[8,8,3,3,3]{1,0,4,3,2:T(8,128)(2,1)} %param.10) | copy-start | bytes 10372
  6.9 4.5 %collective-permute-start = (bf16[4,64,128]{2,1,0:T(8,128)(2,1)S(1)}, bf16[4,64,128]{2,1,0:T(8,128)(2,1)S(1)}, u32[]{:S(2)}, u32[]{:S(2)}) collective-permute-start(bf16[4,64,128]{2,1,0:T(8,128)(2,1)S(1)} %all_gather.3.own), channel_id=1, source_target_pairs={{0,4},{1,0},{2,6},{3,2},{4,8},{5,1},{6,10},{7,3},{8,12},{9,5},{10,... | collective-permute-start | bytes 196616 | tf_op jit(solution)/shard_map/ppermute | solution.py:217
  9.1 0.8 %copy-start.3 = (bf16[16,8,3,3,3]{0,1,4,3,2:T(8,128)(2,1)S(1)}, bf16[16,8,3,3,3]{0,1,4,3,2:T(8,128)(2,1)}, u32[]{:S(2)}) copy-start(bf16[16,8,3,3,3]{0,1,4,3,2:T(8,128)(2,1)} %param.12) | copy-start | bytes 20740
  10.1 0.7 %copy-start.5 = (bf16[8,1,3,3,3]{0,4,3,2,1:T(4,128)(2,1)S(1)}, bf16[8,1,3,3,3]{0,4,3,2,1:T(4,128)(2,1)}, u32[]{:S(2)}) copy-start(bf16[8,1,3,3,3]{0,4,3,2,1:T(4,128)(2,1)} %param.8) | copy-start | bytes 1300
  11.2 0.7 %copy-start = (f32[8]{0:T(128)S(1)}, f32[8]{0:T(128)}, u32[]{:S(2)}) copy-start(f32[8]{0:T(128)} %bias1.1) | copy-start | bytes 100
  11.2 0.7 %copy-start.1 = (f32[8]{0:T(128)S(1)}, f32[8]{0:T(128)}, u32[]{:S(2)}) copy-start(f32[8]{0:T(128)} %bias2.1) | copy-start | bytes 100
  11.2 0.7 %copy-start.2 = (f32[16]{0:T(128)S(1)}, f32[16]{0:T(128)}, u32[]{:S(2)}) copy-start(f32[16]{0:T(128)} %bias3.1) | copy-start | bytes 196
  11.5 1.5 %collective-permute-start.1 = (bf16[4,64,128]{2,1,0:T(8,128)(2,1)S(1)}, bf16[4,64,128]{2,1,0:T(8,128)(2,1)S(1)}, u32[]{:S(2)}, u32[]{:S(2)}) collective-permute-start(bf16[4,64,128]{2,1,0:T(8,128)(2,1)S(1)} %collective-permute-done.got), channel_id=1, source_target_pairs={{0,1},{1,0},{2,3},{3,2},{4,5},{5,4},{6,7},{7,6},{8,9},{9,8},{10,11... | collective-permute-start | bytes 196616 | tf_op jit(solution)/shard_map/ppermute | solution.py:218

commit v2 on v1

--- a/solution.py
+++ b/solution.py
@@ -46,52 +46,84 @@
     return out
 
 
-def bands_kernel(plan, bias1, bias2, bias3, base1, base2, base3, t1, t2, t3, b1, b2, b3):
-    c1, c2, c3 = plan.c1, plan.c2, plan.c3
+def ones_where(hit):
+    return hit.astype(F32).astype(BF)
+
+
+def dot_over_rows(left, right):
+    return lax.dot_general(left, right, (((0,), (0,)), ((), ())), preferred_element_type=F32)
+
+
+def rolled(x, by):
+    return pltpu.roll(x, by, 1) if by else x
+
+
+def bands_12_kernel(plan, bias1, bias2, w1, w2, t1, t2, b1, b2):
+    c1, c2 = plan.c1, plan.c2
     slots = plan.slots
     b1[...] = column_of(bias1, c1, 128)
     b2[...] = column_of(bias2, c2, 128)
-    lanes = lax.broadcasted_iota(jnp.int32, (c1, plan.k1), 1)
-    slot = lax.rem(lax.rem(lanes, plan.plane_k), slots)
-    taps = [jnp.where(slot == b, base1[...], 0.0) for b in range(3)]
-
-    def rolled(x, by):
-        return pltpu.roll(x, by, 1) if by else x
-
-    def tap_at(b, to):
-        return rolled(taps[b], (to - b) % plan.k1)
-
+    tap = lax.broadcasted_iota(jnp.int32, (3, plan.k1), 0)
+    lane = lax.broadcasted_iota(jnp.int32, (3, plan.k1), 1)
+    taps = []
+    for b in range(3):
+        taps.append(
+            sum(
+                dot_over_rows(w1[a, b], ones_where(lane == a * plan.plane_k + tap * slots))
+                for a in range(3)
+            )
+        )
     for y in range(0, plan.r1, 2):
-        rows = [sum(tap_at(b, (row - 3 + b) % slots) for b in range(3)) for row in (y, y + 1)]
+        rows = [
+            sum(rolled(taps[b], (row - 3 + b) % slots) for b in range(3)) for row in (y, y + 1)
+        ]
         t1[y * c1 : (y + 2) * c1, :] = jnp.concatenate(rows, axis=0).astype(BF)
+
     for a in range(3):
-        base = base2[a]
+        parts = [jnp.zeros((c2, 128), F32) for _ in range(plan.k2 // 128)]
+        for b in range(3):
+            for c in range(3):
+                at = (c * plan.r1 + b) * c1
+                tile = w2[a, b, c].astype(F32)
+                tile = jnp.concatenate([tile, jnp.zeros((c2, 128 - c1), F32)], axis=1)
+                parts[at // 128] += rolled(tile, at % 128)
+        base = jnp.concatenate(parts, axis=1)
         for y in range(0, plan.r2, 2):
             rows = [rolled(base, (y + k) * c1) for k in range(2)]
             t2[a, y * c2 : (y + 2) * c2, :] = jnp.concatenate(rows, axis=0).astype(BF)
+
+
+def bands_3_kernel(plan, bias3, w3, t3, b3):
+    c2, c3 = plan.c2, plan.c3
+    for o in range(c3):
+        b3[o * plan.r3 : (o + 1) * plan.r3, :] = jnp.full((plan.r3, 128), bias3[o], F32)
     n3 = plan.r3 * c3
     row = lax.broadcasted_iota(jnp.int32, (n3, n3), 0)
     col = lax.broadcasted_iota(jnp.int32, (n3, n3), 1)
-    turn = ((row // plan.r3 == col % c3) & (row % plan.r3 == col // c3)).astype(F32).astype(BF)
+    turn = ones_where((row // plan.r3 == col % c3) & (row % plan.r3 == col // c3))
+    row = lax.broadcasted_iota(jnp.int32, (9 * c2, plan.k3), 0)
+    lane = lax.broadcasted_iota(jnp.int32, (9 * c2, plan.k3), 1)
+    b, c, i = row // (3 * c2), (row // c2) % 3, row % c2
+    spread = ones_where(lane == (c * plan.r2 + b) * c2 + i)
     for a in range(3):
-        base = base3[a]
+        taken = w3[a].astype(F32).reshape(9 * c2, c3).astype(BF)
+        base = dot_over_rows(taken, spread)
         rows = [rolled(base, 2 * y * c2) for y in range(plan.r3)]
         stacked = jnp.concatenate(rows, axis=0).astype(BF)
         t3[a] = jnp.dot(turn, stacked, preferred_element_type=F32).astype(BF)
-    for o in range(c3):
-        b3[o * plan.r3 : (o + 1) * plan.r3, :] = jnp.full((plan.r3, 128), bias3[o], F32)
-
-
-def layers_kernel(plan, depth, own, got, other, t1, t2, t3, b1, b2, b3, out, x2, x3):
+
+
+def layers_kernel(plan, depth, span, own, got, other, t1, t2, b1, b2, t3, b3, out, x2, x3):
     freq, tile = lax.axis_index("freq"), lax.axis_index("tile")
     last_group, last_strip = lax.axis_size("freq") - 1, lax.axis_size("tile") - 1
     strip, c1, c2 = plan.strip, plan.c1, plan.c2
-    here = pl.multiple_of(tile * strip, 16)
-    above = pl.multiple_of(jnp.maximum(tile - 1, 0) * strip + strip - 16, 16)
-    below = pl.multiple_of(jnp.minimum(tile + 1, last_strip) * strip, 16)
+    here = tile * strip
+    above = jnp.maximum(tile - 1, 0) * strip + strip - 16
+    below = jnp.minimum(tile + 1, last_strip) * strip
+    first = first_row(plan, tile, last_strip + 1, span)
     has_above, has_below = tile > 0, tile < last_strip
     has_lower, has_upper = freq > 0, freq < last_group
-    upward = lax.rem(tile, 2) == 0
+    from_lower = lax.rem(tile, 2) == 1
 
     sub = lax.broadcasted_iota(jnp.int32, (8, 128), 0)
     rim_keep = ((sub < 4) & has_below) | ((sub >= 4) & has_above)
@@ -99,10 +131,14 @@
     def lane_of(rows):
         return lax.broadcasted_iota(jnp.int32, (rows, 128), 1)
 
-    def window(ref, plane):
-        middle = ref[plane, pl.ds(here, strip), :].astype(F32)
-        rim_above = ref[plane, pl.ds(above, 16), :].astype(F32)[8:]
-        rim_below = ref[plane, pl.ds(below, 16), :].astype(F32)[:8]
+    def window(ref, plane, first=first):
+        def rows(at, count):
+            at = jnp.clip(at - first, 0, ref.shape[1] - count)
+            return ref[plane, pl.ds(pl.multiple_of(at, 16), count), :].astype(F32)
+
+        middle = rows(here, strip)
+        rim_above = rows(above, 16)[8:]
+        rim_below = rows(below, 16)[:8]
         rim = jnp.where(rim_keep, jnp.where(sub < 4, rim_below, rim_above), 0.0)
         return jnp.concatenate([middle, rim], axis=0)
 
@@ -115,13 +151,13 @@
         )
 
     slab = []
-    for p in range(depth - 3, depth):
-        rows = jnp.where(upward, window(got, p), window(other, p))
+    for p in range(3):
+        rows = jnp.where(from_lower, window(got, p), window(other, p))
         slab.append(jnp.where(has_lower, rows, 0.0))
     for p in range(depth):
-        slab.append(window(own, p))
+        slab.append(window(own, p, 0))
     for p in range(2):
-        rows = jnp.where(upward, window(other, p), window(got, p))
+        rows = jnp.where(from_lower, window(other, p), window(got, p))
         slab.append(jnp.where(has_upper, rows, 0.0))
     pad = jnp.zeros((plan.plane_k - 3 * plan.slots, 128), F32)
     pieces = [jnp.concatenate([*shifted(rows), pad], axis=0).astype(BF) for rows in slab]
@@ -192,12 +228,37 @@
             out[:, k] = v.reshape(plan.c3, plan.r3, 64).astype(BF)
 
 
-def band_base(kernel, rows, k):
-    out_channels, in_channels = kernel.shape[:2]
-    base = jnp.transpose(kernel.astype(F32), (2, 0, 4, 3, 1))
-    base = jnp.pad(base, ((0, 0), (0, 0), (0, 0), (0, rows - 3), (0, 0)))
-    base = base.reshape(3, out_channels, 3 * rows * in_channels)
-    return jnp.pad(base, ((0, 0), (0, 0), (0, k - base.shape[2])))
+def first_row(plan, tile, tiles, span):
+    return jnp.clip((tile // 2) * 2 * plan.strip - 16, 0, tiles * plan.strip - span)
+
+
+def gathered(plane, tiles):
+    if tiles & (tiles - 1):
+        return lax.all_gather(plane.astype(BF), "tile", axis=0, tiled=True)
+    tile, size, held = lax.axis_index("tile"), 1, plane
+    while size < tiles:
+        taken = lax.ppermute(held, "tile", [(t, t ^ (2 * size - 1)) for t in range(tiles)])
+        if size == 1:
+            taken = lax.optimization_barrier(taken).astype(BF)
+            held = held.astype(BF)
+        upper = (tile // size) % 2 == 1
+        held = jnp.where(
+            upper,
+            jnp.concatenate([taken, held], axis=0),
+            jnp.concatenate([held, taken], axis=0),
+        )
+        size *= 2
+    return held
+
+
+def freq_pairs(groups, tiles):
+    pairs = []
+    for g in range(groups):
+        for t in range(tiles):
+            to = g + 1 if t % 2 == 0 else g - 1
+            target = (to, t ^ 1) if 0 <= to < groups else (g, (t + 2) % tiles)
+            pairs.append((g * tiles + t, target[0] * tiles + target[1]))
+    return pairs
 
 
 def body(sky_cube, kernel_one, bias_one, kernel_two, bias_two, kernel_three, bias_three):
@@ -207,43 +268,48 @@
     c1, c2, c3 = (kernel.shape[0] for kernel in (kernel_one, kernel_two, kernel_three))
     plan = Plan(strip, c1, c2, c3)
 
-    own = lax.all_gather(sky_cube.astype(BF), "tile", axis=0, tiled=True)
-    pairs = []
-    for g in range(groups):
-        for t in range(tiles):
-            to = g + 1 if t % 2 == 0 else g - 1
-            target = to * tiles + t if 0 <= to < groups else g * tiles + (t ^ 1)
-            pairs.append((g * tiles + t, target))
-    got = lax.ppermute(own, ("freq", "tile"), pairs)
-    other = lax.ppermute(got, "tile", [(t, t ^ 1) for t in range(tiles)])
-
-    base1 = jnp.transpose(kernel_one[:, 0].astype(F32), (0, 1, 3, 2))
-    base1 = jnp.pad(base1, ((0, 0), (0, 0), (0, 0), (0, plan.slots - 3)))
-    base1 = base1.reshape(c1, 3, 3 * plan.slots)
-    base1 = jnp.pad(base1, ((0, 0), (0, 0), (0, plan.plane_k - 3 * plan.slots)))
-    base1 = base1.reshape(c1, 3 * plan.plane_k)
-    base1 = jnp.pad(base1, ((0, 0), (0, plan.k1 - 3 * plan.plane_k)))
-    base2 = band_base(kernel_two, plan.r1, plan.k2)
-    base3 = band_base(kernel_three, plan.r2, plan.k3)
-
-    bands = pl.pallas_call(
-        functools.partial(bands_kernel, plan),
-        name="bands",
+    w1 = jnp.transpose(kernel_one[:, 0], (1, 2, 3, 0))
+    w2 = jnp.transpose(kernel_two, (2, 3, 4, 0, 1))
+    w3 = jnp.transpose(kernel_three, (2, 3, 4, 1, 0))
+
+    params = pltpu.CompilerParams(vmem_limit_bytes=32 * 2**20)
+    bands_12 = pl.pallas_call(
+        functools.partial(bands_12_kernel, plan),
+        name="bands_12",
         out_shape=[
             jax.ShapeDtypeStruct((plan.r1 * c1, plan.k1), BF),
             jax.ShapeDtypeStruct((3, plan.r2 * c2, plan.k2), BF),
-            jax.ShapeDtypeStruct((3, plan.r3 * c3, plan.k3), BF),
             jax.ShapeDtypeStruct((c1, 128), F32),
             jax.ShapeDtypeStruct((c2, 128), F32),
+        ],
+        in_specs=[SM] * 2 + [VM] * 2,
+        out_specs=[VM] * 4,
+        compiler_params=params,
+    )(bias_one, bias_two, w1, w2)
+    bands_3 = pl.pallas_call(
+        functools.partial(bands_3_kernel, plan),
+        name="bands_3",
+        out_shape=[
+            jax.ShapeDtypeStruct((3, plan.r3 * c3, plan.k3), BF),
             jax.ShapeDtypeStruct((plan.r3 * c3, 128), F32),
         ],
-        in_specs=[SM] * 3 + [VM] * 3,
-        out_specs=[VM] * 6,
-        compiler_params=pltpu.CompilerParams(vmem_limit_bytes=32 * 2**20),
-    )(bias_one, bias_two, bias_three, base1, base2, base3)
+        in_specs=[SM, VM],
+        out_specs=[VM] * 2,
+        compiler_params=params,
+    )(bias_three, w3)
+
+    tile = lax.axis_index("tile")
+    own = gathered(sky_cube, tiles)
+    own, *bands_12 = lax.optimization_barrier((own, *bands_12))
+    span = min(3 if tiles <= 4 else 4, tiles) * strip
+    begin = (jnp.where(tile % 2 == 0, depth - 3, 0), first_row(plan, tile, tiles, span), 0)
+    message = lax.dynamic_slice(own, begin, (3, span, own.shape[2]))
+    got = lax.ppermute(message, ("freq", "tile"), freq_pairs(groups, tiles))
+    got, *bands_3 = lax.optimization_barrier((got, *bands_3))
+    other = lax.ppermute(got, "tile", [(t, t ^ 1) for t in range(tiles)])
 
     return pl.pallas_call(
-        functools.partial(layers_kernel, plan, depth),
+        functools.partial(layers_kernel, plan, depth, span),
         name="layers",
         out_shape=jax.ShapeDtypeStruct((c3, depth // 2, plan.r3, sky_cube.shape[2] // 2), BF),
         in_specs=[VM] * 9,
@@ -252,8 +318,8 @@
             pltpu.VMEM((plan.k2, (depth + 3) * 128), BF),
             pltpu.VMEM((plan.k3, (depth + 1) * 128), BF),
         ],
-        compiler_params=pltpu.CompilerParams(vmem_limit_bytes=32 * 2**20),
-    )(own, got, other, *bands)
+        compiler_params=params,
+    )(own, got, other, *bands_12, *bands_3)
 
 
 def solution(mesh):

time: 15.3 us -> 13.7 us (0.90)
  the two profiles are of different devices: /device:TPU:0 before, /device:TPU:3 now
where the time goes in v2:
time: 13.7 us; the launch traced here: 13.4 us
  Pallas kernels  4.68 us (34%)
  starting transfers between devices  3.75 us (27%)
  waiting for transfers between devices  2.92 us (21%)
  local copies, waits for them, and re-layouts  1.25 us (9%)
  other arithmetic  0.78 us (6%)
    ppermute x2, starting transfers between devices, gathered(): lax.ppermute(held, 'tile', [(t, t ^ 2 * size - 1) for t in range(tiles)])  2.2 us
    pallas_call x1, Pallas kernels, body(): pl.pallas_call(functools.partial(layers_kernel, plan, depth, span), name=...  2.05 us
    pallas_call x1, Pallas kernels, body(): pl.pallas_call(functools.partial(bands_3_kernel, plan), name='bands_3', o...  1.53 us
    ppermute x1, starting transfers between devices, body(): other = lax.ppermute(got, 'tile', [(t, t ^ 1) for t in range(tiles)])  1.29 us
    unnamed x12, local copies, waits for them, and re-layouts  1.22 us
    ppermute x1, waiting for transfers between devices, body(): got = lax.ppermute(message, ('freq', 'tile'), freq_pairs(groups, tiles))  1.15 us
    pallas_call x1, Pallas kernels, body(): pl.pallas_call(functools.partial(bands_12_kernel, plan), name='bands_12',...  1.1 us
    ppermute x2, waiting for transfers between devices, gathered(): lax.ppermute(held, 'tile', [(t, t ^ 2 * size - 1) for t in range(tiles)])  0.91 us
  transfers between devices with their start and end apart: 4, of which 4 were waited for; matrix products, arithmetic and copies ran while one was open for 0% of the time, Pallas kernels for 20%

profile of v2, /device:TPU:3, one launch (start us, length us, event | category | flops | bytes accessed | tf_op | source)
XLA Modules:
  0.0 13.4 jit_solution(9579846730686080248)
XLA Ops:
  0.0 0.8 %convert.2 = bf16[1,64,128]{2,1,0:T(8,128)(2,1)S(1)} convert(f32[1,64,128]{2,1,0:T(8,128)} %param.7) | non-fusion elementwise | flops 8192 | bytes 49152
  0.8 0.7 %collective-permute-start = (bf16[1,64,128]{2,1,0:T(8,128)(2,1)S(1)}, bf16[1,64,128]{2,1,0:T(8,128)(2,1)S(1)}, u32[]{:S(2)}, u32[]{:S(2)}) collective-permute-start(bf16[1,64,128]{2,1,0:T(8,128)(2,1)S(1)} %convert.2), channel_id=1, source_target_pairs={{0,1},{1,0},{2,3},{3,2},{4,5},{5,4},{6,7},{7,6},{8,9},{9,8},{10,11... | collective-permute-start | bytes 49160 | tf_op jit(solution)/shard_map/ppermute | solution.py:240
  1.4 0.0 copy-start.1
  1.4 0.8 %collective-permute-done = bf16[1,64,128]{2,1,0:T(8,128)(2,1)S(1)} collective-permute-done((bf16[1,64,128]{2,1,0:T(8,128)(2,1)S(1)}, bf16[1,64,128]{2,1,0:T(8,128)(2,1)S(1)}, u32[]{:S(2)}, u32[]{:S(2)}) %collective-permute-start) | collective-permute-done | bytes 16416 | tf_op jit(solution)/shard_map/ppermute | solution.py:240
  2.3 1.5 %collective-permute-start.1 = (bf16[2,64,128]{2,1,0:T(8,128)(2,1)S(1)}, bf16[2,64,128]{2,1,0:T(8,128)(2,1)S(1)}, u32[]{:S(2)}, u32[]{:S(2)}) collective-permute-start(bf16[2,64,128]{2,1,0:T(8,128)(2,1)S(1)} %maximum_select_fusion.1), channel_id=1, source_target_pairs={{0,3},{1,2},{2,1},{3,0},{4,7},{5,6},{6,5},{7,4},{8,11},{9,10},{10,... | collective-permute-start | bytes 98312 | tf_op jit(solution)/shard_map/ppermute | solution.py:240
  3.8 0.0 copy-start.2
  3.8 0.0 copy-start.3
  3.8 0.0 copy-start.4
  3.8 0.0 copy-done.1
  3.8 0.7 %copy-done.2 = bf16[8,1,3,3,3]{0,4,3,2,1:T(4,128)(2,1)S(1)} copy-done((bf16[8,1,3,3,3]{0,4,3,2,1:T(4,128)(2,1)S(1)}, bf16[8,1,3,3,3]{0,4,3,2,1:T(4,128)(2,1)}, u32[]{:S(2)}) %copy-start.2) | copy-done | bytes 456
  4.5 0.0 copy-done.3
  4.5 0.0 copy-done.4
  4.5 1.1 %bands_12.1 = (bf16[160,256]{1,0:T(8,128)(2,1)S(1)}, bf16[3,144,512]{2,1,0:T(8,128)(2,1)S(1)}, f32[8,128]{1,0:T(8,128)S(1)}, f32[8,128]{1,0:T(8,128)S(1)}) custom-call(f32[8]{0:T(128)S(1)} %copy-done.3, f32[8]{0:T(128)S(1)} %copy-done.4, bf16[3,3,3,8]{3,2,1,0:T(4,128)(2,1)S(1)} %bitcast.7, bf16[3,3,3,8,8]{4,3,2,1,0:T(8,128)(2,1)S(1)} %bitcast.6), custom_call_target="tpu_custom_call" | custom-call | tf_op jit(solution)/shard_map/bands_12/pallas_call | solution.py:276
  5.6 0.1 collective-permute-done.1
  5.7 0.0 copy-start
  5.8 0.0 copy-start.5
  5.8 0.3 %collective-permute-start.2 = (bf16[3,48,128]{2,1,0:T(8,128)(2,1)S(1)}, bf16[3,48,128]{2,1,0:T(8,128)(2,1)S(1)}, u32[]{:S(2)}, u32[]{:S(2)}) collective-permute-start(bf16[3,48,128]{2,1,0:T(8,128)(2,1)S(1)} %constant_dynamic-slice_fusion), channel_id=1, source_target_pairs={{0,5},{1,3},{2,7},{3,1},{4,9},{5,0},{6,11},{7,2},{8,13},{9,4},{10,... | collective-permute-start | bytes 110600 | tf_op jit(solution)/shard_map/ppermute | solution.py:307
  6.0 0.5 %copy-done = bf16[16,8,3,3,3]{0,1,4,3,2:T(8,128)(2,1)S(1)} copy-done((bf16[16,8,3,3,3]{0,1,4,3,2:T(8,128)(2,1)S(1)}, bf16[16,8,3,3,3]{0,1,4,3,2:T(8,128)(2,1)}, u32[]{:S(2)}) %copy-start) | copy-done | bytes 6936
  6.5 0.0 copy-done.5
  6.5 1.5 %bands_3.1 = (bf16[3,128,512]{2,1,0:T(8,128)(2,1)S(1)}, f32[128,128]{1,0:T(8,128)S(1)}) custom-call(f32[16]{0:T(128)S(1)} %copy-done.5, bf16[3,3,3,8,16]{4,3,2,1,0:T(8,128)(2,1)S(1)} %bitcast.5), custom_call_target="tpu_custom_call" | custom-call | tf_op jit(solution)/shard_map/bands_3/pallas_call | solution.py:289
  8.1 1.1 %collective-permute-done.2.got = bf16[3,48,128]{2,1,0:T(8,128)(2,1)S(1)} collective-permute-done((bf16[3,48,128]{2,1,0:T(8,128)(2,1)S(1)}, bf16[3,48,128]{2,1,0:T(8,128)(2,1)S(1)}, u32[]{:S(2)}, u32[]{:S(2)}) %collective-permute-start.2) | collective-permute-done | bytes 36896 | tf_op jit(solution)/shard_map/ppermute | solution.py:307
  9.2 1.3 %collective-permute-start.3 = (bf16[3,48,128]{2,1,0:T(8,128)(2,1)S(1)}, bf16[3,48,128]{2,1,0:T(8,128)(2,1)S(1)}, u32[]{:S(2)}, u32[]{:S(2)}) collective-permute-start(bf16[3,48,128]{2,1,0:T(8,128)(2,1)S(1)} %collective-permute-done.2.got), channel_id=1, source_target_pairs={{0,1},{1,0},{2,3},{3,2},{4,5},{5,4},{6,7},{7,6},{8,9},{9,8},{10,11... | collective-permute-start | bytes 110600 | tf_op jit(solution)/shard_map/ppermute | solution.py:309
  10.5 0.9 %collective-permute-done.3.other = bf16[3,48,128]{2,1,0:T(8,128)(2,1)S(1)} collective-permute-done((bf16[3,48,128]{2,1,0:T(8,128)(2,1)S(1)}, bf16[3,48,128]{2,1,0:T(8,128)(2,1)S(1)}, u32[]{:S(2)}, u32[]{:S(2)}) %collective-permute-start.3) | collective-permute-done | bytes 36896 | tf_op jit(solution)/shard_map/ppermute | solution.py:309
  11.4 2.0 %layers.1 = bf16[16,2,8,64]{3,2,1,0:T(8,128)(2,1)} custom-call(bf16[4,64,128]{2,1,0:T(8,128)(2,1)S(1)} %maximum_select_fusion.own, bf16[3,48,128]{2,1,0:T(8,128)(2,1)S(1)} %collective-permute-done.2.got, bf16[3,48,128]{2,1,0:T(8,128)(2,1)S(1)} %collective-permute-done.3.other, bf16[160,256]{1,0:T(8,128)(2,1)S(1)} %get-tuple-element.27.t1, ...), custom_call_target="tpu_custom_call" | custom-call | tf_op jit(solution)/shard_map/layers/pallas_call | solution.py:311
  (3 shorter events, 0.0 us)
Async XLA Ops:
  0.8 1.5 %collective-permute-start = (bf16[1,64,128]{2,1,0:T(8,128)(2,1)S(1)}, bf16[1,64,128]{2,1,0:T(8,128)(2,1)S(1)}, u32[]{:S(2)}, u32[]{:S(2)}) collective-permute-start(bf16[1,64,128]{2,1,0:T(8,128)(2,1)S(1)} %convert.2), channel_id=1, source_target_pairs={{0,1},{1,0},{2,3},{3,2},{4,5},{5,4},{6,7},{7,6},{8,9},{9,8},{10,11... | collective-permute-start | bytes 49160 | tf_op jit(solution)/shard_map/ppermute | solution.py:240
  1.4 2.4 %copy-start.1 = (bf16[8,8,3,3,3]{1,0,4,3,2:T(8,128)(2,1)S(1)}, bf16[8,8,3,3,3]{1,0,4,3,2:T(8,128)(2,1)}, u32[]{:S(2)}) copy-start(bf16[8,8,3,3,3]{1,0,4,3,2:T(8,128)(2,1)} %param.10) | copy-start | bytes 10372
  2.3 3.4 %collective-permute-start.1 = (bf16[2,64,128]{2,1,0:T(8,128)(2,1)S(1)}, bf16[2,64,128]{2,1,0:T(8,128)(2,1)S(1)}, u32[]{:S(2)}, u32[]{:S(2)}) collective-permute-start(bf16[2,64,128]{2,1,0:T(8,128)(2,1)S(1)} %maximum_select_fusion.1), channel_id=1, source_target_pairs={{0,3},{1,2},{2,1},{3,0},{4,7},{5,6},{6,5},{7,4},{8,11},{9,10},{10,... | collective-permute-start | bytes 98312 | tf_op jit(solution)/shard_map/ppermute | solution.py:240
  3.8 0.7 %copy-start.2 = (bf16[8,1,3,3,3]{0,4,3,2,1:T(4,128)(2,1)S(1)}, bf16[8,1,3,3,3]{0,4,3,2,1:T(4,128)(2,1)}, u32[]{:S(2)}) copy-start(bf16[8,1,3,3,3]{0,4,3,2,1:T(4,128)(2,1)} %param.8) | copy-start | bytes 1300
  3.8 0.7 %copy-start.3 = (f32[8]{0:T(128)S(1)}, f32[8]{0:T(128)}, u32[]{:S(2)}) copy-start(f32[8]{0:T(128)} %bias1.1) | copy-start | bytes 100
  3.8 0.7 %copy-start.4 = (f32[8]{0:T(128)S(1)}, f32[8]{0:T(128)}, u32[]{:S(2)}) copy-start(f32[8]{0:T(128)} %bias2.1) | copy-start | bytes 100
  5.7 0.8 %copy-start = (bf16[16,8,3,3,3]{0,1,4,3,2:T(8,128)(2,1)S(1)}, bf16[16,8,3,3,3]{0,1,4,3,2:T(8,128)(2,1)}, u32[]{:S(2)}) copy-start(bf16[16,8,3,3,3]{0,1,4,3,2:T(8,128)(2,1)} %param.12) | copy-start | bytes 20740
  5.8 0.8 %copy-start.5 = (f32[16]{0:T(128)S(1)}, f32[16]{0:T(128)}, u32[]{:S(2)}) copy-start(f32[16]{0:T(128)} %bias3.1) | copy-start | bytes 196
  5.8 3.4 %collective-permute-start.2 = (bf16[3,48,128]{2,1,0:T(8,128)(2,1)S(1)}, bf16[3,48,128]{2,1,0:T(8,128)(2,1)S(1)}, u32[]{:S(2)}, u32[]{:S(2)}) collective-permute-start(bf16[3,48,128]{2,1,0:T(8,128)(2,1)S(1)} %constant_dynamic-slice_fusion), channel_id=1, source_target_pairs={{0,5},{1,3},{2,7},{3,1},{4,9},{5,0},{6,11},{7,2},{8,13},{9,4},{10,... | collective-permute-start | bytes 110600 | tf_op jit(solution)/shard_map/ppermute | solution.py:307
  9.2 2.2 %collective-permute-start.3 = (bf16[3,48,128]{2,1,0:T(8,128)(2,1)S(1)}, bf16[3,48,128]{2,1,0:T(8,128)(2,1)S(1)}, u32[]{:S(2)}, u32[]{:S(2)}) collective-permute-start(bf16[3,48,128]{2,1,0:T(8,128)(2,1)S(1)} %collective-permute-done.2.got), channel_id=1, source_target_pairs={{0,1},{1,0},{2,3},{3,2},{4,5},{5,4},{6,7},{7,6},{8,9},{9,8},{10,11... | collective-permute-start | bytes 110600 | tf_op jit(solution)/shard_map/ppermute | solution.py:309

commit v3 on v0

v3 whole, which is shorter than its diff:
```python
import functools

import jax
import jax.numpy as jnp
from jax import lax
from jax.experimental import pallas as pl
from jax.experimental.pallas import tpu as pltpu
from jax.sharding import PartitionSpec as P

BF = jnp.bfloat16
F32 = jnp.float32
VM = pl.BlockSpec(memory_space=pltpu.VMEM)


def even(n):
    return n + n % 2


def up_to(n, unit):
    return -(-n // unit) * unit


class Plan:
    def __init__(self, strip, depth, c1, c2, c3):
        self.strip, self.depth, self.c1, self.c2, self.c3 = strip, depth, c1, c2, c3
        self.rim = 4
        self.slots = strip + 2 * self.rim
        self.span = 2 * strip + 2 * self.rim
        self.plane_k = up_to(3 * self.slots, 16)
        self.k1 = up_to(3 * self.plane_k, 256)
        self.block2, self.block3 = 6, 4
        self.r2 = up_to(strip + 1, self.block2)
        self.r1 = self.r2 + 2
        self.r3 = strip // 2
        self.n1, self.n2 = self.r1 * c1, self.r2 * c2
        self.in2, self.out2 = (self.block2 + 2) * c1, self.block2 * c2
        self.in3, self.out3 = (2 * self.block3 + 2) * c2, self.block3 * c3
        self.k2, self.k3 = up_to(3 * self.in2, 256), up_to(3 * self.in3, 256)
        self.planes1, self.planes2 = depth + 3, depth + 1


def leaky_relu(values):
    return jnp.maximum(values, 0.1 * values)


def faces_lower(tile):
    return tile % 2 == 1


def column_of(bias_ref, rows):
    at = lax.broadcasted_iota(jnp.int32, (rows, rows), 0)
    lane = lax.broadcasted_iota(jnp.int32, (rows, rows), 1)
    spread = jnp.where(at == lane, jnp.broadcast_to(bias_ref[...], (rows, rows)), 0.0)
    return jnp.broadcast_to(jnp.sum(spread, axis=1, keepdims=True), (rows, 128))


def ones_where(hit):
    return hit.astype(F32).astype(BF)


def dot_over_rows(left, right):
    return lax.dot_general(left, right, (((0,), (0,)), ((), ())), preferred_element_type=F32)


def rolled(x, by):
    return pltpu.roll(x, by, 1) if by else x


def bands_12_kernel(plan, bias1, bias2, bias3, w1, w2, t1, t2, b1, b2, b3):
    c1, c2 = plan.c1, plan.c2
    slots = plan.slots
    b1[...] = column_of(bias1, c1)
    b2[...] = column_of(bias2, c2)
    column = column_of(bias3, plan.c3)
    b3[...] = jnp.broadcast_to(column[:, None], b3.shape)
    tap = lax.broadcasted_iota(jnp.int32, (3, plan.k1), 0)
    lane = lax.broadcasted_iota(jnp.int32, (3, plan.k1), 1)
    taps = []
    for b in range(3):
        taps.append(
            sum(
                dot_over_rows(w1[a, b], ones_where(lane == a * plan.plane_k + tap * slots))
                for a in range(3)
            )
        )
    base = sum(rolled(taps[b], b) for b in range(3))
    for y in range(0, plan.r1, 2):
        rows = [rolled(base, y + k + plan.rim - 3) for k in range(2)]
        t1[y * c1 : (y + 2) * c1, :] = jnp.concatenate(rows, axis=0).astype(BF)

    for c in range(3):
        parts = [jnp.zeros((c2, 128), F32) for _ in range(plan.k2 // 128)]
        for a in range(3):
            for b in range(3):
                at = a * plan.in2 + b * c1
                tile = w2[a, b, c].astype(F32)
                tile = jnp.concatenate([tile, jnp.zeros((c2, 128 - c1), F32)], axis=1)
                parts[at // 128] += rolled(tile, at % 128)
        base = jnp.concatenate(parts, axis=1)
        for y in range(0, plan.block2, 2):
            rows = [rolled(base, (y + k) * c1) for k in range(2)]
            at = c * plan.out2 + y * c2
            t2[at : at + 2 * c2, :] = jnp.concatenate(rows, axis=0).astype(BF)


def bands_3_kernel(plan, w3, t3):
    c2, c3, rows = plan.c2, plan.c3, plan.block3
    n3 = plan.out3
    at = lax.broadcasted_iota(jnp.int32, (2 * n3, n3), 0)
    source = lax.broadcasted_iota(jnp.int32, (2 * n3, n3), 1)
    odd, pair, which, y = at // n3, (at % n3) // (2 * rows), (at // rows) % 2, at % rows
    turn = ones_where(source == y * c3 + 2 * pair + (which + odd) % 2)
    row = lax.broadcasted_iota(jnp.int32, (9 * c2, plan.k3), 0)
    lane = lax.broadcasted_iota(jnp.int32, (9 * c2, plan.k3), 1)
    a, b, i = row // (3 * c2), (row // c2) % 3, row % c2
    spread = ones_where(lane == a * plan.in3 + b * c2 + i)
    for c in range(3):
        taken = w3[:, :, c].astype(F32).reshape(9 * c2, c3).astype(BF)
        base = dot_over_rows(taken, spread)
        stacked = [rolled(base, 2 * y * c2) for y in range(rows)]
        stacked = jnp.concatenate(stacked, axis=0).astype(BF)
        both = jnp.dot(turn, stacked, preferred_element_type=F32).astype(BF)
        for odd in range(2):
            t3[odd, c * n3 : (c + 1) * n3, :] = both[odd * n3 : (odd + 1) * n3]


class Place:
    def __init__(self):
        freq, tile = lax.axis_index("freq"), lax.axis_index("tile")
        self.second = lax.rem(tile, 2) == 1
        self.faces_lower = faces_lower(tile)
        self.has_lower, self.has_upper = freq > 0, freq < lax.axis_size("freq") - 1
        self.has_above, self.has_below = tile > 0, tile < lax.axis_size("tile") - 1


def lane_of(x):
    return lax.broadcasted_iota(jnp.int32, x.shape, 1)


def turned(x, by):
    return pltpu.roll(x, by, 1)


def column_taps(x):
    lane, zero, half = lane_of(x), jnp.zeros_like(x), turned(x, 64)
    before = jnp.where(lane < 64, turned(x, 65), half)
    after = jnp.where(lane < 64, half, turned(x, 63))
    return jnp.where(lane == 0, zero, before), x, jnp.where(lane == 127, zero, after)


def sum_of_taps(before, here, after):
    lane, zero = lane_of(here), jnp.zeros_like(here)
    half = turned(jnp.where(lane < 64, before, after), 64)
    rest = jnp.where(lane < 64, turned(before, 65), turned(after, 63))
    return here + half + jnp.where((lane == 0) | (lane == 127), zero, rest)


def sum_of_even_taps(before, here, after):
    lane, zero = lane_of(here), jnp.zeros_like(here)
    return here + turned(after, 64) + jnp.where(lane == 0, zero, turned(before, 65))


def own_rows(own, plane):
    return own[plane].astype(F32)


def rim_rows(plan, place, ref, plane, inside):
    rows = ref[plane].astype(F32)
    rows = jnp.where(place.second, rows[plan.strip :], rows[: plan.slots])
    return jnp.where(inside, rows, 0.0)


def piece(plan, rows):
    pad = jnp.zeros((plan.plane_k - 3 * plan.slots, 128), F32)
    return jnp.concatenate([*column_taps(rows), pad], axis=0).astype(BF)


def in_twos(planes):
    planes = list(planes)
    return [planes[i : i + 2] for i in range(0, len(planes), 2)]


def layer_one(plan, place, pieces, planes, t1, b1):
    pad = jnp.zeros((plan.k1 - 3 * plan.plane_k, 128), BF)
    strip, made = plan.strip, {}
    for chunk in in_twos(planes):
        x1 = [jnp.concatenate([*pieces[p : p + 3], pad], axis=0) for p in chunk]
        sums = jnp.dot(t1[...], jnp.concatenate(x1, axis=1), preferred_element_type=F32)
        for i, p in enumerate(chunk):
            v = sums[:, i * 128 : (i + 1) * 128].reshape(plan.r1, plan.c1, 128)
            v = leaky_relu(v + b1[...])
            if p < 2:
                v = jnp.where(place.has_lower, v, 0.0)
            if p == plan.planes1 - 1:
                v = jnp.where(place.has_upper, v, 0.0)
            v = jnp.concatenate(
                [
                    jnp.where(place.has_above, v[:2], 0.0),
                    v[2 : strip + 2],
                    jnp.where(place.has_below, v[strip + 2 :], 0.0),
                ],
                axis=0,
            )
            made[p] = v.reshape(plan.n1, 128).astype(BF)
    return made


def blocks_of(planes, rows, step, size, k):
    parts = [plane[step * k : step * k + size] for plane in planes]
    return jnp.concatenate(parts + [jnp.zeros((rows - len(parts) * size, 128), BF)], axis=0)


def layer_two(plan, place, layer_one, planes, t2, b2):
    out2, blocks = plan.out2, {}
    for chunk in in_twos((q, k) for q in planes for k in range(plan.r2 // plan.block2)):
        x = []
        for q, k in chunk:
            x.append(blocks_of([layer_one(q + a) for a in range(3)], plan.k2, out2, plan.in2, k))
        sums = jnp.dot(t2[...], jnp.concatenate(x, axis=1), preferred_element_type=F32)
        for i, (q, k) in enumerate(chunk):
            taps = [sums[c * out2 : (c + 1) * out2, i * 128 : (i + 1) * 128] for c in range(3)]
            v = sum_of_taps(*taps).reshape(plan.block2, plan.c2, 128)
            v = leaky_relu(v + b2[...])
            if q == 0:
                v = jnp.where(place.has_lower, v, 0.0)
            if k == 0:
                v = jnp.concatenate([jnp.where(place.has_above, v[:1], 0.0), v[1:]], axis=0)
            blocks.setdefault(q, []).append(v.reshape(out2, 128).astype(BF))
    return {q: jnp.concatenate(parts, axis=0) for q, parts in blocks.items()}


def layer_three(plan, layer_two, t3, b3, out):
    n3, rows = plan.out3, plan.block3
    for chunk in in_twos(range(plan.depth // 2)):
        for y in range(0, plan.r3, 2 * rows):
            halves = []
            for odd in range(2):
                x = []
                for f in chunk:
                    planes = [layer_two(2 * f + a) for a in range(3)]
                    x.append(blocks_of(planes, plan.k3, 2 * rows * plan.c2, plan.in3, y // rows + odd))
                x = jnp.concatenate(x, axis=1)
                halves.append(jnp.dot(t3[odd], x, preferred_element_type=F32))
            for i, f in enumerate(chunk):
                first, second = (
                    sum_of_even_taps(
                        *(half[c * n3 : (c + 1) * n3, i * 128 : (i + 1) * 128] for c in range(3))
                    ).reshape(plan.c3 // 2, 2 * rows, 128)
                    for half in halves
                )
                sub = lax.broadcasted_iota(jnp.int32, first.shape, 1)
                one = jnp.where(sub < rows, first, second)
                other = jnp.where(sub < rows, second, first)
                other = jnp.concatenate([other[:, rows:], other[:, :rows]], axis=1)
                v = jnp.stack([one, other], axis=1).reshape(plan.c3, 2 * rows, 128)
                v = leaky_relu(v + b3[:, y : y + 2 * rows])
                out[:, f, y : y + 2 * rows] = v[:, :, :64].astype(BF)


def lower_half(plan, place, own, halo, middle, t1, t2, b1, b2):
    pieces = [piece(plan, rim_rows(plan, place, halo, p, place.has_lower)) for p in range(3)]
    pieces += [piece(plan, own_rows(own, p)) for p in range(2)]
    rim = layer_one(plan, place, pieces, range(3), t1, b1)
    return layer_two(plan, place, lambda p: rim[p] if p in rim else middle[p - 3], range(3), t2, b2)


def upper_half(plan, place, own, halo, middle, t1, t2, b1, b2):
    depth = plan.depth
    pieces = [None] * (depth + 1)
    pieces += [piece(plan, own_rows(own, p)) for p in (depth - 2, depth - 1)]
    pieces += [piece(plan, rim_rows(plan, place, halo, p, place.has_upper)) for p in range(2)]
    rim = layer_one(plan, place, pieces, range(depth + 1, depth + 3), t1, b1)
    some = lambda p: rim[p] if p in rim else middle[p - 3]
    return layer_two(plan, place, some, range(3, depth + 1), t2, b2)


def own_kernel(plan, own, t1, b1, middle):
    place, depth = Place(), plan.depth
    pieces = [None] * 3 + [piece(plan, own_rows(own, p)) for p in range(depth)]
    for p, v in layer_one(plan, place, pieces, range(3, depth + 1), t1, b1).items():
        middle[p - 3] = v


def early_kernel(plan, own, got, middle, t1, t2, b1, b2, done):
    place = Place()

    def run(half):
        for q, v in half(plan, place, own, got, middle, t1, t2, b1, b2).items():
            done[q] = v

    pl.when(place.faces_lower)(lambda: run(lower_half))
    pl.when(jnp.logical_not(place.faces_lower))(lambda: run(upper_half))


def late_kernel(plan, own, other, middle, done, t1, t2, b1, b2, t3, b3, out):
    place = Place()

    def run(half):
        late = half(plan, place, own, other, middle, t1, t2, b1, b2)
        layer_three(plan, lambda q: late[q] if q in late else done[q], t3, b3, out)

    pl.when(place.faces_lower)(lambda: run(upper_half))
    pl.when(jnp.logical_not(place.faces_lower))(lambda: run(lower_half))


def gathered(plane, tiles, beside):
    beside, ready = list(beside), []
    if tiles & (tiles - 1):
        return lax.all_gather(plane, "tile", axis=0, tiled=True), *sum(map(tuple, beside), ())
    tile, size, held = lax.axis_index("tile"), 1, plane
    while size < tiles:
        taken = lax.ppermute(held, "tile", [(t, t ^ (2 * size - 1)) for t in range(tiles)])
        if beside:
            taken, *made = lax.optimization_barrier((taken, *beside.pop(0)))
            ready += made
        upper = (tile // size) % 2 == 1
        held = jnp.where(
            upper,
            jnp.concatenate([taken, held], axis=0),
            jnp.concatenate([held, taken], axis=0),
        )
        size *= 2
    return held, *ready, *sum(map(tuple, beside), ())


def even_odd(cube):
    width = cube.shape[2]
    row = lax.broadcasted_iota(jnp.int32, (width, width), 0)
    col = lax.broadcasted_iota(jnp.int32, (width, width), 1)
    order = (row == 2 * (col % (width // 2)) + col // (width // 2)).astype(BF)
    return jnp.einsum("pyx,xw->pyw", cube.astype(BF), order, preferred_element_type=F32).astype(BF)


def freq_pairs(groups, tiles):
    pairs = []
    for g in range(groups):
        for t in range(tiles):
            to = g + 1 if t % 2 == 0 else g - 1
            target = (to, t ^ 1) if 0 <= to < groups else (g, (t + 2) % tiles)
            pairs.append((g * tiles + t, target[0] * tiles + target[1]))
    return pairs


def body(sky_cube, kernel_one, bias_one, kernel_two, bias_two, kernel_three, bias_three):
    tiles, groups = lax.axis_size("tile"), lax.axis_size("freq")
    strip = sky_cube.shape[1] // tiles
    depth = tiles * sky_cube.shape[0]
    c1, c2, c3 = (kernel.shape[0] for kernel in (kernel_one, kernel_two, kernel_three))
    plan = Plan(strip, depth, c1, c2, c3)
    tile = lax.axis_index("tile")

    w1 = jnp.transpose(kernel_one[:, 0], (1, 2, 3, 0))
    w2 = jnp.transpose(kernel_two, (2, 3, 4, 0, 1))
    w3 = jnp.transpose(kernel_three, (2, 3, 4, 1, 0))

    params = pltpu.CompilerParams(vmem_limit_bytes=32 * 2**20)
    bands_12 = pl.pallas_call(
        functools.partial(bands_12_kernel, plan),
        name="bands_12",
        out_shape=[
            jax.ShapeDtypeStruct((plan.n1, plan.k1), BF),
            jax.ShapeDtypeStruct((3 * plan.out2, plan.k2), BF),
            jax.ShapeDtypeStruct((c1, 128), F32),
            jax.ShapeDtypeStruct((c2, 128), F32),
            jax.ShapeDtypeStruct((c3, plan.r3, 128), F32),
        ],
        in_specs=[VM] * 5,
        out_specs=[VM] * 5,
        compiler_params=params,
    )(bias_one[None], bias_two[None], bias_three[None], w1, w2)
    planes = even_odd(sky_cube)
    own, t1, t2, b1, b2, b3 = gathered(planes, tiles, [(), bands_12])
    padded = jnp.pad(own, ((0, 0), (plan.rim, plan.rim), (0, 0)))
    width = own.shape[2]
    begin = (jnp.where(faces_lower(tile), 0, depth - 3), (tile // 2) * 2 * strip, 0)
    message = lax.dynamic_slice(padded, begin, (3, plan.span, width))
    message, w3 = lax.optimization_barrier((message, w3))
    got = lax.ppermute(message, ("freq", "tile"), freq_pairs(groups, tiles))
    own = lax.dynamic_slice(padded, (0, tile * strip, 0), (depth, plan.slots, width))
    bands_3 = pl.pallas_call(
        functools.partial(bands_3_kernel, plan),
        name="bands_3",
        out_shape=jax.ShapeDtypeStruct((2, 3 * plan.out3, plan.k3), BF),
        in_specs=[VM],
        out_specs=VM,
        compiler_params=params,
    )(w3)

    middle = pl.pallas_call(
        functools.partial(own_kernel, plan),
        name="own",
        out_shape=jax.ShapeDtypeStruct((depth - 2, plan.n1, 128), BF),
        in_specs=[VM] * 3,
        out_specs=VM,
        compiler_params=params,
    )(own, t1, b1)
    got, t3, middle = lax.optimization_barrier((got, bands_3, middle))
    other = lax.ppermute(got, "tile", [(t, t ^ 1) for t in range(tiles)])
    done = pl.pallas_call(
        functools.partial(early_kernel, plan),
        name="early",
        out_shape=jax.ShapeDtypeStruct((plan.planes2, plan.n2, 128), BF),
        in_specs=[VM] * 7,
        out_specs=VM,
        compiler_params=params,
    )(own, got, middle, t1, t2, b1, b2)
    other, done = lax.optimization_barrier((other, done))
    return pl.pallas_call(
        functools.partial(late_kernel, plan),
        name="late",
        out_shape=jax.ShapeDtypeStruct((c3, depth // 2, plan.r3, width // 2), BF),
        in_specs=[VM] * 10,
        out_specs=VM,
        compiler_params=params,
    )(own, other, middle, done, t1, t2, b1, b2, t3, b3)


def solution(mesh):
    return jax.shard_map(
        body,
        mesh=mesh,
        in_specs=(P(("freq", "tile"), None, None), P(), P(), P(), P(), P(), P()),
        out_specs=P(None, "freq", "tile", None),
        check_vma=False,
    )
```

time: 109 us -> 13.2 us (0.12)
  the two profiles are of different devices: /device:TPU:0 before, /device:TPU:19 now
where the time goes in v3:
time: 13.2 us; the launch traced here: 13 us
  starting transfers between devices  4.11 us (31%)
  waiting for transfers between devices  3.5 us (27%)
  Pallas kernels  3.4 us (26%)
  local copies, waits for them, and re-layouts  0.93 us (7%)
  matrix products  0.9 us (7%)
    ppermute x2, starting transfers between devices, gathered(): lax.ppermute(held, 'tile', [(t, t ^ 2 * size - 1) for t in range(tiles)])  2.21 us
    ppermute x1, waiting for transfers between devices, body(): got = lax.ppermute(message, ('freq', 'tile'), freq_pairs(groups, tiles))  1.68 us
    ppermute x2, waiting for transfers between devices, gathered(): lax.ppermute(held, 'tile', [(t, t ^ 2 * size - 1) for t in range(tiles)])  1.64 us
    pallas_call x1, Pallas kernels, body(): pl.pallas_call(functools.partial(late_kernel, plan), name='late', out_sha...  1.48 us
    ppermute x1, starting transfers between devices, body(): other = lax.ppermute(got, 'tile', [(t, t ^ 1) for t in range(tiles)])  1.29 us
    dot_general x1, matrix products, even_odd(): jnp.einsum('pyx,xw->pyw', cube.astype(BF), order, preferred_element_type=...  0.9 us
    unnamed x12, local copies, waits for them, and re-layouts  0.88 us
    pallas_call x1, Pallas kernels, body(): pl.pallas_call(functools.partial(early_kernel, plan), name='early', out_s...  0.67 us
  transfers between devices with their start and end apart: 4, of which 4 were waited for; matrix products, arithmetic and copies ran while one was open for 0% of the time, Pallas kernels for 15%

profile of v3, /device:TPU:19, one launch (start us, length us, event | category | flops | bytes accessed | tf_op | source)
XLA Modules:
  0.0 13.0 jit_solution(1525602805371434727)
XLA Ops:
  0.0 0.9 %fusion = bf16[1,64,128]{2,1,0:T(8,128)(2,1)S(1)} fusion(s32[128]{0:T(128)S(1)} %get-tuple-element.43, s32[128]{0:T(128)S(1)} %get-tuple-element.45, s32[128]{0:T(128)S(1)} %get-tuple-element.44, s32[128]{0:T(128)S(1)} %get-tuple-element.46, pred[128]{0:T(512)(128)(4,1)S(1)} %get-tuple-element.41, pred[128]{0:T(512)(128)(4,1)S(1)} %get-tuple-element.42, ...), kind=kOutput, calls=%fused_computation.1 | convolution fusion | flops 2195456 | bytes 51456 | tf_op jit(solution)/shard_map/pyx,xw->pyw/dot_general | solution.py:331
  0.9 0.7 %collective-permute-start = (bf16[1,64,128]{2,1,0:T(8,128)(2,1)S(1)}, bf16[1,64,128]{2,1,0:T(8,128)(2,1)S(1)}, u32[]{:S(2)}, u32[]{:S(2)}) collective-permute-start(bf16[1,64,128]{2,1,0:T(8,128)(2,1)S(1)} %fusion), channel_id=1, source_target_pairs={{0,1},{1,0},{2,3},{3,2},{4,5},{5,4},{6,7},{7,6},{8,9},{9,8},{10,11... | collective-permute-start | bytes 49160 | tf_op jit(solution)/shard_map/ppermute | solution.py:312
  1.6 0.0 copy-start
  1.6 0.8 %collective-permute-done = bf16[1,64,128]{2,1,0:T(8,128)(2,1)S(1)} collective-permute-done((bf16[1,64,128]{2,1,0:T(8,128)(2,1)S(1)}, bf16[1,64,128]{2,1,0:T(8,128)(2,1)S(1)}, u32[]{:S(2)}, u32[]{:S(2)}) %collective-permute-start) | collective-permute-done | bytes 16416 | tf_op jit(solution)/shard_map/ppermute | solution.py:312
  2.5 1.5 %collective-permute-start.1 = (bf16[2,64,128]{2,1,0:T(8,128)(2,1)S(1)}, bf16[2,64,128]{2,1,0:T(8,128)(2,1)S(1)}, u32[]{:S(2)}, u32[]{:S(2)}) collective-permute-start(bf16[2,64,128]{2,1,0:T(8,128)(2,1)S(1)} %maximum_select_fusion.1), channel_id=1, source_target_pairs={{0,3},{1,2},{2,1},{3,0},{4,7},{5,6},{6,5},{7,4},{8,11},{9,10},{10,... | collective-permute-start | bytes 98312 | tf_op jit(solution)/shard_map/ppermute | solution.py:312
  4.0 0.0 copy-start.2
  4.0 0.0 copy-start.3
  4.0 0.0 copy-start.4
  4.0 0.0 copy-start.5
  4.0 0.0 copy-done
  4.0 0.7 %copy-done.2 = bf16[8,1,3,3,3]{0,4,3,2,1:T(4,128)(2,1)S(1)} copy-done((bf16[8,1,3,3,3]{0,4,3,2,1:T(4,128)(2,1)S(1)}, bf16[8,1,3,3,3]{0,4,3,2,1:T(4,128)(2,1)}, u32[]{:S(2)}) %copy-start.2) | copy-done | bytes 456
  4.7 0.0 copy-done.3
  4.7 0.0 copy-done.4
  4.7 0.0 copy-done.5
  4.7 0.4 %bands_12.1 = (bf16[160,256]{1,0:T(8,128)(2,1)S(1)}, bf16[144,256]{1,0:T(8,128)(2,1)S(1)}, f32[8,128]{1,0:T(8,128)S(1)}, f32[8,128]{1,0:T(8,128)S(1)}, f32[16,8,128]{2,1,0:T(8,128)S(1)}) custom-call(f32[1,8]{1,0:T(1,128)S(1)} %bitcast.18, f32[1,8]{1,0:T(1,128)S(1)} %bitcast.19, f32[1,16]{1,0:T(1,128)S(1)} %bitcast.20, bf16[3,3,3,8]{3,2,1,0:T(4,128)(2,1)S(1)} %bitcast.17, ...), custom_call_target="tpu_custom_call" | custom-call | tf_op jit(solution)/shard_map/bands_12/pallas_call | solution.py:357
  5.1 0.8 %collective-permute-done.1 = bf16[2,64,128]{2,1,0:T(8,128)(2,1)S(1)} collective-permute-done((bf16[2,64,128]{2,1,0:T(8,128)(2,1)S(1)}, bf16[2,64,128]{2,1,0:T(8,128)(2,1)S(1)}, u32[]{:S(2)}, u32[]{:S(2)}) %collective-permute-start.1) | collective-permute-done | bytes 32800 | tf_op jit(solution)/shard_map/ppermute | solution.py:312
  5.9 0.0 copy-start.1
  5.9 0.6 %collective-permute-start.2 = (bf16[3,40,128]{2,1,0:T(8,128)(2,1)S(1)}, bf16[3,40,128]{2,1,0:T(8,128)(2,1)S(1)}, u32[]{:S(2)}, u32[]{:S(2)}) collective-permute-start(bf16[3,40,128]{2,1,0:T(8,128)(2,1)S(1)} %pad_dynamic-slice_fusion), channel_id=1, source_target_pairs={{0,5},{1,3},{2,7},{3,1},{4,9},{5,0},{6,11},{7,2},{8,13},{9,4},{10,... | collective-permute-start | bytes 92168 | tf_op jit(solution)/shard_map/ppermute | solution.py:378
  6.6 0.2 %copy-done.1 = bf16[16,8,3,3,3]{0,1,4,3,2:T(8,128)(2,1)S(1)} copy-done((bf16[16,8,3,3,3]{0,1,4,3,2:T(8,128)(2,1)S(1)}, bf16[16,8,3,3,3]{0,1,4,3,2:T(8,128)(2,1)}, u32[]{:S(2)}) %copy-start.1) | copy-done | bytes 6936
  6.7 0.6 %bands_3.1.t3 = bf16[2,192,256]{2,1,0:T(8,128)(2,1)S(1)} custom-call(bf16[3,3,3,8,16]{4,3,2,1,0:T(8,128)(2,1)S(1)} %bitcast.16), custom_call_target="tpu_custom_call" | custom-call | tf_op jit(solution)/shard_map/bands_3/pallas_call | solution.py:380
  7.4 0.3 %own.1.middle = bf16[2,160,128]{2,1,0:T(8,128)(2,1)S(1)} custom-call(bf16[4,24,128]{2,1,0:T(8,128)(2,1)S(1)} %pad_dynamic-slice_fusion.1.own, bf16[160,256]{1,0:T(8,128)(2,1)S(1)} %get-tuple-element.31.t1, f32[8,128]{1,0:T(8,128)S(1)} %get-tuple-element.32.b1), custom_call_target="tpu_custom_call" | custom-call | tf_op jit(solution)/shard_map/own/pallas_call | solution.py:389
  7.6 1.7 %collective-permute-done.2.got = bf16[3,40,128]{2,1,0:T(8,128)(2,1)S(1)} collective-permute-done((bf16[3,40,128]{2,1,0:T(8,128)(2,1)S(1)}, bf16[3,40,128]{2,1,0:T(8,128)(2,1)S(1)}, u32[]{:S(2)}, u32[]{:S(2)}) %collective-permute-start.2) | collective-permute-done | bytes 30752 | tf_op jit(solution)/shard_map/ppermute | solution.py:378
  9.3 1.3 %collective-permute-start.3 = (bf16[3,40,128]{2,1,0:T(8,128)(2,1)S(1)}, bf16[3,40,128]{2,1,0:T(8,128)(2,1)S(1)}, u32[]{:S(2)}, u32[]{:S(2)}) collective-permute-start(bf16[3,40,128]{2,1,0:T(8,128)(2,1)S(1)} %collective-permute-done.2.got), channel_id=1, source_target_pairs={{0,1},{1,0},{2,3},{3,2},{4,5},{5,4},{6,7},{7,6},{8,9},{9,8},{10,11... | collective-permute-start | bytes 92168 | tf_op jit(solution)/shard_map/ppermute | solution.py:398
  10.6 0.7 %early.1.done = bf16[5,144,128]{2,1,0:T(8,128)(2,1)S(1)} custom-call(bf16[4,24,128]{2,1,0:T(8,128)(2,1)S(1)} %pad_dynamic-slice_fusion.1.own, bf16[3,40,128]{2,1,0:T(8,128)(2,1)S(1)} %collective-permute-done.2.got, bf16[2,160,128]{2,1,0:T(8,128)(2,1)S(1)} %own.1.middle, bf16[160,256]{1,0:T(8,128)(2,1)S(1)} %get-tuple-element.31.t1, ...), custom_call_target="tpu_custom_call" | custom-call | tf_op jit(solution)/shard_map/early/pallas_call | solution.py:399
  11.3 0.2 %collective-permute-done.3.other = bf16[3,40,128]{2,1,0:T(8,128)(2,1)S(1)} collective-permute-done((bf16[3,40,128]{2,1,0:T(8,128)(2,1)S(1)}, bf16[3,40,128]{2,1,0:T(8,128)(2,1)S(1)}, u32[]{:S(2)}, u32[]{:S(2)}) %collective-permute-start.3) | collective-permute-done | bytes 30752 | tf_op jit(solution)/shard_map/ppermute | solution.py:398
  11.5 1.5 %late.1 = bf16[16,2,8,64]{3,2,1,0:T(8,128)(2,1)} custom-call(bf16[4,24,128]{2,1,0:T(8,128)(2,1)S(1)} %pad_dynamic-slice_fusion.1.own, bf16[3,40,128]{2,1,0:T(8,128)(2,1)S(1)} %collective-permute-done.3.other, bf16[2,160,128]{2,1,0:T(8,128)(2,1)S(1)} %own.1.middle, bf16[5,144,128]{2,1,0:T(8,128)(2,1)S(1)} %early.1.done, ...), custom_call_target="tpu_custom_call" | custom-call | tf_op jit(solution)/shard_map/late/pallas_call | solution.py:408
  (7 shorter events, 0.1 us)
Async XLA Ops:
  0.9 1.5 %collective-permute-start = (bf16[1,64,128]{2,1,0:T(8,128)(2,1)S(1)}, bf16[1,64,128]{2,1,0:T(8,128)(2,1)S(1)}, u32[]{:S(2)}, u32[]{:S(2)}) collective-permute-start(bf16[1,64,128]{2,1,0:T(8,128)(2,1)S(1)} %fusion), channel_id=1, source_target_pairs={{0,1},{1,0},{2,3},{3,2},{4,5},{5,4},{6,7},{7,6},{8,9},{9,8},{10,11... | collective-permute-start | bytes 49160 | tf_op jit(solution)/shard_map/ppermute | solution.py:312
  1.6 2.4 %copy-start = (bf16[8,8,3,3,3]{1,0,4,3,2:T(8,128)(2,1)S(1)}, bf16[8,8,3,3,3]{1,0,4,3,2:T(8,128)(2,1)}, u32[]{:S(2)}) copy-start(bf16[8,8,3,3,3]{1,0,4,3,2:T(8,128)(2,1)} %param.10) | copy-start | bytes 10372
  2.5 3.4 %collective-permute-start.1 = (bf16[2,64,128]{2,1,0:T(8,128)(2,1)S(1)}, bf16[2,64,128]{2,1,0:T(8,128)(2,1)S(1)}, u32[]{:S(2)}, u32[]{:S(2)}) collective-permute-start(bf16[2,64,128]{2,1,0:T(8,128)(2,1)S(1)} %maximum_select_fusion.1), channel_id=1, source_target_pairs={{0,3},{1,2},{2,1},{3,0},{4,7},{5,6},{6,5},{7,4},{8,11},{9,10},{10,... | collective-permute-start | bytes 98312 | tf_op jit(solution)/shard_map/ppermute | solution.py:312
  4.0 0.7 %copy-start.2 = (bf16[8,1,3,3,3]{0,4,3,2,1:T(4,128)(2,1)S(1)}, bf16[8,1,3,3,3]{0,4,3,2,1:T(4,128)(2,1)}, u32[]{:S(2)}) copy-start(bf16[8,1,3,3,3]{0,4,3,2,1:T(4,128)(2,1)} %param.8) | copy-start | bytes 1300
  4.0 0.7 %copy-start.3 = (f32[8]{0:T(128)S(1)}, f32[8]{0:T(128)}, u32[]{:S(2)}) copy-start(f32[8]{0:T(128)} %param.9) | copy-start | bytes 100
  4.0 0.7 %copy-start.4 = (f32[8]{0:T(128)S(1)}, f32[8]{0:T(128)}, u32[]{:S(2)}) copy-start(f32[8]{0:T(128)} %param.11) | copy-start | bytes 100
  4.0 0.7 %copy-start.5 = (f32[16]{0:T(128)S(1)}, f32[16]{0:T(128)}, u32[]{:S(2)}) copy-start(f32[16]{0:T(128)} %param.13) | copy-start | bytes 196
  5.9 0.8 %copy-start.1 = (bf16[16,8,3,3,3]{0,1,4,3,2:T(8,128)(2,1)S(1)}, bf16[16,8,3,3,3]{0,1,4,3,2:T(8,128)(2,1)}, u32[]{:S(2)}) copy-start(bf16[16,8,3,3,3]{0,1,4,3,2:T(8,128)(2,1)} %param.12) | copy-start | bytes 20740
  5.9 3.4 %collective-permute-start.2 = (bf16[3,40,128]{2,1,0:T(8,128)(2,1)S(1)}, bf16[3,40,128]{2,1,0:T(8,128)(2,1)S(1)}, u32[]{:S(2)}, u32[]{:S(2)}) collective-permute-start(bf16[3,40,128]{2,1,0:T(8,128)(2,1)S(1)} %pad_dynamic-slice_fusion), channel_id=1, source_target_pairs={{0,5},{1,3},{2,7},{3,1},{4,9},{5,0},{6,11},{7,2},{8,13},{9,4},{10,... | collective-permute-start | bytes 92168 | tf_op jit(solution)/shard_map/ppermute | solution.py:378
  9.3 2.2 %collective-permute-start.3 = (bf16[3,40,128]{2,1,0:T(8,128)(2,1)S(1)}, bf16[3,40,128]{2,1,0:T(8,128)(2,1)S(1)}, u32[]{:S(2)}, u32[]{:S(2)}) collective-permute-start(bf16[3,40,128]{2,1,0:T(8,128)(2,1)S(1)} %collective-permute-done.2.got), channel_id=1, source_target_pairs={{0,1},{1,0},{2,3},{3,2},{4,5},{5,4},{6,7},{7,6},{8,9},{9,8},{10,11... | collective-permute-start | bytes 92168 | tf_op jit(solution)/shard_map/ppermute | solution.py:398

commit v4 on v3

--- a/solution.py
+++ b/solution.py
@@ -160,14 +160,13 @@
     return here + turned(after, 64) + jnp.where(lane == 0, zero, turned(before, 65))
 
 
-def own_rows(own, plane):
-    return own[plane].astype(F32)
+def own_rows(plan, place, ref, plane):
+    rows = ref[plane].astype(F32)
+    return jnp.where(place.second, rows[plan.strip :], rows[: plan.slots])
 
 
 def rim_rows(plan, place, ref, plane, inside):
-    rows = ref[plane].astype(F32)
-    rows = jnp.where(place.second, rows[plan.strip :], rows[: plan.slots])
-    return jnp.where(inside, rows, 0.0)
+    return jnp.where(inside, own_rows(plan, place, ref, plane), 0.0)
 
 
 def piece(plan, rows):
@@ -259,7 +258,7 @@
 
 def lower_half(plan, place, own, halo, middle, t1, t2, b1, b2):
     pieces = [piece(plan, rim_rows(plan, place, halo, p, place.has_lower)) for p in range(3)]
-    pieces += [piece(plan, own_rows(own, p)) for p in range(2)]
+    pieces += [piece(plan, own_rows(plan, place, own, p)) for p in range(2)]
     rim = layer_one(plan, place, pieces, range(3), t1, b1)
     return layer_two(plan, place, lambda p: rim[p] if p in rim else middle[p - 3], range(3), t2, b2)
 
@@ -267,7 +266,7 @@
 def upper_half(plan, place, own, halo, middle, t1, t2, b1, b2):
     depth = plan.depth
     pieces = [None] * (depth + 1)
-    pieces += [piece(plan, own_rows(own, p)) for p in (depth - 2, depth - 1)]
+    pieces += [piece(plan, own_rows(plan, place, own, p)) for p in (depth - 2, depth - 1)]
     pieces += [piece(plan, rim_rows(plan, place, halo, p, place.has_upper)) for p in range(2)]
     rim = layer_one(plan, place, pieces, range(depth + 1, depth + 3), t1, b1)
     some = lambda p: rim[p] if p in rim else middle[p - 3]
@@ -276,7 +275,7 @@
 
 def own_kernel(plan, own, t1, b1, middle):
     place, depth = Place(), plan.depth
-    pieces = [None] * 3 + [piece(plan, own_rows(own, p)) for p in range(depth)]
+    pieces = [None] * 3 + [piece(plan, own_rows(plan, place, own, p)) for p in range(depth)]
     for p, v in layer_one(plan, place, pieces, range(3, depth + 1), t1, b1).items():
         middle[p - 3] = v
 
@@ -303,24 +302,63 @@
     pl.when(jnp.logical_not(place.faces_lower))(lambda: run(lower_half))
 
 
-def gathered(plane, tiles, beside):
-    beside, ready = list(beside), []
+def in_order(upper, held, taken):
+    return jnp.where(
+        upper,
+        jnp.concatenate([taken, held], axis=0),
+        jnp.concatenate([held, taken], axis=0),
+    )
+
+
+def chip_rows(plan, planes, chip):
+    padded = jnp.pad(planes, ((0, 0), (plan.rim, plan.rim), (0, 0)))
+    shape = (planes.shape[0], plan.span, planes.shape[2])
+    return lax.dynamic_slice(padded, (0, chip * 2 * plan.strip, 0), shape)
+
+
+def freq_pairs(groups, tiles, flip):
+    pairs = []
+    for g in range(groups):
+        for t in range(tiles):
+            to = g + 1 if t % 2 == 0 else g - 1
+            target = (to, t ^ flip) if 0 <= to < groups else (g, (t + 2) % tiles)
+            pairs.append((g * tiles + t, target[0] * tiles + target[1]))
+    return pairs
+
+
+def gathered(plan, plane, tiles):
     if tiles & (tiles - 1):
-        return lax.all_gather(plane, "tile", axis=0, tiled=True), *sum(map(tuple, beside), ())
+        held = lax.all_gather(plane, "tile", axis=0, tiled=True)
+        return chip_rows(plan, held, lax.axis_index("tile") // 2)
     tile, size, held = lax.axis_index("tile"), 1, plane
     while size < tiles:
         taken = lax.ppermute(held, "tile", [(t, t ^ (2 * size - 1)) for t in range(tiles)])
-        if beside:
-            taken, *made = lax.optimization_barrier((taken, *beside.pop(0)))
-            ready += made
-        upper = (tile // size) % 2 == 1
-        held = jnp.where(
-            upper,
-            jnp.concatenate([taken, held], axis=0),
-            jnp.concatenate([held, taken], axis=0),
-        )
+        held = in_order((tile // size) % 2 == 1, held, taken)
         size *= 2
-    return held, *ready, *sum(map(tuple, beside), ())
+    return chip_rows(plan, held, tile // 2)
+
+
+def some_planes(planes, tile):
+    begin = (jnp.where(faces_lower(tile), planes.shape[0] - 3, 0), 0, 0)
+    return lax.dynamic_slice(planes, begin, (3, *planes.shape[1:]))
+
+
+def exchanged(plan, plane, groups, tiles, weights):
+    axes, tile = ("freq", "tile"), lax.axis_index("tile")
+    if tiles != 4:
+        own = gathered(plan, plane, tiles)
+        message = some_planes(own, tile + 1)
+        return own, lax.ppermute(message, axes, freq_pairs(groups, tiles, 1)), weights
+    taken = lax.ppermute(plane, "tile", [(t, t ^ 1) for t in range(tiles)])
+    pair = in_order(tile % 2 == 1, plane, taken)
+    chip = tile // 2
+    mine, theirs = chip_rows(plan, pair, chip), chip_rows(plan, pair, 1 - chip)
+    across = lax.ppermute(theirs, "tile", [(t, t ^ 3) for t in range(tiles)])
+    ahead = lax.ppermute(mine, axes, freq_pairs(groups, tiles, 1))
+    aside = lax.ppermute(theirs, axes, freq_pairs(groups, tiles, 3))
+    across, *weights = lax.optimization_barrier((across, *weights))
+    own = in_order(chip == 1, mine, across)
+    return own, some_planes(in_order(chip == 1, ahead, aside), tile), weights
 
 
 def even_odd(cube):
@@ -329,16 +367,6 @@
     col = lax.broadcasted_iota(jnp.int32, (width, width), 1)
     order = (row == 2 * (col % (width // 2)) + col // (width // 2)).astype(BF)
     return jnp.einsum("pyx,xw->pyw", cube.astype(BF), order, preferred_element_type=F32).astype(BF)
-
-
-def freq_pairs(groups, tiles):
-    pairs = []
-    for g in range(groups):
-        for t in range(tiles):
-            to = g + 1 if t % 2 == 0 else g - 1
-            target = (to, t ^ 1) if 0 <= to < groups else (g, (t + 2) % tiles)
-            pairs.append((g * tiles + t, target[0] * tiles + target[1]))
-    return pairs
 
 
 def body(sky_cube, kernel_one, bias_one, kernel_two, bias_two, kernel_three, bias_three):
@@ -353,6 +381,10 @@
     w2 = jnp.transpose(kernel_two, (2, 3, 4, 0, 1))
     w3 = jnp.transpose(kernel_three, (2, 3, 4, 1, 0))
 
+    own, got, weights = exchanged(
+        plan, even_odd(sky_cube), groups, tiles, (bias_one[None], bias_two[None], bias_three[None], w1, w2, w3)
+    )
+    bias_one, bias_two, bias_three, w1, w2, w3 = weights
     params = pltpu.CompilerParams(vmem_limit_bytes=32 * 2**20)
     bands_12 = pl.pallas_call(
         functools.partial(bands_12_kernel, plan),
@@ -367,16 +399,7 @@
         in_specs=[VM] * 5,
         out_specs=[VM] * 5,
         compiler_params=params,
-    )(bias_one[None], bias_two[None], bias_three[None], w1, w2)
-    planes = even_odd(sky_cube)
-    own, t1, t2, b1, b2, b3 = gathered(planes, tiles, [(), bands_12])
-    padded = jnp.pad(own, ((0, 0), (plan.rim, plan.rim), (0, 0)))
-    width = own.shape[2]
-    begin = (jnp.where(faces_lower(tile), 0, depth - 3), (tile // 2) * 2 * strip, 0)
-    message = lax.dynamic_slice(padded, begin, (3, plan.span, width))
-    message, w3 = lax.optimization_barrier((message, w3))
-    got = lax.ppermute(message, ("freq", "tile"), freq_pairs(groups, tiles))
-    own = lax.dynamic_slice(padded, (0, tile * strip, 0), (depth, plan.slots, width))
+    )(bias_one, bias_two, bias_three, w1, w2)
     bands_3 = pl.pallas_call(
         functools.partial(bands_3_kernel, plan),
         name="bands_3",
@@ -386,6 +409,7 @@
         compiler_params=params,
     )(w3)
 
+    t1, t2, b1, b2, b3 = bands_12
     middle = pl.pallas_call(
         functools.partial(own_kernel, plan),
         name="own",
@@ -408,7 +432,7 @@
     return pl.pallas_call(
         functools.partial(late_kernel, plan),
         name="late",
-        out_shape=jax.ShapeDtypeStruct((c3, depth // 2, plan.r3, width // 2), BF),
+        out_shape=jax.ShapeDtypeStruct((c3, depth // 2, plan.r3, sky_cube.shape[2] // 2), BF),
         in_specs=[VM] * 10,
         out_specs=VM,
         compiler_params=params,

time: 13.2 us -> 12.7 us (0.962)
  the two profiles are of different devices: /device:TPU:19 before, /device:TPU:0 now
where the time goes in v4:
time: 12.7 us; the launch traced here: 12.4 us
  starting transfers between devices  4.74 us (37%)
  Pallas kernels  3.42 us (27%)
  waiting for transfers between devices  3.03 us (24%)
  matrix products  0.9 us (7%)
  local copies, waits for them, and re-layouts  0.18 us (1%)
    ppermute x1, starting transfers between devices, exchanged(): across = lax.ppermute(theirs, 'tile', [(t, t ^ 3) for t in range(tiles)])  2.69 us
    pallas_call x1, Pallas kernels, body(): pl.pallas_call(functools.partial(late_kernel, plan), name='late', out_sha...  1.56 us
    ppermute x1, starting transfers between devices, exchanged(): aside = lax.ppermute(theirs, axes, freq_pairs(groups, tiles, 3))  1.39 us
    ppermute x1, waiting for transfers between devices, exchanged(): aside = lax.ppermute(theirs, axes, freq_pairs(groups, tiles, 3))  1.11 us
    dot_general x1, matrix products, even_odd(): jnp.einsum('pyx,xw->pyw', cube.astype(BF), order, preferred_element_type=...  0.9 us
    ppermute x1, waiting for transfers between devices, exchanged(): taken = lax.ppermute(plane, 'tile', [(t, t ^ 1) for t in range(tiles)])  0.84 us
    pallas_call x1, Pallas kernels, body(): pl.pallas_call(functools.partial(bands_3_kernel, plan), name='bands_3', o...  0.64 us
    pallas_call x1, Pallas kernels, body(): pl.pallas_call(functools.partial(early_kernel, plan), name='early', out_s...  0.59 us
  transfers between devices with their start and end apart: 5, of which 4 were waited for; matrix products, arithmetic and copies ran while one was open for 0% of the time, Pallas kernels for 15%

profile of v4, /device:TPU:0, one launch (start us, length us, event | category | flops | bytes accessed | tf_op | source)
XLA Modules:
  0.0 12.4 jit_solution(167192130851328489)
XLA Ops:
  0.0 0.9 %fusion = bf16[1,64,128]{2,1,0:T(8,128)(2,1)S(1)} fusion(s32[128]{0:T(128)S(1)} %get-tuple-element.43, s32[128]{0:T(128)S(1)} %get-tuple-element.45, s32[128]{0:T(128)S(1)} %get-tuple-element.44, s32[128]{0:T(128)S(1)} %get-tuple-element.46, pred[128]{0:T(512)(128)(4,1)S(1)} %get-tuple-element.41, pred[128]{0:T(512)(128)(4,1)S(1)} %get-tuple-element.42, ...), kind=kOutput, calls=%fused_computation.1 | convolution fusion | flops 2195456 | bytes 51456 | tf_op jit(solution)/shard_map/pyx,xw->pyw/dot_general | solution.py:369
  0.9 0.5 %collective-permute-start = (bf16[1,64,128]{2,1,0:T(8,128)(2,1)S(1)}, bf16[1,64,128]{2,1,0:T(8,128)(2,1)S(1)}, u32[]{:S(2)}, u32[]{:S(2)}) collective-permute-start(bf16[1,64,128]{2,1,0:T(8,128)(2,1)S(1)} %fusion), channel_id=1, source_target_pairs={{0,1},{1,0},{2,3},{3,2},{4,5},{5,4},{6,7},{7,6},{8,9},{9,8},{10,11... | collective-permute-start | bytes 49160 | tf_op jit(solution)/shard_map/ppermute | solution.py:352
  1.4 0.8 %collective-permute-done = bf16[1,64,128]{2,1,0:T(8,128)(2,1)S(1)} collective-permute-done((bf16[1,64,128]{2,1,0:T(8,128)(2,1)S(1)}, bf16[1,64,128]{2,1,0:T(8,128)(2,1)S(1)}, u32[]{:S(2)}, u32[]{:S(2)}) %collective-permute-start) | collective-permute-done | bytes 16416 | tf_op jit(solution)/shard_map/ppermute | solution.py:352
  2.3 0.0 copy-start.1
  2.3 2.7 %collective-permute-start.1 = (bf16[2,40,128]{2,1,0:T(8,128)(2,1)S(1)}, bf16[2,40,128]{2,1,0:T(8,128)(2,1)S(1)}, u32[]{:S(2)}, u32[]{:S(2)}) collective-permute-start(bf16[2,40,128]{2,1,0:T(8,128)(2,1)S(1)} %get-tuple-element.39), channel_id=1, source_target_pairs={{0,3},{1,2},{2,1},{3,0},{4,7},{5,6},{6,5},{7,4},{8,11},{9,10},{10,... | collective-permute-start | bytes 61448 | tf_op jit(solution)/shard_map/ppermute | solution.py:356
  5.0 1.4 %collective-permute-start.2 = (bf16[2,40,128]{2,1,0:T(8,128)(2,1)S(1)}, bf16[2,40,128]{2,1,0:T(8,128)(2,1)S(1)}, u32[]{:S(2)}, u32[]{:S(2)}) collective-permute-start(bf16[2,40,128]{2,1,0:T(8,128)(2,1)S(1)} %get-tuple-element.39), channel_id=1, source_target_pairs={{0,7},{1,3},{2,5},{3,1},{4,11},{5,2},{6,9},{7,0},{8,15},{9,6},{10,... | collective-permute-start | bytes 61448 | tf_op jit(solution)/shard_map/ppermute | solution.py:358
  6.4 0.1 collective-permute-start.3
  6.5 0.0 collective-permute-done.1
  6.5 0.0 copy-done.1
  6.5 0.0 copy-start
  6.5 0.0 copy-start.2
  6.5 0.0 copy-start.3
  6.5 0.0 copy-start.4
  6.6 0.0 copy-start.5
  6.6 0.6 %bands_3.1.t3 = bf16[2,192,256]{2,1,0:T(8,128)(2,1)S(1)} custom-call(bf16[3,3,3,8,16]{4,3,2,1,0:T(8,128)(2,1)S(1)} %bitcast.16), custom_call_target="tpu_custom_call" | custom-call | tf_op jit(solution)/shard_map/bands_3/pallas_call | solution.py:403
  7.2 0.1 copy-done
  7.3 0.0 copy-done.2
  7.3 0.0 copy-done.3
  7.3 0.0 copy-done.4
  7.3 0.0 copy-done.5
  7.3 0.4 %bands_12.1 = (bf16[160,256]{1,0:T(8,128)(2,1)S(1)}, bf16[144,256]{1,0:T(8,128)(2,1)S(1)}, f32[8,128]{1,0:T(8,128)S(1)}, f32[8,128]{1,0:T(8,128)S(1)}, f32[16,8,128]{2,1,0:T(8,128)S(1)}) custom-call(f32[1,8]{1,0:T(1,128)S(1)} %bitcast.18, f32[1,8]{1,0:T(1,128)S(1)} %bitcast.19, f32[1,16]{1,0:T(1,128)S(1)} %bitcast.20, bf16[3,3,3,8]{3,2,1,0:T(4,128)(2,1)S(1)} %bitcast.17, ...), custom_call_target="tpu_custom_call" | custom-call | tf_op jit(solution)/shard_map/bands_12/pallas_call | solution.py:389
  7.7 0.3 %own.1.middle = bf16[2,160,128]{2,1,0:T(8,128)(2,1)S(1)} custom-call(bf16[4,40,128]{2,1,0:T(8,128)(2,1)S(1)} %maximum_select_fusion.own, bf16[160,256]{1,0:T(8,128)(2,1)S(1)} %get-tuple-element.29.t1, f32[8,128]{1,0:T(8,128)S(1)} %get-tuple-element.30.b1), custom_call_target="tpu_custom_call" | custom-call | tf_op jit(solution)/shard_map/own/pallas_call | solution.py:413
  8.0 1.1 %collective-permute-done.2 = bf16[2,40,128]{2,1,0:T(8,128)(2,1)S(1)} collective-permute-done((bf16[2,40,128]{2,1,0:T(8,128)(2,1)S(1)}, bf16[2,40,128]{2,1,0:T(8,128)(2,1)S(1)}, u32[]{:S(2)}, u32[]{:S(2)}) %collective-permute-start.2) | collective-permute-done | bytes 20512 | tf_op jit(solution)/shard_map/ppermute | solution.py:358
  9.1 0.5 %collective-permute-done.3 = bf16[2,40,128]{2,1,0:T(8,128)(2,1)S(1)} collective-permute-done((bf16[2,40,128]{2,1,0:T(8,128)(2,1)S(1)}, bf16[2,40,128]{2,1,0:T(8,128)(2,1)S(1)}, u32[]{:S(2)}, u32[]{:S(2)}) %collective-permute-start.3) | collective-permute-done | bytes 20512 | tf_op jit(solution)/shard_map/ppermute | solution.py:357
  9.6 0.1 collective-permute-start.4
  9.7 0.6 %early.1.done = bf16[5,144,128]{2,1,0:T(8,128)(2,1)S(1)} custom-call(bf16[4,40,128]{2,1,0:T(8,128)(2,1)S(1)} %maximum_select_fusion.own, bf16[3,40,128]{2,1,0:T(8,128)(2,1)S(1)} %fusion.9.got, bf16[2,160,128]{2,1,0:T(8,128)(2,1)S(1)} %own.1.middle, bf16[160,256]{1,0:T(8,128)(2,1)S(1)} %get-tuple-element.29.t1, bf16[144,256]{1,0:T(8,128)(2,1)S(1)} %get-tuple-element.33.t2, ...), custom_call_target="tpu_custom_call" | custom-call | tf_op jit(solution)/shard_map/early/pallas_call | solution.py:423
  10.3 0.6 %collective-permute-done.4.other = bf16[3,40,128]{2,1,0:T(8,128)(2,1)S(1)} collective-permute-done((bf16[3,40,128]{2,1,0:T(8,128)(2,1)S(1)}, bf16[3,40,128]{2,1,0:T(8,128)(2,1)S(1)}, u32[]{:S(2)}, u32[]{:S(2)}) %collective-permute-start.4) | collective-permute-done | bytes 30752 | tf_op jit(solution)/shard_map/ppermute | solution.py:422
  10.9 1.6 %late.1 = bf16[16,2,8,64]{3,2,1,0:T(8,128)(2,1)} custom-call(bf16[4,40,128]{2,1,0:T(8,128)(2,1)S(1)} %maximum_select_fusion.own, bf16[3,40,128]{2,1,0:T(8,128)(2,1)S(1)} %collective-permute-done.4.other, bf16[2,160,128]{2,1,0:T(8,128)(2,1)S(1)} %own.1.middle, bf16[5,144,128]{2,1,0:T(8,128)(2,1)S(1)} %early.1.done, ...), custom_call_target="tpu_custom_call" | custom-call | tf_op jit(solution)/shard_map/late/pallas_call | solution.py:432
  (7 shorter events, 0.1 us)
Async XLA Ops:
  0.9 1.3 %collective-permute-start = (bf16[1,64,128]{2,1,0:T(8,128)(2,1)S(1)}, bf16[1,64,128]{2,1,0:T(8,128)(2,1)S(1)}, u32[]{:S(2)}, u32[]{:S(2)}) collective-permute-start(bf16[1,64,128]{2,1,0:T(8,128)(2,1)S(1)} %fusion), channel_id=1, source_target_pairs={{0,1},{1,0},{2,3},{3,2},{4,5},{5,4},{6,7},{7,6},{8,9},{9,8},{10,11... | collective-permute-start | bytes 49160 | tf_op jit(solution)/shard_map/ppermute | solution.py:352
  2.3 4.2 %copy-start.1 = (bf16[16,8,3,3,3]{0,1,4,3,2:T(8,128)(2,1)S(1)}, bf16[16,8,3,3,3]{0,1,4,3,2:T(8,128)(2,1)}, u32[]{:S(2)}) copy-start(bf16[16,8,3,3,3]{0,1,4,3,2:T(8,128)(2,1)} %param.12) | copy-start | bytes 20740
  2.3 4.2 %collective-permute-start.1 = (bf16[2,40,128]{2,1,0:T(8,128)(2,1)S(1)}, bf16[2,40,128]{2,1,0:T(8,128)(2,1)S(1)}, u32[]{:S(2)}, u32[]{:S(2)}) collective-permute-start(bf16[2,40,128]{2,1,0:T(8,128)(2,1)S(1)} %get-tuple-element.39), channel_id=1, source_target_pairs={{0,3},{1,2},{2,1},{3,0},{4,7},{5,6},{6,5},{7,4},{8,11},{9,10},{10,... | collective-permute-start | bytes 61448 | tf_op jit(solution)/shard_map/ppermute | solution.py:356
  5.0 4.1 %collective-permute-start.2 = (bf16[2,40,128]{2,1,0:T(8,128)(2,1)S(1)}, bf16[2,40,128]{2,1,0:T(8,128)(2,1)S(1)}, u32[]{:S(2)}, u32[]{:S(2)}) collective-permute-start(bf16[2,40,128]{2,1,0:T(8,128)(2,1)S(1)} %get-tuple-element.39), channel_id=1, source_target_pairs={{0,7},{1,3},{2,5},{3,1},{4,11},{5,2},{6,9},{7,0},{8,15},{9,6},{10,... | collective-permute-start | bytes 61448 | tf_op jit(solution)/shard_map/ppermute | solution.py:358
  6.4 3.2 %collective-permute-start.3 = (bf16[2,40,128]{2,1,0:T(8,128)(2,1)S(1)}, bf16[2,40,128]{2,1,0:T(8,128)(2,1)S(1)}, u32[]{:S(2)}, u32[]{:S(2)}) collective-permute-start(bf16[2,40,128]{2,1,0:T(8,128)(2,1)S(1)} %get-tuple-element.40), channel_id=1, source_target_pairs={{0,5},{1,3},{2,7},{3,1},{4,9},{5,0},{6,11},{7,2},{8,13},{9,4},{10,... | collective-permute-start | bytes 61448 | tf_op jit(solution)/shard_map/ppermute | solution.py:357
  6.5 0.8 %copy-start = (bf16[8,8,3,3,3]{1,0,4,3,2:T(8,128)(2,1)S(1)}, bf16[8,8,3,3,3]{1,0,4,3,2:T(8,128)(2,1)}, u32[]{:S(2)}) copy-start(bf16[8,8,3,3,3]{1,0,4,3,2:T(8,128)(2,1)} %param.10) | copy-start | bytes 10372
  6.5 0.8 %copy-start.2 = (bf16[8,1,3,3,3]{0,4,3,2,1:T(4,128)(2,1)S(1)}, bf16[8,1,3,3,3]{0,4,3,2,1:T(4,128)(2,1)}, u32[]{:S(2)}) copy-start(bf16[8,1,3,3,3]{0,4,3,2,1:T(4,128)(2,1)} %param.8) | copy-start | bytes 1300
  6.5 0.8 %copy-start.3 = (f32[8]{0:T(128)S(1)}, f32[8]{0:T(128)}, u32[]{:S(2)}) copy-start(f32[8]{0:T(128)} %param.9) | copy-start | bytes 100
  6.5 0.8 %copy-start.4 = (f32[8]{0:T(128)S(1)}, f32[8]{0:T(128)}, u32[]{:S(2)}) copy-start(f32[8]{0:T(128)} %param.11) | copy-start | bytes 100
  6.6 0.8 %copy-start.5 = (f32[16]{0:T(128)S(1)}, f32[16]{0:T(128)}, u32[]{:S(2)}) copy-start(f32[16]{0:T(128)} %param.13) | copy-start | bytes 196
  9.6 1.3 %collective-permute-start.4 = (bf16[3,40,128]{2,1,0:T(8,128)(2,1)S(1)}, bf16[3,40,128]{2,1,0:T(8,128)(2,1)S(1)}, u32[]{:S(2)}, u32[]{:S(2)}) collective-permute-start(bf16[3,40,128]{2,1,0:T(8,128)(2,1)S(1)} %fusion.9.got), channel_id=1, source_target_pairs={{0,1},{1,0},{2,3},{3,2},{4,5},{5,4},{6,7},{7,6},{8,9},{9,8},{10,11... | collective-permute-start | bytes 92168 | tf_op jit(solution)/shard_map/ppermute | solution.py:422

commit v5 on v4

--- a/solution.py
+++ b/solution.py
@@ -256,36 +256,34 @@
                 out[:, f, y : y + 2 * rows] = v[:, :, :64].astype(BF)
 
 
-def lower_half(plan, place, own, halo, middle, t1, t2, b1, b2):
+def lower_half(plan, place, own, halo, t1, t2, b1, b2, middle=None):
     pieces = [piece(plan, rim_rows(plan, place, halo, p, place.has_lower)) for p in range(3)]
-    pieces += [piece(plan, own_rows(plan, place, own, p)) for p in range(2)]
-    rim = layer_one(plan, place, pieces, range(3), t1, b1)
-    return layer_two(plan, place, lambda p: rim[p] if p in rim else middle[p - 3], range(3), t2, b2)
-
-
-def upper_half(plan, place, own, halo, middle, t1, t2, b1, b2):
+    pieces += [piece(plan, own_rows(plan, place, own, p)) for p in range(plan.depth if middle is None else 2)]
+    made = layer_one(plan, place, pieces, range(plan.depth + 1 if middle is None else 3), t1, b1)
+    some = lambda p: made[p] if p in made else middle[p - 3]
+    return layer_two(plan, place, some, range(3), t2, b2), made
+
+
+def upper_half(plan, place, own, halo, t1, t2, b1, b2, middle=None):
     depth = plan.depth
-    pieces = [None] * (depth + 1)
-    pieces += [piece(plan, own_rows(plan, place, own, p)) for p in (depth - 2, depth - 1)]
+    first = 0 if middle is None else depth - 2
+    pieces = [None] * (3 + first)
+    pieces += [piece(plan, own_rows(plan, place, own, p)) for p in range(first, depth)]
     pieces += [piece(plan, rim_rows(plan, place, halo, p, place.has_upper)) for p in range(2)]
-    rim = layer_one(plan, place, pieces, range(depth + 1, depth + 3), t1, b1)
-    some = lambda p: rim[p] if p in rim else middle[p - 3]
-    return layer_two(plan, place, some, range(3, depth + 1), t2, b2)
-
-
-def own_kernel(plan, own, t1, b1, middle):
-    place, depth = Place(), plan.depth
-    pieces = [None] * 3 + [piece(plan, own_rows(plan, place, own, p)) for p in range(depth)]
-    for p, v in layer_one(plan, place, pieces, range(3, depth + 1), t1, b1).items():
-        middle[p - 3] = v
-
-
-def early_kernel(plan, own, got, middle, t1, t2, b1, b2, done):
+    made = layer_one(plan, place, pieces, range(3 + first, depth + 3), t1, b1)
+    some = lambda p: made[p] if p in made else middle[p - 3]
+    return layer_two(plan, place, some, range(3, depth + 1), t2, b2), made
+
+
+def early_kernel(plan, own, got, t1, t2, b1, b2, done, middle):
     place = Place()
 
     def run(half):
-        for q, v in half(plan, place, own, got, middle, t1, t2, b1, b2).items():
+        planes, made = half(plan, place, own, got, t1, t2, b1, b2)
+        for q, v in planes.items():
             done[q] = v
+        for p in range(3, plan.depth + 1):
+            middle[p - 3] = made[p]
 
     pl.when(place.faces_lower)(lambda: run(lower_half))
     pl.when(jnp.logical_not(place.faces_lower))(lambda: run(upper_half))
@@ -295,7 +293,7 @@
     place = Place()
 
     def run(half):
-        late = half(plan, place, own, other, middle, t1, t2, b1, b2)
+        late, _ = half(plan, place, own, other, t1, t2, b1, b2, middle)
         layer_three(plan, lambda q: late[q] if q in late else done[q], t3, b3, out)
 
     pl.when(place.faces_lower)(lambda: run(upper_half))
@@ -343,22 +341,24 @@
     return lax.dynamic_slice(planes, begin, (3, *planes.shape[1:]))
 
 
-def exchanged(plan, plane, groups, tiles, weights):
+def exchanged(plan, plane, groups, tiles, weights, make_bands):
     axes, tile = ("freq", "tile"), lax.axis_index("tile")
     if tiles != 4:
         own = gathered(plan, plane, tiles)
         message = some_planes(own, tile + 1)
-        return own, lax.ppermute(message, axes, freq_pairs(groups, tiles, 1)), weights
+        return own, lax.ppermute(message, axes, freq_pairs(groups, tiles, 1)), make_bands(weights)
     taken = lax.ppermute(plane, "tile", [(t, t ^ 1) for t in range(tiles)])
     pair = in_order(tile % 2 == 1, plane, taken)
     chip = tile // 2
     mine, theirs = chip_rows(plan, pair, chip), chip_rows(plan, pair, 1 - chip)
+    aside = lax.ppermute(theirs, axes, freq_pairs(groups, tiles, 3))
+    ahead = lax.ppermute(mine, axes, freq_pairs(groups, tiles, 1))
     across = lax.ppermute(theirs, "tile", [(t, t ^ 3) for t in range(tiles)])
-    ahead = lax.ppermute(mine, axes, freq_pairs(groups, tiles, 1))
-    aside = lax.ppermute(theirs, axes, freq_pairs(groups, tiles, 3))
-    across, *weights = lax.optimization_barrier((across, *weights))
+    aside, *weights = lax.optimization_barrier((aside, *weights))
+    bands = make_bands(weights)
+    ahead, *bands = lax.optimization_barrier((ahead, *bands))
     own = in_order(chip == 1, mine, across)
-    return own, some_planes(in_order(chip == 1, ahead, aside), tile), weights
+    return own, some_planes(in_order(chip == 1, ahead, aside), tile), bands
 
 
 def even_odd(cube):
@@ -381,53 +381,50 @@
     w2 = jnp.transpose(kernel_two, (2, 3, 4, 0, 1))
     w3 = jnp.transpose(kernel_three, (2, 3, 4, 1, 0))
 
+    params = pltpu.CompilerParams(vmem_limit_bytes=32 * 2**20)
+
+    def make_bands(weights):
+        bias_one, bias_two, bias_three, w1, w2, w3 = weights
+        bands_12 = pl.pallas_call(
+            functools.partial(bands_12_kernel, plan),
+            name="bands_12",
+            out_shape=[
+                jax.ShapeDtypeStruct((plan.n1, plan.k1), BF),
+                jax.ShapeDtypeStruct((3 * plan.out2, plan.k2), BF),
+                jax.ShapeDtypeStruct((c1, 128), F32),
+                jax.ShapeDtypeStruct((c2, 128), F32),
+                jax.ShapeDtypeStruct((c3, plan.r3, 128), F32),
+            ],
+            in_specs=[VM] * 5,
+            out_specs=[VM] * 5,
+            compiler_params=params,
+        )(bias_one, bias_two, bias_three, w1, w2)
+        bands_3 = pl.pallas_call(
+            functools.partial(bands_3_kernel, plan),
+            name="bands_3",
+            out_shape=jax.ShapeDtypeStruct((2, 3 * plan.out3, plan.k3), BF),
+            in_specs=[VM],
+            out_specs=VM,
+            compiler_params=params,
+        )(w3)
+        return (*bands_12, bands_3)
+
     own, got, weights = exchanged(
-        plan, even_odd(sky_cube), groups, tiles, (bias_one[None], bias_two[None], bias_three[None], w1, w2, w3)
+        plan, even_odd(sky_cube), groups, tiles, (bias_one[None], bias_two[None], bias_three[None], w1, w2, w3), make_bands
     )
-    bias_one, bias_two, bias_three, w1, w2, w3 = weights
-    params = pltpu.CompilerParams(vmem_limit_bytes=32 * 2**20)
-    bands_12 = pl.pallas_call(
-        functools.partial(bands_12_kernel, plan),
-        name="bands_12",
-        out_shape=[
-            jax.ShapeDtypeStruct((plan.n1, plan.k1), BF),
-            jax.ShapeDtypeStruct((3 * plan.out2, plan.k2), BF),
-            jax.ShapeDtypeStruct((c1, 128), F32),
-            jax.ShapeDtypeStruct((c2, 128), F32),
-            jax.ShapeDtypeStruct((c3, plan.r3, 128), F32),
-        ],
-        in_specs=[VM] * 5,
-        out_specs=[VM] * 5,
-        compiler_params=params,
-    )(bias_one, bias_two, bias_three, w1, w2)
-    bands_3 = pl.pallas_call(
-        functools.partial(bands_3_kernel, plan),
-        name="bands_3",
-        out_shape=jax.ShapeDtypeStruct((2, 3 * plan.out3, plan.k3), BF),
-        in_specs=[VM],
-        out_specs=VM,
-        compiler_params=params,
-    )(w3)
-
-    t1, t2, b1, b2, b3 = bands_12
-    middle = pl.pallas_call(
-        functools.partial(own_kernel, plan),
-        name="own",
-        out_shape=jax.ShapeDtypeStruct((depth - 2, plan.n1, 128), BF),
-        in_specs=[VM] * 3,
-        out_specs=VM,
-        compiler_params=params,
-    )(own, t1, b1)
-    got, t3, middle = lax.optimization_barrier((got, bands_3, middle))
+    t1, t2, b1, b2, b3, t3 = weights
     other = lax.ppermute(got, "tile", [(t, t ^ 1) for t in range(tiles)])
-    done = pl.pallas_call(
+    done, middle = pl.pallas_call(
         functools.partial(early_kernel, plan),
         name="early",
-        out_shape=jax.ShapeDtypeStruct((plan.planes2, plan.n2, 128), BF),
-        in_specs=[VM] * 7,
-        out_specs=VM,
+        out_shape=[
+            jax.ShapeDtypeStruct((plan.planes2, plan.n2, 128), BF),
+            jax.ShapeDtypeStruct((depth - 2, plan.n1, 128), BF),
+        ],
+        in_specs=[VM] * 6,
+        out_specs=[VM] * 2,
         compiler_params=params,
-    )(own, got, middle, t1, t2, b1, b2)
+    )(own, got, t1, t2, b1, b2)
     other, done = lax.optimization_barrier((other, done))
     return pl.pallas_call(
         functools.partial(late_kernel, plan),

time: 12.7 us -> 12.2 us (0.961)
  Pallas kernels: 3.42 us -> 3.18 us
  waiting for transfers between devices: 3.03 us -> 2.86 us
    ppermute x1, starting transfers between devices: 2.69 us -> 0.05 us  [exchanged(): across = lax.ppermute(theirs, 'tile', [(t, t ^ 3) for t in range(tiles)])]
    ppermute x1, starting transfers between devices: 1.39 us -> 3.62 us  [exchanged(): aside = lax.ppermute(theirs, axes, freq_pairs(groups, tiles, 3))]
    ppermute x1, waiting for transfers between devices: 0.59 us -> 0.19 us  [body(): other = lax.ppermute(got, 'tile', [(t, t ^ 1) for t in range(tiles)])]
    ppermute x1, waiting for transfers between devices: 0.01 us -> 0.38 us  [exchanged(): across = lax.ppermute(theirs, 'tile', [(t, t ^ 3) for t in range(tiles)])]
    ppermute x1, starting transfers between devices: 0.12 us -> 0.49 us  [exchanged(): ahead = lax.ppermute(mine, axes, freq_pairs(groups, tiles, 1))]
    pallas_call x3 -> x2, Pallas kernels: 1.26 us -> 1.01 us  [the longest x1 0.64 us: make_bands(): pl.pallas_call(functools.partial(bands_3_kernel, plan), name='bands_3', o...]
    ppermute x1, waiting for transfers between devices: 1.11 us -> 0.94 us  [exchanged(): aside = lax.ppermute(theirs, axes, freq_pairs(groups, tiles, 3))]
  transfers between devices with their start and end apart: 5 -> 5, of which waited for: 4 -> 5; matrix products, arithmetic and copies ran while one was open for 0% -> 0% of each run, Pallas kernels for 15% -> 13%
where the time goes in v5:
time: 12.2 us; the launch traced here: 12 us
  starting transfers between devices  4.7 us (39%)
  Pallas kernels  3.18 us (26%)
  waiting for transfers between devices  2.86 us (23%)
  matrix products  0.9 us (7%)
  local copies, waits for them, and re-layouts  0.2 us (2%)
    ppermute x1, starting transfers between devices, exchanged(): aside = lax.ppermute(theirs, axes, freq_pairs(groups, tiles, 3))  3.62 us
    pallas_call x1, Pallas kernels, body(): pl.pallas_call(functools.partial(late_kernel, plan), name='late', out_sha...  1.56 us
    ppermute x1, waiting for transfers between devices, exchanged(): aside = lax.ppermute(theirs, axes, freq_pairs(groups, tiles, 3))  0.94 us
    dot_general x1, matrix products, even_odd(): jnp.einsum('pyx,xw->pyw', cube.astype(BF), order, preferred_element_type=...  0.9 us
    ppermute x1, waiting for transfers between devices, exchanged(): taken = lax.ppermute(plane, 'tile', [(t, t ^ 1) for t in range(tiles)])  0.84 us
    pallas_call x1, Pallas kernels, make_bands(): pl.pallas_call(functools.partial(bands_3_kernel, plan), name='bands_3', o...  0.64 us
    pallas_call x1, Pallas kernels, body(): pl.pallas_call(functools.partial(early_kernel, plan), name='early', out_s...  0.61 us
    ppermute x1, waiting for transfers between devices, exchanged(): ahead = lax.ppermute(mine, axes, freq_pairs(groups, tiles, 1))  0.52 us
  transfers between devices with their start and end apart: 5, of which 5 were waited for; matrix products, arithmetic and copies ran while one was open for 0% of the time, Pallas kernels for 13%

profile of v5, /device:TPU:0, one launch (start us, length us, event | category | flops | bytes accessed | tf_op | source)
XLA Modules:
  0.0 12.0 jit_solution(14570636127773359552)
XLA Ops:
  0.0 0.9 %fusion = bf16[1,64,128]{2,1,0:T(8,128)(2,1)S(1)} fusion(s32[128]{0:T(128)S(1)} %get-tuple-element.55, s32[128]{0:T(128)S(1)} %get-tuple-element.57, s32[128]{0:T(128)S(1)} %get-tuple-element.56, s32[128]{0:T(128)S(1)} %get-tuple-element.58, pred[128]{0:T(512)(128)(4,1)S(1)} %get-tuple-element.53, pred[128]{0:T(512)(128)(4,1)S(1)} %get-tuple-element.54, ...), kind=kOutput, calls=%fused_computation.1 | convolution fusion | flops 2195456 | bytes 51456 | tf_op jit(solution)/shard_map/pyx,xw->pyw/dot_general | solution.py:369
  0.9 0.5 %collective-permute-start = (bf16[1,64,128]{2,1,0:T(8,128)(2,1)S(1)}, bf16[1,64,128]{2,1,0:T(8,128)(2,1)S(1)}, u32[]{:S(2)}, u32[]{:S(2)}) collective-permute-start(bf16[1,64,128]{2,1,0:T(8,128)(2,1)S(1)} %fusion), channel_id=1, source_target_pairs={{0,1},{1,0},{2,3},{3,2},{4,5},{5,4},{6,7},{7,6},{8,9},{9,8},{10,11... | collective-permute-start | bytes 49160 | tf_op jit(solution)/shard_map/ppermute | solution.py:350
  1.4 0.8 %collective-permute-done = bf16[1,64,128]{2,1,0:T(8,128)(2,1)S(1)} collective-permute-done((bf16[1,64,128]{2,1,0:T(8,128)(2,1)S(1)}, bf16[1,64,128]{2,1,0:T(8,128)(2,1)S(1)}, u32[]{:S(2)}, u32[]{:S(2)}) %collective-permute-start) | collective-permute-done | bytes 16416 | tf_op jit(solution)/shard_map/ppermute | solution.py:350
  2.2 0.0 copy-start.1
  2.3 3.6 %collective-permute-start.2 = (bf16[2,40,128]{2,1,0:T(8,128)(2,1)S(1)}, bf16[2,40,128]{2,1,0:T(8,128)(2,1)S(1)}, u32[]{:S(2)}, u32[]{:S(2)}) collective-permute-start(bf16[2,40,128]{2,1,0:T(8,128)(2,1)S(1)} %get-tuple-element.51), channel_id=1, source_target_pairs={{0,7},{1,3},{2,5},{3,1},{4,11},{5,2},{6,9},{7,0},{8,15},{9,6},{10,... | collective-permute-start | bytes 61448 | tf_op jit(solution)/shard_map/ppermute | solution.py:354
  5.9 0.5 %collective-permute-start.3 = (bf16[2,40,128]{2,1,0:T(8,128)(2,1)S(1)}, bf16[2,40,128]{2,1,0:T(8,128)(2,1)S(1)}, u32[]{:S(2)}, u32[]{:S(2)}) collective-permute-start(bf16[2,40,128]{2,1,0:T(8,128)(2,1)S(1)} %get-tuple-element.52), channel_id=1, source_target_pairs={{0,5},{1,3},{2,7},{3,1},{4,9},{5,0},{6,11},{7,2},{8,13},{9,4},{10,... | collective-permute-start | bytes 61448 | tf_op jit(solution)/shard_map/ppermute | solution.py:355
  6.4 0.1 collective-permute-start.1
  6.4 0.9 %collective-permute-done.2 = bf16[2,40,128]{2,1,0:T(8,128)(2,1)S(1)} collective-permute-done((bf16[2,40,128]{2,1,0:T(8,128)(2,1)S(1)}, bf16[2,40,128]{2,1,0:T(8,128)(2,1)S(1)}, u32[]{:S(2)}, u32[]{:S(2)}) %collective-permute-start.2) | collective-permute-done | bytes 20512 | tf_op jit(solution)/shard_map/ppermute | solution.py:354
  7.4 0.0 copy-done.1
  7.4 0.0 copy-start
  7.4 0.0 copy-start.2
  7.4 0.0 copy-start.3
  7.4 0.0 copy-start.4
  7.4 0.0 copy-start.5
  7.4 0.6 %bands_3.1.t3 = bf16[2,192,256]{2,1,0:T(8,128)(2,1)S(1)} custom-call(bf16[3,3,3,8,16]{4,3,2,1,0:T(8,128)(2,1)S(1)} %bitcast.16), custom_call_target="tpu_custom_call" | custom-call | tf_op jit(solution)/shard_map/bands_3/pallas_call | solution.py:402
  8.1 0.1 %copy-done = bf16[8,8,3,3,3]{1,0,4,3,2:T(8,128)(2,1)S(1)} copy-done((bf16[8,8,3,3,3]{1,0,4,3,2:T(8,128)(2,1)S(1)}, bf16[8,8,3,3,3]{1,0,4,3,2:T(8,128)(2,1)}, u32[]{:S(2)}) %copy-start) | copy-done | bytes 3480
  8.2 0.0 copy-done.2
  8.2 0.0 copy-done.3
  8.2 0.0 copy-done.4
  8.2 0.0 copy-done.5
  8.2 0.4 %bands_12.1 = (bf16[160,256]{1,0:T(8,128)(2,1)S(1)}, bf16[144,256]{1,0:T(8,128)(2,1)S(1)}, f32[8,128]{1,0:T(8,128)S(1)}, f32[8,128]{1,0:T(8,128)S(1)}, f32[16,8,128]{2,1,0:T(8,128)S(1)}) custom-call(f32[1,8]{1,0:T(1,128)S(1)} %bitcast.18, f32[1,8]{1,0:T(1,128)S(1)} %bitcast.19, f32[1,16]{1,0:T(1,128)S(1)} %bitcast.20, bf16[3,3,3,8]{3,2,1,0:T(4,128)(2,1)S(1)} %bitcast.17, ...), custom_call_target="tpu_custom_call" | custom-call | tf_op jit(solution)/shard_map/bands_12/pallas_call | solution.py:388
  8.6 0.5 %collective-permute-done.3 = bf16[2,40,128]{2,1,0:T(8,128)(2,1)S(1)} collective-permute-done((bf16[2,40,128]{2,1,0:T(8,128)(2,1)S(1)}, bf16[2,40,128]{2,1,0:T(8,128)(2,1)S(1)}, u32[]{:S(2)}, u32[]{:S(2)}) %collective-permute-start.3) | collective-permute-done | bytes 20512 | tf_op jit(solution)/shard_map/ppermute | solution.py:355
  9.1 0.1 collective-permute-start.4
  9.2 0.4 %collective-permute-done.1 = bf16[2,40,128]{2,1,0:T(8,128)(2,1)S(1)} collective-permute-done((bf16[2,40,128]{2,1,0:T(8,128)(2,1)S(1)}, bf16[2,40,128]{2,1,0:T(8,128)(2,1)S(1)}, u32[]{:S(2)}, u32[]{:S(2)}) %collective-permute-start.1) | collective-permute-done | bytes 20512 | tf_op jit(solution)/shard_map/ppermute | solution.py:356
  9.6 0.6 %early.1 = (bf16[5,144,128]{2,1,0:T(8,128)(2,1)S(1)}, bf16[2,160,128]{2,1,0:T(8,128)(2,1)S(1)}) custom-call(bf16[4,40,128]{2,1,0:T(8,128)(2,1)S(1)} %maximum_select_fusion.own, bf16[3,40,128]{2,1,0:T(8,128)(2,1)S(1)} %fusion.9.got, bf16[160,256]{1,0:T(8,128)(2,1)S(1)} %get-tuple-element.41.t1, bf16[144,256]{1,0:T(8,128)(2,1)S(1)} %get-tuple-element.42.t2, ...), custom_call_target="tpu_custom_call" | custom-call | tf_op jit(solution)/shard_map/early/pallas_call | solution.py:417
  10.2 0.2 %collective-permute-done.4.other = bf16[3,40,128]{2,1,0:T(8,128)(2,1)S(1)} collective-permute-done((bf16[3,40,128]{2,1,0:T(8,128)(2,1)S(1)}, bf16[3,40,128]{2,1,0:T(8,128)(2,1)S(1)}, u32[]{:S(2)}, u32[]{:S(2)}) %collective-permute-start.4) | collective-permute-done | bytes 30752 | tf_op jit(solution)/shard_map/ppermute | solution.py:416
  10.4 1.6 %late.1 = bf16[16,2,8,64]{3,2,1,0:T(8,128)(2,1)} custom-call(bf16[4,40,128]{2,1,0:T(8,128)(2,1)S(1)} %maximum_select_fusion.own, bf16[3,40,128]{2,1,0:T(8,128)(2,1)S(1)} %collective-permute-done.4.other, bf16[2,160,128]{2,1,0:T(8,128)(2,1)S(1)} %get-tuple-element.47.middle, bf16[5,144,128]{2,1,0:T(8,128)(2,1)S(1)} %get-tuple-element.48.done, ...), custom_call_target="tpu_custom_call" | custom-call | tf_op jit(solution)/shard_map/late/pallas_call | solution.py:429
  (7 shorter events, 0.1 us)
Async XLA Ops:
  0.9 1.3 %collective-permute-start = (bf16[1,64,128]{2,1,0:T(8,128)(2,1)S(1)}, bf16[1,64,128]{2,1,0:T(8,128)(2,1)S(1)}, u32[]{:S(2)}, u32[]{:S(2)}) collective-permute-start(bf16[1,64,128]{2,1,0:T(8,128)(2,1)S(1)} %fusion), channel_id=1, source_target_pairs={{0,1},{1,0},{2,3},{3,2},{4,5},{5,4},{6,7},{7,6},{8,9},{9,8},{10,11... | collective-permute-start | bytes 49160 | tf_op jit(solution)/shard_map/ppermute | solution.py:350
  2.2 5.2 %copy-start.1 = (bf16[16,8,3,3,3]{0,1,4,3,2:T(8,128)(2,1)S(1)}, bf16[16,8,3,3,3]{0,1,4,3,2:T(8,128)(2,1)}, u32[]{:S(2)}) copy-start(bf16[16,8,3,3,3]{0,1,4,3,2:T(8,128)(2,1)} %param.12) | copy-start | bytes 20740
  2.3 5.1 %collective-permute-start.2 = (bf16[2,40,128]{2,1,0:T(8,128)(2,1)S(1)}, bf16[2,40,128]{2,1,0:T(8,128)(2,1)S(1)}, u32[]{:S(2)}, u32[]{:S(2)}) collective-permute-start(bf16[2,40,128]{2,1,0:T(8,128)(2,1)S(1)} %get-tuple-element.51), channel_id=1, source_target_pairs={{0,7},{1,3},{2,5},{3,1},{4,11},{5,2},{6,9},{7,0},{8,15},{9,6},{10,... | collective-permute-start | bytes 61448 | tf_op jit(solution)/shard_map/ppermute | solution.py:354
  5.9 3.2 %collective-permute-start.3 = (bf16[2,40,128]{2,1,0:T(8,128)(2,1)S(1)}, bf16[2,40,128]{2,1,0:T(8,128)(2,1)S(1)}, u32[]{:S(2)}, u32[]{:S(2)}) collective-permute-start(bf16[2,40,128]{2,1,0:T(8,128)(2,1)S(1)} %get-tuple-element.52), channel_id=1, source_target_pairs={{0,5},{1,3},{2,7},{3,1},{4,9},{5,0},{6,11},{7,2},{8,13},{9,4},{10,... | collective-permute-start | bytes 61448 | tf_op jit(solution)/shard_map/ppermute | solution.py:355
  6.4 3.2 %collective-permute-start.1 = (bf16[2,40,128]{2,1,0:T(8,128)(2,1)S(1)}, bf16[2,40,128]{2,1,0:T(8,128)(2,1)S(1)}, u32[]{:S(2)}, u32[]{:S(2)}) collective-permute-start(bf16[2,40,128]{2,1,0:T(8,128)(2,1)S(1)} %get-tuple-element.51), channel_id=1, source_target_pairs={{0,3},{1,2},{2,1},{3,0},{4,7},{5,6},{6,5},{7,4},{8,11},{9,10},{10,... | collective-permute-start | bytes 61448 | tf_op jit(solution)/shard_map/ppermute | solution.py:356
  7.4 0.8 %copy-start = (bf16[8,8,3,3,3]{1,0,4,3,2:T(8,128)(2,1)S(1)}, bf16[8,8,3,3,3]{1,0,4,3,2:T(8,128)(2,1)}, u32[]{:S(2)}) copy-start(bf16[8,8,3,3,3]{1,0,4,3,2:T(8,128)(2,1)} %param.10) | copy-start | bytes 10372
  7.4 0.8 %copy-start.2 = (bf16[8,1,3,3,3]{0,4,3,2,1:T(4,128)(2,1)S(1)}, bf16[8,1,3,3,3]{0,4,3,2,1:T(4,128)(2,1)}, u32[]{:S(2)}) copy-start(bf16[8,1,3,3,3]{0,4,3,2,1:T(4,128)(2,1)} %param.8) | copy-start | bytes 1300
  7.4 0.8 %copy-start.3 = (f32[8]{0:T(128)S(1)}, f32[8]{0:T(128)}, u32[]{:S(2)}) copy-start(f32[8]{0:T(128)} %param.9) | copy-start | bytes 100
  7.4 0.8 %copy-start.4 = (f32[8]{0:T(128)S(1)}, f32[8]{0:T(128)}, u32[]{:S(2)}) copy-start(f32[8]{0:T(128)} %param.11) | copy-start | bytes 100
  7.4 0.8 %copy-start.5 = (f32[16]{0:T(128)S(1)}, f32[16]{0:T(128)}, u32[]{:S(2)}) copy-start(f32[16]{0:T(128)} %param.13) | copy-start | bytes 196
  9.1 1.3 %collective-permute-start.4 = (bf16[3,40,128]{2,1,0:T(8,128)(2,1)S(1)}, bf16[3,40,128]{2,1,0:T(8,128)(2,1)S(1)}, u32[]{:S(2)}, u32[]{:S(2)}) collective-permute-start(bf16[3,40,128]{2,1,0:T(8,128)(2,1)S(1)} %fusion.9.got), channel_id=1, source_target_pairs={{0,1},{1,0},{2,3},{3,2},{4,5},{5,4},{6,7},{7,6},{8,9},{9,8},{10,11... | collective-permute-start | bytes 92168 | tf_op jit(solution)/shard_map/ppermute | solution.py:416

commit v6 on v5

--- a/solution.py
+++ b/solution.py
@@ -66,9 +66,10 @@
     return pltpu.roll(x, by, 1) if by else x
 
 
-def bands_12_kernel(plan, bias1, bias2, bias3, w1, w2, t1, t2, b1, b2, b3):
+def bands_kernel(plan, bias1, bias2, bias3, w1, w2, w3, t1, t2, b1, b2, b3, t3):
     c1, c2 = plan.c1, plan.c2
     slots = plan.slots
+    bands_3(plan, w3, t3)
     b1[...] = column_of(bias1, c1)
     b2[...] = column_of(bias2, c2)
     column = column_of(bias3, plan.c3)
@@ -103,16 +104,22 @@
             t2[at : at + 2 * c2, :] = jnp.concatenate(rows, axis=0).astype(BF)
 
 
-def bands_3_kernel(plan, w3, t3):
+def parts_of(count, *sizes):
+    at, digits = lax.broadcasted_iota(jnp.int32, (count, 1), 0), []
+    for size in reversed(sizes):
+        digits.append(lax.rem(at, size))
+        at = lax.div(at, size)
+    return at, *reversed(digits)
+
+
+def bands_3(plan, w3, t3):
     c2, c3, rows = plan.c2, plan.c3, plan.block3
     n3 = plan.out3
-    at = lax.broadcasted_iota(jnp.int32, (2 * n3, n3), 0)
+    odd, pair, which, y = parts_of(2 * n3, c3 // 2, 2, rows)
     source = lax.broadcasted_iota(jnp.int32, (2 * n3, n3), 1)
-    odd, pair, which, y = at // n3, (at % n3) // (2 * rows), (at // rows) % 2, at % rows
-    turn = ones_where(source == y * c3 + 2 * pair + (which + odd) % 2)
-    row = lax.broadcasted_iota(jnp.int32, (9 * c2, plan.k3), 0)
+    turn = ones_where(source == y * c3 + 2 * pair + lax.rem(which + odd, 2))
+    a, b, i = parts_of(9 * c2, 3, c2)
     lane = lax.broadcasted_iota(jnp.int32, (9 * c2, plan.k3), 1)
-    a, b, i = row // (3 * c2), (row // c2) % 3, row % c2
     spread = ones_where(lane == a * plan.in3 + b * c2 + i)
     for c in range(3):
         taken = w3[:, :, c].astype(F32).reshape(9 * c2, c3).astype(BF)
@@ -351,12 +358,12 @@
     pair = in_order(tile % 2 == 1, plane, taken)
     chip = tile // 2
     mine, theirs = chip_rows(plan, pair, chip), chip_rows(plan, pair, 1 - chip)
+    ahead = lax.ppermute(mine, axes, freq_pairs(groups, tiles, 1))
     aside = lax.ppermute(theirs, axes, freq_pairs(groups, tiles, 3))
-    ahead = lax.ppermute(mine, axes, freq_pairs(groups, tiles, 1))
     across = lax.ppermute(theirs, "tile", [(t, t ^ 3) for t in range(tiles)])
-    aside, *weights = lax.optimization_barrier((aside, *weights))
+    ahead, *weights = lax.optimization_barrier((ahead, *weights))
     bands = make_bands(weights)
-    ahead, *bands = lax.optimization_barrier((ahead, *bands))
+    aside, *bands = lax.optimization_barrier((aside, *bands))
     own = in_order(chip == 1, mine, across)
     return own, some_planes(in_order(chip == 1, ahead, aside), tile), bands
 
@@ -384,30 +391,21 @@
     params = pltpu.CompilerParams(vmem_limit_bytes=32 * 2**20)
 
     def make_bands(weights):
-        bias_one, bias_two, bias_three, w1, w2, w3 = weights
-        bands_12 = pl.pallas_call(
-            functools.partial(bands_12_kernel, plan),
-            name="bands_12",
+        return pl.pallas_call(
+            functools.partial(bands_kernel, plan),
+            name="bands",
             out_shape=[
                 jax.ShapeDtypeStruct((plan.n1, plan.k1), BF),
                 jax.ShapeDtypeStruct((3 * plan.out2, plan.k2), BF),
                 jax.ShapeDtypeStruct((c1, 128), F32),
                 jax.ShapeDtypeStruct((c2, 128), F32),
                 jax.ShapeDtypeStruct((c3, plan.r3, 128), F32),
+                jax.ShapeDtypeStruct((2, 3 * plan.out3, plan.k3), BF),
             ],
-            in_specs=[VM] * 5,
-            out_specs=[VM] * 5,
+            in_specs=[VM] * 6,
+            out_specs=[VM] * 6,
             compiler_params=params,
-        )(bias_one, bias_two, bias_three, w1, w2)
-        bands_3 = pl.pallas_call(
-            functools.partial(bands_3_kernel, plan),
-            name="bands_3",
-            out_shape=jax.ShapeDtypeStruct((2, 3 * plan.out3, plan.k3), BF),
-            in_specs=[VM],
-            out_specs=VM,
-            compiler_params=params,
-        )(w3)
-        return (*bands_12, bands_3)
+        )(*weights)
 
     own, got, weights = exchanged(
         plan, even_odd(sky_cube), groups, tiles, (bias_one[None], bias_two[None], bias_three[None], w1, w2, w3), make_bands

time: 12.2 us -> 12.1 us (level)
  local copies, waits for them, and re-layouts: 0.2 us -> 0.71 us
  waiting for transfers between devices: 2.86 us -> 2.49 us
  Pallas kernels: 3.18 us -> 3 us
    ppermute x1, starting transfers between devices: 3.62 us -> 1.44 us  [exchanged(): aside = lax.ppermute(theirs, axes, freq_pairs(groups, tiles, 3))]
    ppermute x1, starting transfers between devices: 0.49 us -> 2.67 us  [exchanged(): ahead = lax.ppermute(mine, axes, freq_pairs(groups, tiles, 1))]
    ppermute x1, waiting for transfers between devices: 0.52 us -> 0.01 us  [exchanged(): ahead = lax.ppermute(mine, axes, freq_pairs(groups, tiles, 1))]
    unnamed x12, local copies, waits for them, and re-layouts: 0.16 us -> 0.67 us
    pallas_call x2 -> x1, Pallas kernels: 1.01 us -> 0.83 us  [make_bands(): pl.pallas_call(functools.partial(bands_kernel, plan), name='bands', out_s...]
    ppermute x1, waiting for transfers between devices: 0.94 us -> 1.08 us  [exchanged(): aside = lax.ppermute(theirs, axes, freq_pairs(groups, tiles, 3))]
  transfers between devices with their start and end apart: 5 -> 5, of which waited for: 5 -> 4; matrix products, arithmetic and copies ran while one was open for 0% -> 0% of each run, Pallas kernels for 13% -> 12%
where the time goes in v6:
time: 12.1 us; the launch traced here: 11.9 us
  starting transfers between devices  4.7 us (39%)
  Pallas kernels  3 us (25%)
  waiting for transfers between devices  2.49 us (21%)
  matrix products  0.9 us (7%)
  local copies, waits for them, and re-layouts  0.71 us (6%)
    ppermute x1, starting transfers between devices, exchanged(): ahead = lax.ppermute(mine, axes, freq_pairs(groups, tiles, 1))  2.67 us
    pallas_call x1, Pallas kernels, body(): pl.pallas_call(functools.partial(late_kernel, plan), name='late', out_sha...  1.56 us
    ppermute x1, starting transfers between devices, exchanged(): aside = lax.ppermute(theirs, axes, freq_pairs(groups, tiles, 3))  1.44 us
    ppermute x1, waiting for transfers between devices, exchanged(): aside = lax.ppermute(theirs, axes, freq_pairs(groups, tiles, 3))  1.08 us
    dot_general x1, matrix products, even_odd(): jnp.einsum('pyx,xw->pyw', cube.astype(BF), order, preferred_element_type=...  0.9 us
    ppermute x1, waiting for transfers between devices, exchanged(): taken = lax.ppermute(plane, 'tile', [(t, t ^ 1) for t in range(tiles)])  0.84 us
    pallas_call x1, Pallas kernels, make_bands(): pl.pallas_call(functools.partial(bands_kernel, plan), name='bands', out_s...  0.83 us
    unnamed x12, local copies, waits for them, and re-layouts  0.67 us
  transfers between devices with their start and end apart: 5, of which 4 were waited for; matrix products, arithmetic and copies ran while one was open for 0% of the time, Pallas kernels for 12%

profile of v6, /device:TPU:0, one launch (start us, length us, event | category | flops | bytes accessed | tf_op | source)
XLA Modules:
  0.0 11.9 jit_solution(806052709371708068)
XLA Ops:
  0.0 0.9 %fusion = bf16[1,64,128]{2,1,0:T(8,128)(2,1)S(1)} fusion(s32[128]{0:T(128)S(1)} %get-tuple-element.57, s32[128]{0:T(128)S(1)} %get-tuple-element.59, s32[128]{0:T(128)S(1)} %get-tuple-element.58, s32[128]{0:T(128)S(1)} %get-tuple-element.60, pred[128]{0:T(512)(128)(4,1)S(1)} %get-tuple-element.55, pred[128]{0:T(512)(128)(4,1)S(1)} %get-tuple-element.56, ...), kind=kOutput, calls=%fused_computation.1 | convolution fusion | flops 2195456 | bytes 51456 | tf_op jit(solution)/shard_map/pyx,xw->pyw/dot_general | solution.py:376
  0.9 0.5 %collective-permute-start = (bf16[1,64,128]{2,1,0:T(8,128)(2,1)S(1)}, bf16[1,64,128]{2,1,0:T(8,128)(2,1)S(1)}, u32[]{:S(2)}, u32[]{:S(2)}) collective-permute-start(bf16[1,64,128]{2,1,0:T(8,128)(2,1)S(1)} %fusion), channel_id=1, source_target_pairs={{0,1},{1,0},{2,3},{3,2},{4,5},{5,4},{6,7},{7,6},{8,9},{9,8},{10,11... | collective-permute-start | bytes 49160 | tf_op jit(solution)/shard_map/ppermute | solution.py:357
  1.4 0.8 %collective-permute-done = bf16[1,64,128]{2,1,0:T(8,128)(2,1)S(1)} collective-permute-done((bf16[1,64,128]{2,1,0:T(8,128)(2,1)S(1)}, bf16[1,64,128]{2,1,0:T(8,128)(2,1)S(1)}, u32[]{:S(2)}, u32[]{:S(2)}) %collective-permute-start) | collective-permute-done | bytes 16416 | tf_op jit(solution)/shard_map/ppermute | solution.py:357
  2.2 0.0 copy-start.1
  2.2 0.0 copy-start
  2.3 0.0 copy-start.2
  2.3 2.7 %collective-permute-start.3 = (bf16[2,40,128]{2,1,0:T(8,128)(2,1)S(1)}, bf16[2,40,128]{2,1,0:T(8,128)(2,1)S(1)}, u32[]{:S(2)}, u32[]{:S(2)}) collective-permute-start(bf16[2,40,128]{2,1,0:T(8,128)(2,1)S(1)} %get-tuple-element.54), channel_id=1, source_target_pairs={{0,5},{1,3},{2,7},{3,1},{4,9},{5,0},{6,11},{7,2},{8,13},{9,4},{10,... | collective-permute-start | bytes 61448 | tf_op jit(solution)/shard_map/ppermute | solution.py:361
  5.0 1.4 %collective-permute-start.2 = (bf16[2,40,128]{2,1,0:T(8,128)(2,1)S(1)}, bf16[2,40,128]{2,1,0:T(8,128)(2,1)S(1)}, u32[]{:S(2)}, u32[]{:S(2)}) collective-permute-start(bf16[2,40,128]{2,1,0:T(8,128)(2,1)S(1)} %get-tuple-element.53), channel_id=1, source_target_pairs={{0,7},{1,3},{2,5},{3,1},{4,11},{5,2},{6,9},{7,0},{8,15},{9,6},{10,... | collective-permute-start | bytes 61448 | tf_op jit(solution)/shard_map/ppermute | solution.py:362
  6.4 0.1 collective-permute-start.1
  6.5 0.0 collective-permute-done.3
  6.5 0.0 copy-start.3
  6.5 0.0 copy-start.4
  6.5 0.0 copy-start.5
  6.5 0.0 copy-done.1
  6.5 0.0 copy-done
  6.5 0.0 copy-done.2
  6.5 0.6 %copy-done.3 = f32[8]{0:T(128)S(1)} copy-done((f32[8]{0:T(128)S(1)}, f32[8]{0:T(128)}, u32[]{:S(2)}) %copy-start.3) | copy-done | bytes 56
  7.1 0.0 copy-done.4
  7.1 0.0 copy-done.5
  7.2 0.8 %bands.1 = (bf16[160,256]{1,0:T(8,128)(2,1)S(1)}, bf16[144,256]{1,0:T(8,128)(2,1)S(1)}, f32[8,128]{1,0:T(8,128)S(1)}, f32[8,128]{1,0:T(8,128)S(1)}, f32[16,8,128...) custom-call(f32[1,8]{1,0:T(1,128)S(1)} %bitcast.18, f32[1,8]{1,0:T(1,128)S(1)} %bitcast.19, f32[1,16]{1,0:T(1,128)S(1)} %bitcast.20, ...), custom_call_target="tpu_custom_call" | custom-call | tf_op jit(solution)/shard_map/bands/pallas_call | solution.py:394
  8.0 1.1 %collective-permute-done.2 = bf16[2,40,128]{2,1,0:T(8,128)(2,1)S(1)} collective-permute-done((bf16[2,40,128]{2,1,0:T(8,128)(2,1)S(1)}, bf16[2,40,128]{2,1,0:T(8,128)(2,1)S(1)}, u32[]{:S(2)}, u32[]{:S(2)}) %collective-permute-start.2) | collective-permute-done | bytes 20512 | tf_op jit(solution)/shard_map/ppermute | solution.py:362
  9.1 0.1 collective-permute-start.4
  9.2 0.4 %collective-permute-done.1 = bf16[2,40,128]{2,1,0:T(8,128)(2,1)S(1)} collective-permute-done((bf16[2,40,128]{2,1,0:T(8,128)(2,1)S(1)}, bf16[2,40,128]{2,1,0:T(8,128)(2,1)S(1)}, u32[]{:S(2)}, u32[]{:S(2)}) %collective-permute-start.1) | collective-permute-done | bytes 20512 | tf_op jit(solution)/shard_map/ppermute | solution.py:363
  9.6 0.6 %early.1 = (bf16[5,144,128]{2,1,0:T(8,128)(2,1)S(1)}, bf16[2,160,128]{2,1,0:T(8,128)(2,1)S(1)}) custom-call(bf16[4,40,128]{2,1,0:T(8,128)(2,1)S(1)} %maximum_select_fusion.own, bf16[3,40,128]{2,1,0:T(8,128)(2,1)S(1)} %fusion.9.got, bf16[160,256]{1,0:T(8,128)(2,1)S(1)} %get-tuple-element.43.t1, bf16[144,256]{1,0:T(8,128)(2,1)S(1)} %get-tuple-element.44.t2, ...), custom_call_target="tpu_custom_call" | custom-call | tf_op jit(solution)/shard_map/early/pallas_call | solution.py:415
  10.2 0.1 %collective-permute-done.4.other = bf16[3,40,128]{2,1,0:T(8,128)(2,1)S(1)} collective-permute-done((bf16[3,40,128]{2,1,0:T(8,128)(2,1)S(1)}, bf16[3,40,128]{2,1,0:T(8,128)(2,1)S(1)}, u32[]{:S(2)}, u32[]{:S(2)}) %collective-permute-start.4) | collective-permute-done | bytes 30752 | tf_op jit(solution)/shard_map/ppermute | solution.py:414
  10.4 1.6 %late.1 = bf16[16,2,8,64]{3,2,1,0:T(8,128)(2,1)} custom-call(bf16[4,40,128]{2,1,0:T(8,128)(2,1)S(1)} %maximum_select_fusion.own, bf16[3,40,128]{2,1,0:T(8,128)(2,1)S(1)} %collective-permute-done.4.other, bf16[2,160,128]{2,1,0:T(8,128)(2,1)S(1)} %get-tuple-element.49.middle, bf16[5,144,128]{2,1,0:T(8,128)(2,1)S(1)} %get-tuple-element.50.done, ...), custom_call_target="tpu_custom_call" | custom-call | tf_op jit(solution)/shard_map/late/pallas_call | solution.py:427
  (7 shorter events, 0.1 us)
Async XLA Ops:
  0.9 1.3 %collective-permute-start = (bf16[1,64,128]{2,1,0:T(8,128)(2,1)S(1)}, bf16[1,64,128]{2,1,0:T(8,128)(2,1)S(1)}, u32[]{:S(2)}, u32[]{:S(2)}) collective-permute-start(bf16[1,64,128]{2,1,0:T(8,128)(2,1)S(1)} %fusion), channel_id=1, source_target_pairs={{0,1},{1,0},{2,3},{3,2},{4,5},{5,4},{6,7},{7,6},{8,9},{9,8},{10,11... | collective-permute-start | bytes 49160 | tf_op jit(solution)/shard_map/ppermute | solution.py:357
  2.2 4.3 %copy-start.1 = (bf16[16,8,3,3,3]{0,1,4,3,2:T(8,128)(2,1)S(1)}, bf16[16,8,3,3,3]{0,1,4,3,2:T(8,128)(2,1)}, u32[]{:S(2)}) copy-start(bf16[16,8,3,3,3]{0,1,4,3,2:T(8,128)(2,1)} %param.12) | copy-start | bytes 20740
  2.2 4.3 %copy-start = (bf16[8,8,3,3,3]{1,0,4,3,2:T(8,128)(2,1)S(1)}, bf16[8,8,3,3,3]{1,0,4,3,2:T(8,128)(2,1)}, u32[]{:S(2)}) copy-start(bf16[8,8,3,3,3]{1,0,4,3,2:T(8,128)(2,1)} %param.10) | copy-start | bytes 10372
  2.3 4.2 %copy-start.2 = (bf16[8,1,3,3,3]{0,4,3,2,1:T(4,128)(2,1)S(1)}, bf16[8,1,3,3,3]{0,4,3,2,1:T(4,128)(2,1)}, u32[]{:S(2)}) copy-start(bf16[8,1,3,3,3]{0,4,3,2,1:T(4,128)(2,1)} %param.8) | copy-start | bytes 1300
  2.3 4.2 %collective-permute-start.3 = (bf16[2,40,128]{2,1,0:T(8,128)(2,1)S(1)}, bf16[2,40,128]{2,1,0:T(8,128)(2,1)S(1)}, u32[]{:S(2)}, u32[]{:S(2)}) collective-permute-start(bf16[2,40,128]{2,1,0:T(8,128)(2,1)S(1)} %get-tuple-element.54), channel_id=1, source_target_pairs={{0,5},{1,3},{2,7},{3,1},{4,9},{5,0},{6,11},{7,2},{8,13},{9,4},{10,... | collective-permute-start | bytes 61448 | tf_op jit(solution)/shard_map/ppermute | solution.py:361
  5.0 4.1 %collective-permute-start.2 = (bf16[2,40,128]{2,1,0:T(8,128)(2,1)S(1)}, bf16[2,40,128]{2,1,0:T(8,128)(2,1)S(1)}, u32[]{:S(2)}, u32[]{:S(2)}) collective-permute-start(bf16[2,40,128]{2,1,0:T(8,128)(2,1)S(1)} %get-tuple-element.53), channel_id=1, source_target_pairs={{0,7},{1,3},{2,5},{3,1},{4,11},{5,2},{6,9},{7,0},{8,15},{9,6},{10,... | collective-permute-start | bytes 61448 | tf_op jit(solution)/shard_map/ppermute | solution.py:362
  6.4 3.2 %collective-permute-start.1 = (bf16[2,40,128]{2,1,0:T(8,128)(2,1)S(1)}, bf16[2,40,128]{2,1,0:T(8,128)(2,1)S(1)}, u32[]{:S(2)}, u32[]{:S(2)}) collective-permute-start(bf16[2,40,128]{2,1,0:T(8,128)(2,1)S(1)} %get-tuple-element.53), channel_id=1, source_target_pairs={{0,3},{1,2},{2,1},{3,0},{4,7},{5,6},{6,5},{7,4},{8,11},{9,10},{10,... | collective-permute-start | bytes 61448 | tf_op jit(solution)/shard_map/ppermute | solution.py:363
  6.5 0.7 %copy-start.3 = (f32[8]{0:T(128)S(1)}, f32[8]{0:T(128)}, u32[]{:S(2)}) copy-start(f32[8]{0:T(128)} %param.9) | copy-start | bytes 100
  6.5 0.7 %copy-start.4 = (f32[8]{0:T(128)S(1)}, f32[8]{0:T(128)}, u32[]{:S(2)}) copy-start(f32[8]{0:T(128)} %param.11) | copy-start | bytes 100
  6.5 0.7 %copy-start.5 = (f32[16]{0:T(128)S(1)}, f32[16]{0:T(128)}, u32[]{:S(2)}) copy-start(f32[16]{0:T(128)} %param.13) | copy-start | bytes 196
  9.1 1.3 %collective-permute-start.4 = (bf16[3,40,128]{2,1,0:T(8,128)(2,1)S(1)}, bf16[3,40,128]{2,1,0:T(8,128)(2,1)S(1)}, u32[]{:S(2)}, u32[]{:S(2)}) collective-permute-start(bf16[3,40,128]{2,1,0:T(8,128)(2,1)S(1)} %fusion.9.got), channel_id=1, source_target_pairs={{0,1},{1,0},{2,3},{3,2},{4,5},{5,4},{6,7},{7,6},{8,9},{9,8},{10,11... | collective-permute-start | bytes 92168 | tf_op jit(solution)/shard_map/ppermute | solution.py:414

commit v7 on v6

--- a/solution.py
+++ b/solution.py
@@ -237,30 +237,30 @@
 
 def layer_three(plan, layer_two, t3, b3, out):
     n3, rows = plan.out3, plan.block3
-    for chunk in in_twos(range(plan.depth // 2)):
+    for f in range(plan.depth // 2):
+        planes = [layer_two(2 * f + a) for a in range(3)]
         for y in range(0, plan.r3, 2 * rows):
-            halves = []
-            for odd in range(2):
-                x = []
-                for f in chunk:
-                    planes = [layer_two(2 * f + a) for a in range(3)]
-                    x.append(blocks_of(planes, plan.k3, 2 * rows * plan.c2, plan.in3, y // rows + odd))
-                x = jnp.concatenate(x, axis=1)
-                halves.append(jnp.dot(t3[odd], x, preferred_element_type=F32))
-            for i, f in enumerate(chunk):
-                first, second = (
-                    sum_of_even_taps(
-                        *(half[c * n3 : (c + 1) * n3, i * 128 : (i + 1) * 128] for c in range(3))
-                    ).reshape(plan.c3 // 2, 2 * rows, 128)
-                    for half in halves
+            first, second = (
+                jnp.dot(
+                    t3[odd],
+                    blocks_of(planes, plan.k3, 2 * rows * plan.c2, plan.in3, y // rows + odd),
+                    preferred_element_type=F32,
                 )
-                sub = lax.broadcasted_iota(jnp.int32, first.shape, 1)
-                one = jnp.where(sub < rows, first, second)
-                other = jnp.where(sub < rows, second, first)
-                other = jnp.concatenate([other[:, rows:], other[:, :rows]], axis=1)
-                v = jnp.stack([one, other], axis=1).reshape(plan.c3, 2 * rows, 128)
-                v = leaky_relu(v + b3[:, y : y + 2 * rows])
-                out[:, f, y : y + 2 * rows] = v[:, :, :64].astype(BF)
+                for odd in range(2)
+            )
+            first, second = (
+                sum_of_even_taps(*(half[c * n3 : (c + 1) * n3] for c in range(3))).reshape(
+                    plan.c3 // 2, 2 * rows, 128
+                )
+                for half in (first, second)
+            )
+            sub = lax.broadcasted_iota(jnp.int32, first.shape, 1)
+            one = jnp.where(sub < rows, first, second)
+            other = jnp.where(sub < rows, second, first)
+            other = jnp.concatenate([other[:, rows:], other[:, :rows]], axis=1)
+            v = jnp.stack([one, other], axis=1).reshape(plan.c3, 2 * rows, 128)
+            v = leaky_relu(v + b3[:, y : y + 2 * rows])
+            out[:, f, y : y + 2 * rows] = v[:, :, :64].astype(BF)
 
 
 def lower_half(plan, place, own, halo, t1, t2, b1, b2, middle=None):
@@ -351,11 +351,11 @@
 def exchanged(plan, plane, groups, tiles, weights, make_bands):
     axes, tile = ("freq", "tile"), lax.axis_index("tile")
     if tiles != 4:
-        own = gathered(plan, plane, tiles)
+        own = gathered(plan, even_odd(plane), tiles)
         message = some_planes(own, tile + 1)
         return own, lax.ppermute(message, axes, freq_pairs(groups, tiles, 1)), make_bands(weights)
     taken = lax.ppermute(plane, "tile", [(t, t ^ 1) for t in range(tiles)])
-    pair = in_order(tile % 2 == 1, plane, taken)
+    pair = even_odd(in_order(tile % 2 == 1, plane, taken))
     chip = tile // 2
     mine, theirs = chip_rows(plan, pair, chip), chip_rows(plan, pair, 1 - chip)
     ahead = lax.ppermute(mine, axes, freq_pairs(groups, tiles, 1))
@@ -368,12 +368,12 @@
     return own, some_planes(in_order(chip == 1, ahead, aside), tile), bands
 
 
-def even_odd(cube):
-    width = cube.shape[2]
+def even_odd(planes):
+    width = planes.shape[2]
     row = lax.broadcasted_iota(jnp.int32, (width, width), 0)
     col = lax.broadcasted_iota(jnp.int32, (width, width), 1)
     order = (row == 2 * (col % (width // 2)) + col // (width // 2)).astype(BF)
-    return jnp.einsum("pyx,xw->pyw", cube.astype(BF), order, preferred_element_type=F32).astype(BF)
+    return jnp.einsum("pyx,xw->pyw", planes, order, preferred_element_type=F32).astype(BF)
 
 
 def body(sky_cube, kernel_one, bias_one, kernel_two, bias_two, kernel_three, bias_three):
@@ -408,7 +408,7 @@
         )(*weights)
 
     own, got, weights = exchanged(
-        plan, even_odd(sky_cube), groups, tiles, (bias_one[None], bias_two[None], bias_three[None], w1, w2, w3), make_bands
+        plan, sky_cube.astype(BF), groups, tiles, (bias_one[None], bias_two[None], bias_three[None], w1, w2, w3), make_bands
     )
     t1, t2, b1, b2, b3, t3 = weights
     other = lax.ppermute(got, "tile", [(t, t ^ 1) for t in range(tiles)])

time: 12.1 us -> 12.1 us (level)
  matrix products: 0.9 us -> 0.14 us
  other arithmetic: 0.06 us -> 0.81 us
    convert_element_type x0 -> x1, other arithmetic: none -> 0.76 us  [body(): sky_cube.astype(BF)]
    dot_general x1, matrix products: 0.9 us -> 0.14 us  [even_odd(): jnp.einsum('pyx,xw->pyw', planes, order, preferred_element_type=F32)]
where the time goes in v7:
time: 12.1 us; the launch traced here: 11.9 us
  starting transfers between devices  4.68 us (39%)
  Pallas kernels  3.02 us (25%)
  waiting for transfers between devices  2.44 us (20%)
  other arithmetic  0.81 us (7%)
  local copies, waits for them, and re-layouts  0.71 us (6%)
  matrix products  0.14 us (1%)
    ppermute x1, starting transfers between devices, exchanged(): ahead = lax.ppermute(mine, axes, freq_pairs(groups, tiles, 1))  2.67 us
    pallas_call x1, Pallas kernels, body(): pl.pallas_call(functools.partial(late_kernel, plan), name='late', out_sha...  1.58 us
    ppermute x1, starting transfers between devices, exchanged(): aside = lax.ppermute(theirs, axes, freq_pairs(groups, tiles, 3))  1.44 us
    ppermute x1, waiting for transfers between devices, exchanged(): aside = lax.ppermute(theirs, axes, freq_pairs(groups, tiles, 3))  1.08 us
    pallas_call x1, Pallas kernels, make_bands(): pl.pallas_call(functools.partial(bands_kernel, plan), name='bands', out_s...  0.83 us
    ppermute x1, waiting for transfers between devices, exchanged(): taken = lax.ppermute(plane, 'tile', [(t, t ^ 1) for t in range(tiles)])  0.79 us
    convert_element_type x1, other arithmetic, body(): sky_cube.astype(BF)  0.76 us
    unnamed x12, local copies, waits for them, and re-layouts  0.66 us
  transfers between devices with their start and end apart: 5, of which 4 were waited for; matrix products, arithmetic and copies ran while one was open for 0% of the time, Pallas kernels for 12%

profile of v7, /device:TPU:0, one launch (start us, length us, event | category | flops | bytes accessed | tf_op | source)
XLA Modules:
  0.0 11.9 jit_solution(7414463078609922737)
XLA Ops:
  0.0 0.8 %convert_element_type.10 = bf16[1,64,128]{2,1,0:T(8,128)(2,1)S(1)} convert(f32[1,64,128]{2,1,0:T(8,128)} %param.7) | non-fusion elementwise | flops 8192 | bytes 49152 | tf_op jit(solution)/shard_map/convert_element_type | solution.py:411
  0.8 0.5 %collective-permute-start = (bf16[1,64,128]{2,1,0:T(8,128)(2,1)S(1)}, bf16[1,64,128]{2,1,0:T(8,128)(2,1)S(1)}, u32[]{:S(2)}, u32[]{:S(2)}) collective-permute-start(bf16[1,64,128]{2,1,0:T(8,128)(2,1)S(1)} %convert_element_type.10), channel_id=1, source_target_pairs={{0,1},{1,0},{2,3},{3,2},{4,5},{5,4},{6,7},{7,6},{8,9},{9,8},{10,11... | collective-permute-start | bytes 49160 | tf_op jit(solution)/shard_map/ppermute | solution.py:357
  1.3 0.8 %collective-permute-done = bf16[1,64,128]{2,1,0:T(8,128)(2,1)S(1)} collective-permute-done((bf16[1,64,128]{2,1,0:T(8,128)(2,1)S(1)}, bf16[1,64,128]{2,1,0:T(8,128)(2,1)S(1)}, u32[]{:S(2)}, u32[]{:S(2)}) %collective-permute-start) | collective-permute-done | bytes 16416 | tf_op jit(solution)/shard_map/ppermute | solution.py:357
  2.1 0.0 copy-start.1
  2.1 0.1 %convolution_convert_fusion = bf16[2,64,128]{2,1,0:T(8,128)(2,1)S(1)} fusion(bf16[1,64,128]{2,1,0:T(8,128)(2,1)S(1)} %convert_element_type.10, bf16[1,64,128]{2,1,0:T(8,128)(2,1)S(1)} %collective-permute-done, s32[128]{0:T(128)S(1)} %get-tuple-element.57, s32[128]{0:T(128)S(1)} %get-tuple-element.59, s32[128]{0:T(128)S(1)} %get-tuple-element.58, ...), kind=kOutput, calls=%fused_computation | convolution fusion | flops 4341760 | bytes 67841 | tf_op jit(solution)/shard_map/pyx,xw->pyw/dot_general | solution.py:376
  2.2 0.0 copy-start
  2.3 0.0 copy-start.2
  2.3 2.7 %collective-permute-start.3 = (bf16[2,40,128]{2,1,0:T(8,128)(2,1)S(1)}, bf16[2,40,128]{2,1,0:T(8,128)(2,1)S(1)}, u32[]{:S(2)}, u32[]{:S(2)}) collective-permute-start(bf16[2,40,128]{2,1,0:T(8,128)(2,1)S(1)} %get-tuple-element.54), channel_id=1, source_target_pairs={{0,5},{1,3},{2,7},{3,1},{4,9},{5,0},{6,11},{7,2},{8,13},{9,4},{10,... | collective-permute-start | bytes 61448 | tf_op jit(solution)/shard_map/ppermute | solution.py:361
  4.9 1.4 %collective-permute-start.2 = (bf16[2,40,128]{2,1,0:T(8,128)(2,1)S(1)}, bf16[2,40,128]{2,1,0:T(8,128)(2,1)S(1)}, u32[]{:S(2)}, u32[]{:S(2)}) collective-permute-start(bf16[2,40,128]{2,1,0:T(8,128)(2,1)S(1)} %get-tuple-element.53), channel_id=1, source_target_pairs={{0,7},{1,3},{2,5},{3,1},{4,11},{5,2},{6,9},{7,0},{8,15},{9,6},{10,... | collective-permute-start | bytes 61448 | tf_op jit(solution)/shard_map/ppermute | solution.py:362
  6.4 0.1 collective-permute-start.1
  6.4 0.0 collective-permute-done.3
  6.4 0.0 copy-start.3
  6.4 0.0 copy-start.4
  6.4 0.0 copy-start.5
  6.4 0.0 copy-done.1
  6.5 0.0 copy-done
  6.5 0.0 copy-done.2
  6.5 0.6 %copy-done.3 = f32[8]{0:T(128)S(1)} copy-done((f32[8]{0:T(128)S(1)}, f32[8]{0:T(128)}, u32[]{:S(2)}) %copy-start.3) | copy-done | bytes 56
  7.1 0.0 copy-done.4
  7.1 0.0 copy-done.5
  7.1 0.8 %bands.1 = (bf16[160,256]{1,0:T(8,128)(2,1)S(1)}, bf16[144,256]{1,0:T(8,128)(2,1)S(1)}, f32[8,128]{1,0:T(8,128)S(1)}, f32[8,128]{1,0:T(8,128)S(1)}, f32[16,8,128...) custom-call(f32[1,8]{1,0:T(1,128)S(1)} %bitcast.14, f32[1,8]{1,0:T(1,128)S(1)} %bitcast.15, f32[1,16]{1,0:T(1,128)S(1)} %bitcast.16, ...), custom_call_target="tpu_custom_call" | custom-call | tf_op jit(solution)/shard_map/bands/pallas_call | solution.py:394
  8.0 1.1 %collective-permute-done.2 = bf16[2,40,128]{2,1,0:T(8,128)(2,1)S(1)} collective-permute-done((bf16[2,40,128]{2,1,0:T(8,128)(2,1)S(1)}, bf16[2,40,128]{2,1,0:T(8,128)(2,1)S(1)}, u32[]{:S(2)}, u32[]{:S(2)}) %collective-permute-start.2) | collective-permute-done | bytes 20512 | tf_op jit(solution)/shard_map/ppermute | solution.py:362
  9.1 0.1 collective-permute-start.4
  9.2 0.4 %collective-permute-done.1 = bf16[2,40,128]{2,1,0:T(8,128)(2,1)S(1)} collective-permute-done((bf16[2,40,128]{2,1,0:T(8,128)(2,1)S(1)}, bf16[2,40,128]{2,1,0:T(8,128)(2,1)S(1)}, u32[]{:S(2)}, u32[]{:S(2)}) %collective-permute-start.1) | collective-permute-done | bytes 20512 | tf_op jit(solution)/shard_map/ppermute | solution.py:363
  9.6 0.6 %early.1 = (bf16[5,144,128]{2,1,0:T(8,128)(2,1)S(1)}, bf16[2,160,128]{2,1,0:T(8,128)(2,1)S(1)}) custom-call(bf16[4,40,128]{2,1,0:T(8,128)(2,1)S(1)} %maximum_select_fusion.own, bf16[3,40,128]{2,1,0:T(8,128)(2,1)S(1)} %fusion.16.got, bf16[160,256]{1,0:T(8,128)(2,1)S(1)} %get-tuple-element.43.t1, bf16[144,256]{1,0:T(8,128)(2,1)S(1)} %get-tuple-element.44.t2, ...), custom_call_target="tpu_custom_call" | custom-call | tf_op jit(solution)/shard_map/early/pallas_call | solution.py:415
  10.2 0.1 %collective-permute-done.4.other = bf16[3,40,128]{2,1,0:T(8,128)(2,1)S(1)} collective-permute-done((bf16[3,40,128]{2,1,0:T(8,128)(2,1)S(1)}, bf16[3,40,128]{2,1,0:T(8,128)(2,1)S(1)}, u32[]{:S(2)}, u32[]{:S(2)}) %collective-permute-start.4) | collective-permute-done | bytes 30752 | tf_op jit(solution)/shard_map/ppermute | solution.py:414
  10.3 1.6 %late.1 = bf16[16,2,8,64]{3,2,1,0:T(8,128)(2,1)} custom-call(bf16[4,40,128]{2,1,0:T(8,128)(2,1)S(1)} %maximum_select_fusion.own, bf16[3,40,128]{2,1,0:T(8,128)(2,1)S(1)} %collective-permute-done.4.other, bf16[2,160,128]{2,1,0:T(8,128)(2,1)S(1)} %get-tuple-element.49.middle, bf16[5,144,128]{2,1,0:T(8,128)(2,1)S(1)} %get-tuple-element.50.done, ...), custom_call_target="tpu_custom_call" | custom-call | tf_op jit(solution)/shard_map/late/pallas_call | solution.py:427
  (6 shorter events, 0.1 us)
Async XLA Ops:
  0.8 1.3 %collective-permute-start = (bf16[1,64,128]{2,1,0:T(8,128)(2,1)S(1)}, bf16[1,64,128]{2,1,0:T(8,128)(2,1)S(1)}, u32[]{:S(2)}, u32[]{:S(2)}) collective-permute-start(bf16[1,64,128]{2,1,0:T(8,128)(2,1)S(1)} %convert_element_type.10), channel_id=1, source_target_pairs={{0,1},{1,0},{2,3},{3,2},{4,5},{5,4},{6,7},{7,6},{8,9},{9,8},{10,11... | collective-permute-start | bytes 49160 | tf_op jit(solution)/shard_map/ppermute | solution.py:357
  2.1 4.4 %copy-start.1 = (bf16[16,8,3,3,3]{0,1,4,3,2:T(8,128)(2,1)S(1)}, bf16[16,8,3,3,3]{0,1,4,3,2:T(8,128)(2,1)}, u32[]{:S(2)}) copy-start(bf16[16,8,3,3,3]{0,1,4,3,2:T(8,128)(2,1)} %param.12) | copy-start | bytes 20740
  2.2 4.3 %copy-start = (bf16[8,8,3,3,3]{1,0,4,3,2:T(8,128)(2,1)S(1)}, bf16[8,8,3,3,3]{1,0,4,3,2:T(8,128)(2,1)}, u32[]{:S(2)}) copy-start(bf16[8,8,3,3,3]{1,0,4,3,2:T(8,128)(2,1)} %param.10) | copy-start | bytes 10372
  2.3 4.2 %copy-start.2 = (bf16[8,1,3,3,3]{0,4,3,2,1:T(4,128)(2,1)S(1)}, bf16[8,1,3,3,3]{0,4,3,2,1:T(4,128)(2,1)}, u32[]{:S(2)}) copy-start(bf16[8,1,3,3,3]{0,4,3,2,1:T(4,128)(2,1)} %param.8) | copy-start | bytes 1300
  2.3 4.2 %collective-permute-start.3 = (bf16[2,40,128]{2,1,0:T(8,128)(2,1)S(1)}, bf16[2,40,128]{2,1,0:T(8,128)(2,1)S(1)}, u32[]{:S(2)}, u32[]{:S(2)}) collective-permute-start(bf16[2,40,128]{2,1,0:T(8,128)(2,1)S(1)} %get-tuple-element.54), channel_id=1, source_target_pairs={{0,5},{1,3},{2,7},{3,1},{4,9},{5,0},{6,11},{7,2},{8,13},{9,4},{10,... | collective-permute-start | bytes 61448 | tf_op jit(solution)/shard_map/ppermute | solution.py:361
  4.9 4.1 %collective-permute-start.2 = (bf16[2,40,128]{2,1,0:T(8,128)(2,1)S(1)}, bf16[2,40,128]{2,1,0:T(8,128)(2,1)S(1)}, u32[]{:S(2)}, u32[]{:S(2)}) collective-permute-start(bf16[2,40,128]{2,1,0:T(8,128)(2,1)S(1)} %get-tuple-element.53), channel_id=1, source_target_pairs={{0,7},{1,3},{2,5},{3,1},{4,11},{5,2},{6,9},{7,0},{8,15},{9,6},{10,... | collective-permute-start | bytes 61448 | tf_op jit(solution)/shard_map/ppermute | solution.py:362
  6.4 3.2 %collective-permute-start.1 = (bf16[2,40,128]{2,1,0:T(8,128)(2,1)S(1)}, bf16[2,40,128]{2,1,0:T(8,128)(2,1)S(1)}, u32[]{:S(2)}, u32[]{:S(2)}) collective-permute-start(bf16[2,40,128]{2,1,0:T(8,128)(2,1)S(1)} %get-tuple-element.53), channel_id=1, source_target_pairs={{0,3},{1,2},{2,1},{3,0},{4,7},{5,6},{6,5},{7,4},{8,11},{9,10},{10,... | collective-permute-start | bytes 61448 | tf_op jit(solution)/shard_map/ppermute | solution.py:363
  6.4 0.7 %copy-start.3 = (f32[8]{0:T(128)S(1)}, f32[8]{0:T(128)}, u32[]{:S(2)}) copy-start(f32[8]{0:T(128)} %param.9) | copy-start | bytes 100
  6.4 0.7 %copy-start.4 = (f32[8]{0:T(128)S(1)}, f32[8]{0:T(128)}, u32[]{:S(2)}) copy-start(f32[8]{0:T(128)} %param.11) | copy-start | bytes 100
  6.4 0.7 %copy-start.5 = (f32[16]{0:T(128)S(1)}, f32[16]{0:T(128)}, u32[]{:S(2)}) copy-start(f32[16]{0:T(128)} %param.13) | copy-start | bytes 196
  9.1 1.3 %collective-permute-start.4 = (bf16[3,40,128]{2,1,0:T(8,128)(2,1)S(1)}, bf16[3,40,128]{2,1,0:T(8,128)(2,1)S(1)}, u32[]{:S(2)}, u32[]{:S(2)}) collective-permute-start(bf16[3,40,128]{2,1,0:T(8,128)(2,1)S(1)} %fusion.16.got), channel_id=1, source_target_pairs={{0,1},{1,0},{2,3},{3,2},{4,5},{5,4},{6,7},{7,6},{8,9},{9,8},{10,11... | collective-permute-start | bytes 92168 | tf_op jit(solution)/shard_map/ppermute | solution.py:414

commit v8 on v7

--- a/solution.py
+++ b/solution.py
@@ -348,14 +348,38 @@
     return lax.dynamic_slice(planes, begin, (3, *planes.shape[1:]))
 
 
+def even_first(width):
+    row = lax.broadcasted_iota(jnp.int32, (width, width), 0)
+    col = lax.broadcasted_iota(jnp.int32, (width, width), 1)
+    return ones_where(row == 2 * lax.rem(col, width // 2) + lax.div(col, width // 2))
+
+
+def pair_kernel(plane, taken, pair):
+    upper = lax.rem(lax.axis_index("tile"), 2) == 1
+    order = even_first(plane.shape[2])
+    here, there = (
+        jnp.dot(ref[0].astype(BF), order, preferred_element_type=F32).astype(BF) for ref in (plane, taken)
+    )
+    pair[0] = jnp.where(upper, there, here)
+    pair[1] = jnp.where(upper, here, there)
+
+
 def exchanged(plan, plane, groups, tiles, weights, make_bands):
     axes, tile = ("freq", "tile"), lax.axis_index("tile")
     if tiles != 4:
-        own = gathered(plan, even_odd(plane), tiles)
+        planes = jnp.einsum("pyx,xw->pyw", plane.astype(BF), even_first(plane.shape[2]), preferred_element_type=F32)
+        own = gathered(plan, planes.astype(BF), tiles)
         message = some_planes(own, tile + 1)
         return own, lax.ppermute(message, axes, freq_pairs(groups, tiles, 1)), make_bands(weights)
     taken = lax.ppermute(plane, "tile", [(t, t ^ 1) for t in range(tiles)])
-    pair = even_odd(in_order(tile % 2 == 1, plane, taken))
+    pair = pl.pallas_call(
+        pair_kernel,
+        name="pair",
+        out_shape=jax.ShapeDtypeStruct((2, *plane.shape[1:]), BF),
+        in_specs=[VM] * 2,
+        out_specs=VM,
+        compiler_params=pltpu.CompilerParams(vmem_limit_bytes=32 * 2**20),
+    )(plane.astype(BF), taken)
     chip = tile // 2
     mine, theirs = chip_rows(plan, pair, chip), chip_rows(plan, pair, 1 - chip)
     ahead = lax.ppermute(mine, axes, freq_pairs(groups, tiles, 1))
@@ -366,14 +390,6 @@
     aside, *bands = lax.optimization_barrier((aside, *bands))
     own = in_order(chip == 1, mine, across)
     return own, some_planes(in_order(chip == 1, ahead, aside), tile), bands
-
-
-def even_odd(planes):
-    width = planes.shape[2]
-    row = lax.broadcasted_iota(jnp.int32, (width, width), 0)
-    col = lax.broadcasted_iota(jnp.int32, (width, width), 1)
-    order = (row == 2 * (col % (width // 2)) + col // (width // 2)).astype(BF)
-    return jnp.einsum("pyx,xw->pyw", planes, order, preferred_element_type=F32).astype(BF)
 
 
 def body(sky_cube, kernel_one, bias_one, kernel_two, bias_two, kernel_three, bias_three):
@@ -408,7 +424,7 @@
         )(*weights)
 
     own, got, weights = exchanged(
-        plan, sky_cube.astype(BF), groups, tiles, (bias_one[None], bias_two[None], bias_three[None], w1, w2, w3), make_bands
+        plan, sky_cube, groups, tiles, (bias_one[None], bias_two[None], bias_three[None], w1, w2, w3), make_bands
     )
     t1, t2, b1, b2, b3, t3 = weights
     other = lax.ppermute(got, "tile", [(t, t ^ 1) for t in range(tiles)])

time: 12.1 us -> 11.6 us (0.959)
  other arithmetic: 0.81 us -> 0.04 us
  local copies, waits for them, and re-layouts: 0.71 us -> 1.02 us
  Pallas kernels: 3.02 us -> 3.16 us
  matrix products: 0.14 us -> 0 us
    convert_element_type x1, other arithmetic: 0.76 us -> 0.01 us  [exchanged(): plane.astype(BF)]
    unnamed x12 -> x14, local copies, waits for them, and re-layouts: 0.66 us -> 0.98 us
    pallas_call x0 -> x1, Pallas kernels: none -> 0.14 us  [exchanged(): pl.pallas_call(pair_kernel, name='pair', out_shape=jax.ShapeDtypeStruct((...]
    dot_general x1 -> x0, matrix products: 0.14 us -> none  [even_odd(): jnp.einsum('pyx,xw->pyw', planes, order, preferred_element_type=F32)]
  transfers between devices with their start and end apart: 5 -> 5, of which waited for: 4 -> 4; matrix products, arithmetic and copies ran while one was open for 0% -> 0% of each run, Pallas kernels for 12% -> 13%
where the time goes in v8:
time: 11.6 us; the launch traced here: 11.4 us
  starting transfers between devices  4.68 us (40%)
  Pallas kernels  3.16 us (27%)
  waiting for transfers between devices  2.41 us (21%)
  local copies, waits for them, and re-layouts  1.02 us (9%)
    ppermute x1, starting transfers between devices, exchanged(): ahead = lax.ppermute(mine, axes, freq_pairs(groups, tiles, 1))  2.67 us
    pallas_call x1, Pallas kernels, body(): pl.pallas_call(functools.partial(late_kernel, plan), name='late', out_sha...  1.57 us
    ppermute x1, starting transfers between devices, exchanged(): aside = lax.ppermute(theirs, axes, freq_pairs(groups, tiles, 3))  1.44 us
    ppermute x1, waiting for transfers between devices, exchanged(): aside = lax.ppermute(theirs, axes, freq_pairs(groups, tiles, 3))  1.08 us
    unnamed x14, local copies, waits for them, and re-layouts  0.98 us
    pallas_call x1, Pallas kernels, make_bands(): pl.pallas_call(functools.partial(bands_kernel, plan), name='bands', out_s...  0.83 us
    ppermute x1, waiting for transfers between devices, exchanged(): taken = lax.ppermute(plane, 'tile', [(t, t ^ 1) for t in range(tiles)])  0.76 us
    pallas_call x1, Pallas kernels, body(): pl.pallas_call(functools.partial(early_kernel, plan), name='early', out_s...  0.61 us
  transfers between devices with their start and end apart: 5, of which 4 were waited for; matrix products, arithmetic and copies ran while one was open for 0% of the time, Pallas kernels for 13%

profile of v8, /device:TPU:0, one launch (start us, length us, event | category | flops | bytes accessed | tf_op | source)
XLA Modules:
  0.0 11.4 jit_solution(11573544209902240050)
XLA Ops:
  0.0 0.0 copy-start.6
  0.0 0.5 %collective-permute-start = (f32[1,64,128]{2,1,0:T(8,128)}, f32[1,64,128]{2,1,0:T(8,128)S(1)}, u32[]{:S(2)}, u32[]{:S(2)}) collective-permute-start(f32[1,64,128]{2,1,0:T(8,128)} %param.7), channel_id=1, source_target_pairs={{0,1},{1,0},{2,3},{3,2},{4,5},{5,4},{6,7},{7,6},{8,9},{9,8},{10,11... | collective-permute-start | bytes 98312 | tf_op jit(solution)/shard_map/ppermute | solution.py:374
  0.5 0.3 %copy-done.6 = f32[1,64,128]{2,1,0:T(8,128)S(1)} copy-done((f32[1,64,128]{2,1,0:T(8,128)S(1)}, f32[1,64,128]{2,1,0:T(8,128)}, u32[]{:S(2)}) %copy-start.6) | copy-done | bytes 32792
  0.8 0.8 %collective-permute-done.taken = f32[1,64,128]{2,1,0:T(8,128)S(1)} collective-permute-done((f32[1,64,128]{2,1,0:T(8,128)}, f32[1,64,128]{2,1,0:T(8,128)S(1)}, u32[]{:S(2)}, u32[]{:S(2)}) %collective-permute-start) | collective-permute-done | bytes 32800 | tf_op jit(solution)/shard_map/ppermute | solution.py:374
  1.5 0.0 copy-start.1
  1.5 0.1 %pair.1 = bf16[2,64,128]{2,1,0:T(8,128)(2,1)S(1)} custom-call(bf16[1,64,128]{2,1,0:T(8,128)(2,1)S(1)} %convert_element_type.6.plane, f32[1,64,128]{2,1,0:T(8,128)S(1)} %collective-permute-done.taken), custom_call_target="tpu_custom_call" | custom-call | tf_op jit(solution)/shard_map/pair/pallas_call | solution.py:375
  1.7 0.0 copy-start
  1.7 2.7 %collective-permute-start.3 = (bf16[2,40,128]{2,1,0:T(8,128)(2,1)S(1)}, bf16[2,40,128]{2,1,0:T(8,128)(2,1)S(1)}, u32[]{:S(2)}, u32[]{:S(2)}) collective-permute-start(bf16[2,40,128]{2,1,0:T(8,128)(2,1)S(1)} %get-tuple-element.54), channel_id=1, source_target_pairs={{0,5},{1,3},{2,7},{3,1},{4,9},{5,0},{6,11},{7,2},{8,13},{9,4},{10,... | collective-permute-start | bytes 61448 | tf_op jit(solution)/shard_map/ppermute | solution.py:385
  4.4 1.4 %collective-permute-start.2 = (bf16[2,40,128]{2,1,0:T(8,128)(2,1)S(1)}, bf16[2,40,128]{2,1,0:T(8,128)(2,1)S(1)}, u32[]{:S(2)}, u32[]{:S(2)}) collective-permute-start(bf16[2,40,128]{2,1,0:T(8,128)(2,1)S(1)} %get-tuple-element.53), channel_id=1, source_target_pairs={{0,7},{1,3},{2,5},{3,1},{4,11},{5,2},{6,9},{7,0},{8,15},{9,6},{10,... | collective-permute-start | bytes 61448 | tf_op jit(solution)/shard_map/ppermute | solution.py:386
  5.9 0.0 copy-start.2
  5.9 0.1 collective-permute-start.1
  5.9 0.0 collective-permute-done.3
  5.9 0.0 copy-start.3
  5.9 0.0 copy-start.4
  5.9 0.0 copy-start.5
  5.9 0.0 copy-done.1
  5.9 0.0 copy-done
  5.9 0.6 %copy-done.2 = bf16[8,1,3,3,3]{0,4,3,2,1:T(4,128)(2,1)S(1)} copy-done((bf16[8,1,3,3,3]{0,4,3,2,1:T(4,128)(2,1)S(1)}, bf16[8,1,3,3,3]{0,4,3,2,1:T(4,128)(2,1)}, u32[]{:S(2)}) %copy-start.2) | copy-done | bytes 456
  6.6 0.0 copy-done.3
  6.6 0.0 copy-done.4
  6.6 0.0 copy-done.5
  6.6 0.8 %bands.1 = (bf16[160,256]{1,0:T(8,128)(2,1)S(1)}, bf16[144,256]{1,0:T(8,128)(2,1)S(1)}, f32[8,128]{1,0:T(8,128)S(1)}, f32[8,128]{1,0:T(8,128)S(1)}, f32[16,8,128...) custom-call(f32[1,8]{1,0:T(1,128)S(1)} %bitcast.11, f32[1,8]{1,0:T(1,128)S(1)} %bitcast.12, f32[1,16]{1,0:T(1,128)S(1)} %bitcast.13, ...), custom_call_target="tpu_custom_call" | custom-call | tf_op jit(solution)/shard_map/bands/pallas_call | solution.py:410
  7.4 1.1 %collective-permute-done.2 = bf16[2,40,128]{2,1,0:T(8,128)(2,1)S(1)} collective-permute-done((bf16[2,40,128]{2,1,0:T(8,128)(2,1)S(1)}, bf16[2,40,128]{2,1,0:T(8,128)(2,1)S(1)}, u32[]{:S(2)}, u32[]{:S(2)}) %collective-permute-start.2) | collective-permute-done | bytes 20512 | tf_op jit(solution)/shard_map/ppermute | solution.py:386
  8.5 0.1 collective-permute-start.4
  8.6 0.4 %collective-permute-done.1 = bf16[2,40,128]{2,1,0:T(8,128)(2,1)S(1)} collective-permute-done((bf16[2,40,128]{2,1,0:T(8,128)(2,1)S(1)}, bf16[2,40,128]{2,1,0:T(8,128)(2,1)S(1)}, u32[]{:S(2)}, u32[]{:S(2)}) %collective-permute-start.1) | collective-permute-done | bytes 20512 | tf_op jit(solution)/shard_map/ppermute | solution.py:387
  9.1 0.6 %early.1 = (bf16[5,144,128]{2,1,0:T(8,128)(2,1)S(1)}, bf16[2,160,128]{2,1,0:T(8,128)(2,1)S(1)}) custom-call(bf16[4,40,128]{2,1,0:T(8,128)(2,1)S(1)} %maximum_select_fusion.own, bf16[3,40,128]{2,1,0:T(8,128)(2,1)S(1)} %fusion.1.got, bf16[160,256]{1,0:T(8,128)(2,1)S(1)} %get-tuple-element.43.t1, bf16[144,256]{1,0:T(8,128)(2,1)S(1)} %get-tuple-element.44.t2, ...), custom_call_target="tpu_custom_call" | custom-call | tf_op jit(solution)/shard_map/early/pallas_call | solution.py:431
  9.7 0.1 %collective-permute-done.4.other = bf16[3,40,128]{2,1,0:T(8,128)(2,1)S(1)} collective-permute-done((bf16[3,40,128]{2,1,0:T(8,128)(2,1)S(1)}, bf16[3,40,128]{2,1,0:T(8,128)(2,1)S(1)}, u32[]{:S(2)}, u32[]{:S(2)}) %collective-permute-start.4) | collective-permute-done | bytes 30752 | tf_op jit(solution)/shard_map/ppermute | solution.py:430
  9.8 1.6 %late.1 = bf16[16,2,8,64]{3,2,1,0:T(8,128)(2,1)} custom-call(bf16[4,40,128]{2,1,0:T(8,128)(2,1)S(1)} %maximum_select_fusion.own, bf16[3,40,128]{2,1,0:T(8,128)(2,1)S(1)} %collective-permute-done.4.other, bf16[2,160,128]{2,1,0:T(8,128)(2,1)S(1)} %get-tuple-element.49.middle, bf16[5,144,128]{2,1,0:T(8,128)(2,1)S(1)} %get-tuple-element.50.done, ...), custom_call_target="tpu_custom_call" | custom-call | tf_op jit(solution)/shard_map/late/pallas_call | solution.py:443
  (4 shorter events, 0.1 us)
Async XLA Ops:
  0.0 0.8 %copy-start.6 = (f32[1,64,128]{2,1,0:T(8,128)S(1)}, f32[1,64,128]{2,1,0:T(8,128)}, u32[]{:S(2)}) copy-start(f32[1,64,128]{2,1,0:T(8,128)} %param.7) | copy-start | bytes 98308
  0.0 1.5 %collective-permute-start = (f32[1,64,128]{2,1,0:T(8,128)}, f32[1,64,128]{2,1,0:T(8,128)S(1)}, u32[]{:S(2)}, u32[]{:S(2)}) collective-permute-start(f32[1,64,128]{2,1,0:T(8,128)} %param.7), channel_id=1, source_target_pairs={{0,1},{1,0},{2,3},{3,2},{4,5},{5,4},{6,7},{7,6},{8,9},{9,8},{10,11... | collective-permute-start | bytes 98312 | tf_op jit(solution)/shard_map/ppermute | solution.py:374
  1.5 4.4 %copy-start.1 = (bf16[16,8,3,3,3]{0,1,4,3,2:T(8,128)(2,1)S(1)}, bf16[16,8,3,3,3]{0,1,4,3,2:T(8,128)(2,1)}, u32[]{:S(2)}) copy-start(bf16[16,8,3,3,3]{0,1,4,3,2:T(8,128)(2,1)} %param.12) | copy-start | bytes 20740
  1.7 4.3 %copy-start = (bf16[8,8,3,3,3]{1,0,4,3,2:T(8,128)(2,1)S(1)}, bf16[8,8,3,3,3]{1,0,4,3,2:T(8,128)(2,1)}, u32[]{:S(2)}) copy-start(bf16[8,8,3,3,3]{1,0,4,3,2:T(8,128)(2,1)} %param.10) | copy-start | bytes 10372
  1.7 4.2 %collective-permute-start.3 = (bf16[2,40,128]{2,1,0:T(8,128)(2,1)S(1)}, bf16[2,40,128]{2,1,0:T(8,128)(2,1)S(1)}, u32[]{:S(2)}, u32[]{:S(2)}) collective-permute-start(bf16[2,40,128]{2,1,0:T(8,128)(2,1)S(1)} %get-tuple-element.54), channel_id=1, source_target_pairs={{0,5},{1,3},{2,7},{3,1},{4,9},{5,0},{6,11},{7,2},{8,13},{9,4},{10,... | collective-permute-start | bytes 61448 | tf_op jit(solution)/shard_map/ppermute | solution.py:385
  4.4 4.1 %collective-permute-start.2 = (bf16[2,40,128]{2,1,0:T(8,128)(2,1)S(1)}, bf16[2,40,128]{2,1,0:T(8,128)(2,1)S(1)}, u32[]{:S(2)}, u32[]{:S(2)}) collective-permute-start(bf16[2,40,128]{2,1,0:T(8,128)(2,1)S(1)} %get-tuple-element.53), channel_id=1, source_target_pairs={{0,7},{1,3},{2,5},{3,1},{4,11},{5,2},{6,9},{7,0},{8,15},{9,6},{10,... | collective-permute-start | bytes 61448 | tf_op jit(solution)/shard_map/ppermute | solution.py:386
  5.9 0.7 %copy-start.2 = (bf16[8,1,3,3,3]{0,4,3,2,1:T(4,128)(2,1)S(1)}, bf16[8,1,3,3,3]{0,4,3,2,1:T(4,128)(2,1)}, u32[]{:S(2)}) copy-start(bf16[8,1,3,3,3]{0,4,3,2,1:T(4,128)(2,1)} %param.8) | copy-start | bytes 1300
  5.9 3.2 %collective-permute-start.1 = (bf16[2,40,128]{2,1,0:T(8,128)(2,1)S(1)}, bf16[2,40,128]{2,1,0:T(8,128)(2,1)S(1)}, u32[]{:S(2)}, u32[]{:S(2)}) collective-permute-start(bf16[2,40,128]{2,1,0:T(8,128)(2,1)S(1)} %get-tuple-element.53), channel_id=1, source_target_pairs={{0,3},{1,2},{2,1},{3,0},{4,7},{5,6},{6,5},{7,4},{8,11},{9,10},{10,... | collective-permute-start | bytes 61448 | tf_op jit(solution)/shard_map/ppermute | solution.py:387
  5.9 0.7 %copy-start.3 = (f32[8]{0:T(128)S(1)}, f32[8]{0:T(128)}, u32[]{:S(2)}) copy-start(f32[8]{0:T(128)} %param.9) | copy-start | bytes 100
  5.9 0.7 %copy-start.4 = (f32[8]{0:T(128)S(1)}, f32[8]{0:T(128)}, u32[]{:S(2)}) copy-start(f32[8]{0:T(128)} %param.11) | copy-start | bytes 100
  5.9 0.7 %copy-start.5 = (f32[16]{0:T(128)S(1)}, f32[16]{0:T(128)}, u32[]{:S(2)}) copy-start(f32[16]{0:T(128)} %param.13) | copy-start | bytes 196
  8.5 1.3 %collective-permute-start.4 = (bf16[3,40,128]{2,1,0:T(8,128)(2,1)S(1)}, bf16[3,40,128]{2,1,0:T(8,128)(2,1)S(1)}, u32[]{:S(2)}, u32[]{:S(2)}) collective-permute-start(bf16[3,40,128]{2,1,0:T(8,128)(2,1)S(1)} %fusion.1.got), channel_id=1, source_target_pairs={{0,1},{1,0},{2,3},{3,2},{4,5},{5,4},{6,7},{7,6},{8,9},{9,8},{10,11... | collective-permute-start | bytes 92168 | tf_op jit(solution)/shard_map/ppermute | solution.py:430

commit v9 on v8

--- a/solution.py
+++ b/solution.py
@@ -354,14 +354,18 @@
     return ones_where(row == 2 * lax.rem(col, width // 2) + lax.div(col, width // 2))
 
 
-def pair_kernel(plane, taken, pair):
-    upper = lax.rem(lax.axis_index("tile"), 2) == 1
+def pair_kernel(plan, plane, taken, mine, theirs):
+    tile = lax.axis_index("tile")
+    upper, second = lax.rem(tile, 2) == 1, tile >= 2
     order = even_first(plane.shape[2])
-    here, there = (
-        jnp.dot(ref[0].astype(BF), order, preferred_element_type=F32).astype(BF) for ref in (plane, taken)
-    )
-    pair[0] = jnp.where(upper, there, here)
-    pair[1] = jnp.where(upper, here, there)
+    inside = plan.span - plan.rim
+    edge = jnp.zeros((plan.rim, plane.shape[2]), F32)
+    here, there = (jnp.dot(ref[0].astype(BF), order, preferred_element_type=F32) for ref in (plane, taken))
+    for p, rows in enumerate((jnp.where(upper, there, here), jnp.where(upper, here, there))):
+        top = jnp.concatenate([edge, rows[:inside]], axis=0)
+        bottom = jnp.concatenate([rows[rows.shape[0] - inside :], edge], axis=0)
+        mine[p] = jnp.where(second, bottom, top).astype(BF)
+        theirs[p] = jnp.where(second, top, bottom).astype(BF)
 
 
 def exchanged(plan, plane, groups, tiles, weights, make_bands):
@@ -372,16 +376,16 @@
         message = some_planes(own, tile + 1)
         return own, lax.ppermute(message, axes, freq_pairs(groups, tiles, 1)), make_bands(weights)
     taken = lax.ppermute(plane, "tile", [(t, t ^ 1) for t in range(tiles)])
-    pair = pl.pallas_call(
-        pair_kernel,
+    window = jax.ShapeDtypeStruct((2, plan.span, plane.shape[2]), BF)
+    mine, theirs = pl.pallas_call(
+        functools.partial(pair_kernel, plan),
         name="pair",
-        out_shape=jax.ShapeDtypeStruct((2, *plane.shape[1:]), BF),
+        out_shape=[window] * 2,
         in_specs=[VM] * 2,
-        out_specs=VM,
+        out_specs=[VM] * 2,
         compiler_params=pltpu.CompilerParams(vmem_limit_bytes=32 * 2**20),
     )(plane.astype(BF), taken)
     chip = tile // 2
-    mine, theirs = chip_rows(plan, pair, chip), chip_rows(plan, pair, 1 - chip)
     ahead = lax.ppermute(mine, axes, freq_pairs(groups, tiles, 1))
     aside = lax.ppermute(theirs, axes, freq_pairs(groups, tiles, 3))
     across = lax.ppermute(theirs, "tile", [(t, t ^ 3) for t in range(tiles)])

time: 11.6 us -> 11.5 us (level)
  other arithmetic: 0.04 us -> 0.81 us
  waiting for transfers between devices: 2.41 us -> 1.94 us
  local copies, waits for them, and re-layouts: 1.02 us -> 0.66 us
    convert_element_type x1, other arithmetic: 0.01 us -> 0.77 us  [exchanged(): plane.astype(BF)]
    ppermute x1, waiting for transfers between devices: 0.76 us -> 0.29 us  [exchanged(): taken = lax.ppermute(plane, 'tile', [(t, t ^ 1) for t in range(tiles)])]
    unnamed x14 -> x12, local copies, waits for them, and re-layouts: 0.98 us -> 0.66 us
  transfers between devices with their start and end apart: 5 -> 5, of which waited for: 4 -> 4; matrix products, arithmetic and copies ran while one was open for 0% -> 7% of each run, Pallas kernels for 13% -> 13%
where the time goes in v9:
time: 11.5 us; the launch traced here: 11.3 us
  starting transfers between devices  4.68 us (41%)
  Pallas kernels  3.16 us (27%)
  waiting for transfers between devices  1.94 us (17%)
  other arithmetic  0.81 us (7%)
  local copies, waits for them, and re-layouts  0.66 us (6%)
    ppermute x1, starting transfers between devices, exchanged(): ahead = lax.ppermute(mine, axes, freq_pairs(groups, tiles, 1))  2.67 us
    pallas_call x1, Pallas kernels, body(): pl.pallas_call(functools.partial(late_kernel, plan), name='late', out_sha...  1.58 us
    ppermute x1, starting transfers between devices, exchanged(): aside = lax.ppermute(theirs, axes, freq_pairs(groups, tiles, 3))  1.44 us
    ppermute x1, waiting for transfers between devices, exchanged(): aside = lax.ppermute(theirs, axes, freq_pairs(groups, tiles, 3))  1.08 us
    pallas_call x1, Pallas kernels, make_bands(): pl.pallas_call(functools.partial(bands_kernel, plan), name='bands', out_s...  0.83 us
    convert_element_type x1, other arithmetic, exchanged(): plane.astype(BF)  0.77 us
    unnamed x12, local copies, waits for them, and re-layouts  0.66 us
    pallas_call x1, Pallas kernels, body(): pl.pallas_call(functools.partial(early_kernel, plan), name='early', out_s...  0.61 us
  transfers between devices with their start and end apart: 5, of which 4 were waited for; matrix products, arithmetic and copies ran while one was open for 7% of the time, Pallas kernels for 13%

profile of v9, /device:TPU:0, one launch (start us, length us, event | category | flops | bytes accessed | tf_op | source)
XLA Modules:
  0.0 11.3 jit_solution(17493731879270533414)
XLA Ops:
  0.0 0.5 %collective-permute-start = (f32[1,64,128]{2,1,0:T(8,128)}, f32[1,64,128]{2,1,0:T(8,128)S(1)}, u32[]{:S(2)}, u32[]{:S(2)}) collective-permute-start(f32[1,64,128]{2,1,0:T(8,128)} %param.7), channel_id=1, source_target_pairs={{0,1},{1,0},{2,3},{3,2},{4,5},{5,4},{6,7},{7,6},{8,9},{9,8},{10,11... | collective-permute-start | bytes 98312 | tf_op jit(solution)/shard_map/ppermute | solution.py:378
  0.5 0.0 copy-start.2
  0.5 0.8 %convert_element_type.3.plane = bf16[1,64,128]{2,1,0:T(8,128)(2,1)S(1)} convert(f32[1,64,128]{2,1,0:T(8,128)} %param.7) | non-fusion elementwise | flops 8192 | bytes 49152 | tf_op jit(solution)/shard_map/convert_element_type | solution.py:387
  1.2 0.0 copy-start
  1.2 0.0 copy-start.1
  1.2 0.3 %collective-permute-done.taken = f32[1,64,128]{2,1,0:T(8,128)S(1)} collective-permute-done((f32[1,64,128]{2,1,0:T(8,128)}, f32[1,64,128]{2,1,0:T(8,128)S(1)}, u32[]{:S(2)}, u32[]{:S(2)}) %collective-permute-start) | collective-permute-done | bytes 32800 | tf_op jit(solution)/shard_map/ppermute | solution.py:378
  1.5 0.1 %pair.1 = (bf16[2,40,128]{2,1,0:T(8,128)(2,1)S(1)}, bf16[2,40,128]{2,1,0:T(8,128)(2,1)S(1)}) custom-call(bf16[1,64,128]{2,1,0:T(8,128)(2,1)S(1)} %convert_element_type.3.plane, f32[1,64,128]{2,1,0:T(8,128)S(1)} %collective-permute-done.taken), custom_call_target="tpu_custom_call" | custom-call | tf_op jit(solution)/shard_map/pair/pallas_call | solution.py:380
  1.7 2.7 %collective-permute-start.3 = (bf16[2,40,128]{2,1,0:T(8,128)(2,1)S(1)}, bf16[2,40,128]{2,1,0:T(8,128)(2,1)S(1)}, u32[]{:S(2)}, u32[]{:S(2)}) collective-permute-start(bf16[2,40,128]{2,1,0:T(8,128)(2,1)S(1)} %get-tuple-element.32), channel_id=1, source_target_pairs={{0,5},{1,3},{2,7},{3,1},{4,9},{5,0},{6,11},{7,2},{8,13},{9,4},{10,... | collective-permute-start | bytes 61448 | tf_op jit(solution)/shard_map/ppermute | solution.py:389
  4.3 1.4 %collective-permute-start.2 = (bf16[2,40,128]{2,1,0:T(8,128)(2,1)S(1)}, bf16[2,40,128]{2,1,0:T(8,128)(2,1)S(1)}, u32[]{:S(2)}, u32[]{:S(2)}) collective-permute-start(bf16[2,40,128]{2,1,0:T(8,128)(2,1)S(1)} %get-tuple-element.31), channel_id=1, source_target_pairs={{0,7},{1,3},{2,5},{3,1},{4,11},{5,2},{6,9},{7,0},{8,15},{9,6},{10,... | collective-permute-start | bytes 61448 | tf_op jit(solution)/shard_map/ppermute | solution.py:390
  5.8 0.1 collective-permute-start.1
  5.8 0.0 collective-permute-done.3
  5.8 0.0 copy-start.3
  5.8 0.0 copy-start.4
  5.8 0.0 copy-start.5
  5.9 0.0 copy-done.2
  5.9 0.0 copy-done
  5.9 0.0 copy-done.1
  5.9 0.6 %copy-done.3 = f32[8]{0:T(128)S(1)} copy-done((f32[8]{0:T(128)S(1)}, f32[8]{0:T(128)}, u32[]{:S(2)}) %copy-start.3) | copy-done | bytes 56
  6.5 0.0 copy-done.4
  6.5 0.0 copy-done.5
  6.5 0.8 %bands.1 = (bf16[160,256]{1,0:T(8,128)(2,1)S(1)}, bf16[144,256]{1,0:T(8,128)(2,1)S(1)}, f32[8,128]{1,0:T(8,128)S(1)}, f32[8,128]{1,0:T(8,128)S(1)}, f32[16,8,128...) custom-call(f32[1,8]{1,0:T(1,128)S(1)} %bitcast.11, f32[1,8]{1,0:T(1,128)S(1)} %bitcast.12, f32[1,16]{1,0:T(1,128)S(1)} %bitcast.13, ...), custom_call_target="tpu_custom_call" | custom-call | tf_op jit(solution)/shard_map/bands/pallas_call | solution.py:414
  7.4 1.1 %collective-permute-done.2 = bf16[2,40,128]{2,1,0:T(8,128)(2,1)S(1)} collective-permute-done((bf16[2,40,128]{2,1,0:T(8,128)(2,1)S(1)}, bf16[2,40,128]{2,1,0:T(8,128)(2,1)S(1)}, u32[]{:S(2)}, u32[]{:S(2)}) %collective-permute-start.2) | collective-permute-done | bytes 20512 | tf_op jit(solution)/shard_map/ppermute | solution.py:390
  8.5 0.1 collective-permute-start.4
  8.6 0.4 %collective-permute-done.1 = bf16[2,40,128]{2,1,0:T(8,128)(2,1)S(1)} collective-permute-done((bf16[2,40,128]{2,1,0:T(8,128)(2,1)S(1)}, bf16[2,40,128]{2,1,0:T(8,128)(2,1)S(1)}, u32[]{:S(2)}, u32[]{:S(2)}) %collective-permute-start.1) | collective-permute-done | bytes 20512 | tf_op jit(solution)/shard_map/ppermute | solution.py:391
  9.0 0.6 %early.1 = (bf16[5,144,128]{2,1,0:T(8,128)(2,1)S(1)}, bf16[2,160,128]{2,1,0:T(8,128)(2,1)S(1)}) custom-call(bf16[4,40,128]{2,1,0:T(8,128)(2,1)S(1)} %maximum_select_fusion.own, bf16[3,40,128]{2,1,0:T(8,128)(2,1)S(1)} %fusion.1.got, bf16[160,256]{1,0:T(8,128)(2,1)S(1)} %get-tuple-element.47.t1, bf16[144,256]{1,0:T(8,128)(2,1)S(1)} %get-tuple-element.48.t2, ...), custom_call_target="tpu_custom_call" | custom-call | tf_op jit(solution)/shard_map/early/pallas_call | solution.py:435
  9.6 0.1 %collective-permute-done.4.other = bf16[3,40,128]{2,1,0:T(8,128)(2,1)S(1)} collective-permute-done((bf16[3,40,128]{2,1,0:T(8,128)(2,1)S(1)}, bf16[3,40,128]{2,1,0:T(8,128)(2,1)S(1)}, u32[]{:S(2)}, u32[]{:S(2)}) %collective-permute-start.4) | collective-permute-done | bytes 30752 | tf_op jit(solution)/shard_map/ppermute | solution.py:434
  9.8 1.6 %late.1 = bf16[16,2,8,64]{3,2,1,0:T(8,128)(2,1)} custom-call(bf16[4,40,128]{2,1,0:T(8,128)(2,1)S(1)} %maximum_select_fusion.own, bf16[3,40,128]{2,1,0:T(8,128)(2,1)S(1)} %collective-permute-done.4.other, bf16[2,160,128]{2,1,0:T(8,128)(2,1)S(1)} %get-tuple-element.53.middle, bf16[5,144,128]{2,1,0:T(8,128)(2,1)S(1)} %get-tuple-element.54.done, ...), custom_call_target="tpu_custom_call" | custom-call | tf_op jit(solution)/shard_map/late/pallas_call | solution.py:447
  (2 shorter events, 0.0 us)
Async XLA Ops:
  0.0 1.5 %collective-permute-start = (f32[1,64,128]{2,1,0:T(8,128)}, f32[1,64,128]{2,1,0:T(8,128)S(1)}, u32[]{:S(2)}, u32[]{:S(2)}) collective-permute-start(f32[1,64,128]{2,1,0:T(8,128)} %param.7), channel_id=1, source_target_pairs={{0,1},{1,0},{2,3},{3,2},{4,5},{5,4},{6,7},{7,6},{8,9},{9,8},{10,11... | collective-permute-start | bytes 98312 | tf_op jit(solution)/shard_map/ppermute | solution.py:378
  0.5 5.4 %copy-start.2 = (bf16[8,1,3,3,3]{0,4,3,2,1:T(4,128)(2,1)S(1)}, bf16[8,1,3,3,3]{0,4,3,2,1:T(4,128)(2,1)}, u32[]{:S(2)}) copy-start(bf16[8,1,3,3,3]{0,4,3,2,1:T(4,128)(2,1)} %param.8) | copy-start | bytes 1300
  1.2 4.6 %copy-start = (bf16[8,8,3,3,3]{1,0,4,3,2:T(8,128)(2,1)S(1)}, bf16[8,8,3,3,3]{1,0,4,3,2:T(8,128)(2,1)}, u32[]{:S(2)}) copy-start(bf16[8,8,3,3,3]{1,0,4,3,2:T(8,128)(2,1)} %param.10) | copy-start | bytes 10372
  1.2 4.6 %copy-start.1 = (bf16[16,8,3,3,3]{0,1,4,3,2:T(8,128)(2,1)S(1)}, bf16[16,8,3,3,3]{0,1,4,3,2:T(8,128)(2,1)}, u32[]{:S(2)}) copy-start(bf16[16,8,3,3,3]{0,1,4,3,2:T(8,128)(2,1)} %param.12) | copy-start | bytes 20740
  1.7 4.2 %collective-permute-start.3 = (bf16[2,40,128]{2,1,0:T(8,128)(2,1)S(1)}, bf16[2,40,128]{2,1,0:T(8,128)(2,1)S(1)}, u32[]{:S(2)}, u32[]{:S(2)}) collective-permute-start(bf16[2,40,128]{2,1,0:T(8,128)(2,1)S(1)} %get-tuple-element.32), channel_id=1, source_target_pairs={{0,5},{1,3},{2,7},{3,1},{4,9},{5,0},{6,11},{7,2},{8,13},{9,4},{10,... | collective-permute-start | bytes 61448 | tf_op jit(solution)/shard_map/ppermute | solution.py:389
  4.3 4.1 %collective-permute-start.2 = (bf16[2,40,128]{2,1,0:T(8,128)(2,1)S(1)}, bf16[2,40,128]{2,1,0:T(8,128)(2,1)S(1)}, u32[]{:S(2)}, u32[]{:S(2)}) collective-permute-start(bf16[2,40,128]{2,1,0:T(8,128)(2,1)S(1)} %get-tuple-element.31), channel_id=1, source_target_pairs={{0,7},{1,3},{2,5},{3,1},{4,11},{5,2},{6,9},{7,0},{8,15},{9,6},{10,... | collective-permute-start | bytes 61448 | tf_op jit(solution)/shard_map/ppermute | solution.py:390
  5.8 3.2 %collective-permute-start.1 = (bf16[2,40,128]{2,1,0:T(8,128)(2,1)S(1)}, bf16[2,40,128]{2,1,0:T(8,128)(2,1)S(1)}, u32[]{:S(2)}, u32[]{:S(2)}) collective-permute-start(bf16[2,40,128]{2,1,0:T(8,128)(2,1)S(1)} %get-tuple-element.31), channel_id=1, source_target_pairs={{0,3},{1,2},{2,1},{3,0},{4,7},{5,6},{6,5},{7,4},{8,11},{9,10},{10,... | collective-permute-start | bytes 61448 | tf_op jit(solution)/shard_map/ppermute | solution.py:391
  5.8 0.7 %copy-start.3 = (f32[8]{0:T(128)S(1)}, f32[8]{0:T(128)}, u32[]{:S(2)}) copy-start(f32[8]{0:T(128)} %param.9) | copy-start | bytes 100
  5.8 0.7 %copy-start.4 = (f32[8]{0:T(128)S(1)}, f32[8]{0:T(128)}, u32[]{:S(2)}) copy-start(f32[8]{0:T(128)} %param.11) | copy-start | bytes 100
  5.8 0.7 %copy-start.5 = (f32[16]{0:T(128)S(1)}, f32[16]{0:T(128)}, u32[]{:S(2)}) copy-start(f32[16]{0:T(128)} %param.13) | copy-start | bytes 196
  8.5 1.3 %collective-permute-start.4 = (bf16[3,40,128]{2,1,0:T(8,128)(2,1)S(1)}, bf16[3,40,128]{2,1,0:T(8,128)(2,1)S(1)}, u32[]{:S(2)}, u32[]{:S(2)}) collective-permute-start(bf16[3,40,128]{2,1,0:T(8,128)(2,1)S(1)} %fusion.1.got), channel_id=1, source_target_pairs={{0,1},{1,0},{2,3},{3,2},{4,5},{5,4},{6,7},{7,6},{8,9},{9,8},{10,11... | collective-permute-start | bytes 92168 | tf_op jit(solution)/shard_map/ppermute | solution.py:434

commit v10 on v9

--- a/solution.py
+++ b/solution.py
@@ -235,9 +235,9 @@
     return {q: jnp.concatenate(parts, axis=0) for q, parts in blocks.items()}
 
 
-def layer_three(plan, layer_two, t3, b3, out):
+def layer_three(plan, layer_two, t3, b3, out, order):
     n3, rows = plan.out3, plan.block3
-    for f in range(plan.depth // 2):
+    for f in order:
         planes = [layer_two(2 * f + a) for a in range(3)]
         for y in range(0, plan.r3, 2 * rows):
             first, second = (
@@ -266,9 +266,9 @@
 def lower_half(plan, place, own, halo, t1, t2, b1, b2, middle=None):
     pieces = [piece(plan, rim_rows(plan, place, halo, p, place.has_lower)) for p in range(3)]
     pieces += [piece(plan, own_rows(plan, place, own, p)) for p in range(plan.depth if middle is None else 2)]
-    made = layer_one(plan, place, pieces, range(plan.depth + 1 if middle is None else 3), t1, b1)
+    made = layer_one(plan, place, pieces, range(plan.depth + 1) if middle is None else (2, 1, 0), t1, b1)
     some = lambda p: made[p] if p in made else middle[p - 3]
-    return layer_two(plan, place, some, range(3), t2, b2), made
+    return layer_two(plan, place, some, (2, 1, 0), t2, b2), made
 
 
 def upper_half(plan, place, own, halo, t1, t2, b1, b2, middle=None):
@@ -299,12 +299,13 @@
 def late_kernel(plan, own, other, middle, done, t1, t2, b1, b2, t3, b3, out):
     place = Place()
 
-    def run(half):
+    def run(half, order):
         late, _ = half(plan, place, own, other, t1, t2, b1, b2, middle)
-        layer_three(plan, lambda q: late[q] if q in late else done[q], t3, b3, out)
-
-    pl.when(place.faces_lower)(lambda: run(upper_half))
-    pl.when(jnp.logical_not(place.faces_lower))(lambda: run(lower_half))
+        layer_three(plan, lambda q: late[q] if q in late else done[q], t3, b3, out, order)
+
+    first = range(plan.depth // 2)
+    pl.when(place.faces_lower)(lambda: run(upper_half, first))
+    pl.when(jnp.logical_not(place.faces_lower))(lambda: run(lower_half, first[::-1]))
 
 
 def in_order(upper, held, taken):

time: 11.5 us -> 11.5 us (level)
  no operation moved by 1% of the time
where the time goes in v10:
time: 11.5 us; the launch traced here: 11.3 us
  starting transfers between devices  4.68 us (41%)
  Pallas kernels  3.11 us (27%)
  waiting for transfers between devices  1.94 us (17%)
  other arithmetic  0.81 us (7%)
  local copies, waits for them, and re-layouts  0.66 us (6%)
    ppermute x1, starting transfers between devices, exchanged(): ahead = lax.ppermute(mine, axes, freq_pairs(groups, tiles, 1))  2.67 us
    pallas_call x1, Pallas kernels, body(): pl.pallas_call(functools.partial(late_kernel, plan), name='late', out_sha...  1.53 us
    ppermute x1, starting transfers between devices, exchanged(): aside = lax.ppermute(theirs, axes, freq_pairs(groups, tiles, 3))  1.44 us
    ppermute x1, waiting for transfers between devices, exchanged(): aside = lax.ppermute(theirs, axes, freq_pairs(groups, tiles, 3))  1.08 us
    pallas_call x1, Pallas kernels, make_bands(): pl.pallas_call(functools.partial(bands_kernel, plan), name='bands', out_s...  0.83 us
    convert_element_type x1, other arithmetic, exchanged(): plane.astype(BF)  0.77 us
    unnamed x12, local copies, waits for them, and re-layouts  0.66 us
    pallas_call x1, Pallas kernels, body(): pl.pallas_call(functools.partial(early_kernel, plan), name='early', out_s...  0.61 us
  transfers between devices with their start and end apart: 5, of which 4 were waited for; matrix products, arithmetic and copies ran while one was open for 7% of the time, Pallas kernels for 13%

profile of v10, /device:TPU:0, one launch (start us, length us, event | category | flops | bytes accessed | tf_op | source)
XLA Modules:
  0.0 11.3 jit_solution(8714144891900665847)
XLA Ops:
  0.0 0.5 %collective-permute-start = (f32[1,64,128]{2,1,0:T(8,128)}, f32[1,64,128]{2,1,0:T(8,128)S(1)}, u32[]{:S(2)}, u32[]{:S(2)}) collective-permute-start(f32[1,64,128]{2,1,0:T(8,128)} %param.7), channel_id=1, source_target_pairs={{0,1},{1,0},{2,3},{3,2},{4,5},{5,4},{6,7},{7,6},{8,9},{9,8},{10,11... | collective-permute-start | bytes 98312 | tf_op jit(solution)/shard_map/ppermute | solution.py:379
  0.5 0.0 copy-start.2
  0.5 0.8 %convert_element_type.3.plane = bf16[1,64,128]{2,1,0:T(8,128)(2,1)S(1)} convert(f32[1,64,128]{2,1,0:T(8,128)} %param.7) | non-fusion elementwise | flops 8192 | bytes 49152 | tf_op jit(solution)/shard_map/convert_element_type | solution.py:388
  1.2 0.0 copy-start
  1.2 0.0 copy-start.1
  1.2 0.3 %collective-permute-done.taken = f32[1,64,128]{2,1,0:T(8,128)S(1)} collective-permute-done((f32[1,64,128]{2,1,0:T(8,128)}, f32[1,64,128]{2,1,0:T(8,128)S(1)}, u32[]{:S(2)}, u32[]{:S(2)}) %collective-permute-start) | collective-permute-done | bytes 32800 | tf_op jit(solution)/shard_map/ppermute | solution.py:379
  1.5 0.1 %pair.1 = (bf16[2,40,128]{2,1,0:T(8,128)(2,1)S(1)}, bf16[2,40,128]{2,1,0:T(8,128)(2,1)S(1)}) custom-call(bf16[1,64,128]{2,1,0:T(8,128)(2,1)S(1)} %convert_element_type.3.plane, f32[1,64,128]{2,1,0:T(8,128)S(1)} %collective-permute-done.taken), custom_call_target="tpu_custom_call" | custom-call | tf_op jit(solution)/shard_map/pair/pallas_call | solution.py:381
  1.7 2.7 %collective-permute-start.3 = (bf16[2,40,128]{2,1,0:T(8,128)(2,1)S(1)}, bf16[2,40,128]{2,1,0:T(8,128)(2,1)S(1)}, u32[]{:S(2)}, u32[]{:S(2)}) collective-permute-start(bf16[2,40,128]{2,1,0:T(8,128)(2,1)S(1)} %get-tuple-element.32), channel_id=1, source_target_pairs={{0,5},{1,3},{2,7},{3,1},{4,9},{5,0},{6,11},{7,2},{8,13},{9,4},{10,... | collective-permute-start | bytes 61448 | tf_op jit(solution)/shard_map/ppermute | solution.py:390
  4.3 1.4 %collective-permute-start.2 = (bf16[2,40,128]{2,1,0:T(8,128)(2,1)S(1)}, bf16[2,40,128]{2,1,0:T(8,128)(2,1)S(1)}, u32[]{:S(2)}, u32[]{:S(2)}) collective-permute-start(bf16[2,40,128]{2,1,0:T(8,128)(2,1)S(1)} %get-tuple-element.31), channel_id=1, source_target_pairs={{0,7},{1,3},{2,5},{3,1},{4,11},{5,2},{6,9},{7,0},{8,15},{9,6},{10,... | collective-permute-start | bytes 61448 | tf_op jit(solution)/shard_map/ppermute | solution.py:391
  5.8 0.1 collective-permute-start.1
  5.8 0.0 collective-permute-done.3
  5.8 0.0 copy-start.3
  5.8 0.0 copy-start.4
  5.8 0.0 copy-start.5
  5.9 0.0 copy-done.2
  5.9 0.0 copy-done
  5.9 0.0 copy-done.1
  5.9 0.6 %copy-done.3 = f32[8]{0:T(128)S(1)} copy-done((f32[8]{0:T(128)S(1)}, f32[8]{0:T(128)}, u32[]{:S(2)}) %copy-start.3) | copy-done | bytes 56
  6.5 0.0 copy-done.4
  6.5 0.0 copy-done.5
  6.5 0.8 %bands.1 = (bf16[160,256]{1,0:T(8,128)(2,1)S(1)}, bf16[144,256]{1,0:T(8,128)(2,1)S(1)}, f32[8,128]{1,0:T(8,128)S(1)}, f32[8,128]{1,0:T(8,128)S(1)}, f32[16,8,128...) custom-call(f32[1,8]{1,0:T(1,128)S(1)} %bitcast.11, f32[1,8]{1,0:T(1,128)S(1)} %bitcast.12, f32[1,16]{1,0:T(1,128)S(1)} %bitcast.13, ...), custom_call_target="tpu_custom_call" | custom-call | tf_op jit(solution)/shard_map/bands/pallas_call | solution.py:415
  7.4 1.1 %collective-permute-done.2 = bf16[2,40,128]{2,1,0:T(8,128)(2,1)S(1)} collective-permute-done((bf16[2,40,128]{2,1,0:T(8,128)(2,1)S(1)}, bf16[2,40,128]{2,1,0:T(8,128)(2,1)S(1)}, u32[]{:S(2)}, u32[]{:S(2)}) %collective-permute-start.2) | collective-permute-done | bytes 20512 | tf_op jit(solution)/shard_map/ppermute | solution.py:391
  8.5 0.1 collective-permute-start.4
  8.6 0.4 %collective-permute-done.1 = bf16[2,40,128]{2,1,0:T(8,128)(2,1)S(1)} collective-permute-done((bf16[2,40,128]{2,1,0:T(8,128)(2,1)S(1)}, bf16[2,40,128]{2,1,0:T(8,128)(2,1)S(1)}, u32[]{:S(2)}, u32[]{:S(2)}) %collective-permute-start.1) | collective-permute-done | bytes 20512 | tf_op jit(solution)/shard_map/ppermute | solution.py:392
  9.0 0.6 %early.1 = (bf16[5,144,128]{2,1,0:T(8,128)(2,1)S(1)}, bf16[2,160,128]{2,1,0:T(8,128)(2,1)S(1)}) custom-call(bf16[4,40,128]{2,1,0:T(8,128)(2,1)S(1)} %maximum_select_fusion.own, bf16[3,40,128]{2,1,0:T(8,128)(2,1)S(1)} %fusion.1.got, bf16[160,256]{1,0:T(8,128)(2,1)S(1)} %get-tuple-element.47.t1, bf16[144,256]{1,0:T(8,128)(2,1)S(1)} %get-tuple-element.48.t2, ...), custom_call_target="tpu_custom_call" | custom-call | tf_op jit(solution)/shard_map/early/pallas_call | solution.py:436
  9.6 0.1 %collective-permute-done.4.other = bf16[3,40,128]{2,1,0:T(8,128)(2,1)S(1)} collective-permute-done((bf16[3,40,128]{2,1,0:T(8,128)(2,1)S(1)}, bf16[3,40,128]{2,1,0:T(8,128)(2,1)S(1)}, u32[]{:S(2)}, u32[]{:S(2)}) %collective-permute-start.4) | collective-permute-done | bytes 30752 | tf_op jit(solution)/shard_map/ppermute | solution.py:435
  9.8 1.5 %late.1 = bf16[16,2,8,64]{3,2,1,0:T(8,128)(2,1)} custom-call(bf16[4,40,128]{2,1,0:T(8,128)(2,1)S(1)} %maximum_select_fusion.own, bf16[3,40,128]{2,1,0:T(8,128)(2,1)S(1)} %collective-permute-done.4.other, bf16[2,160,128]{2,1,0:T(8,128)(2,1)S(1)} %get-tuple-element.53.middle, bf16[5,144,128]{2,1,0:T(8,128)(2,1)S(1)} %get-tuple-element.54.done, ...), custom_call_target="tpu_custom_call" | custom-call | tf_op jit(solution)/shard_map/late/pallas_call | solution.py:448
  (2 shorter events, 0.0 us)
Async XLA Ops:
  0.0 1.5 %collective-permute-start = (f32[1,64,128]{2,1,0:T(8,128)}, f32[1,64,128]{2,1,0:T(8,128)S(1)}, u32[]{:S(2)}, u32[]{:S(2)}) collective-permute-start(f32[1,64,128]{2,1,0:T(8,128)} %param.7), channel_id=1, source_target_pairs={{0,1},{1,0},{2,3},{3,2},{4,5},{5,4},{6,7},{7,6},{8,9},{9,8},{10,11... | collective-permute-start | bytes 98312 | tf_op jit(solution)/shard_map/ppermute | solution.py:379
  0.5 5.4 %copy-start.2 = (bf16[8,1,3,3,3]{0,4,3,2,1:T(4,128)(2,1)S(1)}, bf16[8,1,3,3,3]{0,4,3,2,1:T(4,128)(2,1)}, u32[]{:S(2)}) copy-start(bf16[8,1,3,3,3]{0,4,3,2,1:T(4,128)(2,1)} %param.8) | copy-start | bytes 1300
  1.2 4.6 %copy-start = (bf16[8,8,3,3,3]{1,0,4,3,2:T(8,128)(2,1)S(1)}, bf16[8,8,3,3,3]{1,0,4,3,2:T(8,128)(2,1)}, u32[]{:S(2)}) copy-start(bf16[8,8,3,3,3]{1,0,4,3,2:T(8,128)(2,1)} %param.10) | copy-start | bytes 10372
  1.2 4.6 %copy-start.1 = (bf16[16,8,3,3,3]{0,1,4,3,2:T(8,128)(2,1)S(1)}, bf16[16,8,3,3,3]{0,1,4,3,2:T(8,128)(2,1)}, u32[]{:S(2)}) copy-start(bf16[16,8,3,3,3]{0,1,4,3,2:T(8,128)(2,1)} %param.12) | copy-start | bytes 20740
  1.7 4.2 %collective-permute-start.3 = (bf16[2,40,128]{2,1,0:T(8,128)(2,1)S(1)}, bf16[2,40,128]{2,1,0:T(8,128)(2,1)S(1)}, u32[]{:S(2)}, u32[]{:S(2)}) collective-permute-start(bf16[2,40,128]{2,1,0:T(8,128)(2,1)S(1)} %get-tuple-element.32), channel_id=1, source_target_pairs={{0,5},{1,3},{2,7},{3,1},{4,9},{5,0},{6,11},{7,2},{8,13},{9,4},{10,... | collective-permute-start | bytes 61448 | tf_op jit(solution)/shard_map/ppermute | solution.py:390
  4.3 4.1 %collective-permute-start.2 = (bf16[2,40,128]{2,1,0:T(8,128)(2,1)S(1)}, bf16[2,40,128]{2,1,0:T(8,128)(2,1)S(1)}, u32[]{:S(2)}, u32[]{:S(2)}) collective-permute-start(bf16[2,40,128]{2,1,0:T(8,128)(2,1)S(1)} %get-tuple-element.31), channel_id=1, source_target_pairs={{0,7},{1,3},{2,5},{3,1},{4,11},{5,2},{6,9},{7,0},{8,15},{9,6},{10,... | collective-permute-start | bytes 61448 | tf_op jit(solution)/shard_map/ppermute | solution.py:391
  5.8 3.2 %collective-permute-start.1 = (bf16[2,40,128]{2,1,0:T(8,128)(2,1)S(1)}, bf16[2,40,128]{2,1,0:T(8,128)(2,1)S(1)}, u32[]{:S(2)}, u32[]{:S(2)}) collective-permute-start(bf16[2,40,128]{2,1,0:T(8,128)(2,1)S(1)} %get-tuple-element.31), channel_id=1, source_target_pairs={{0,3},{1,2},{2,1},{3,0},{4,7},{5,6},{6,5},{7,4},{8,11},{9,10},{10,... | collective-permute-start | bytes 61448 | tf_op jit(solution)/shard_map/ppermute | solution.py:392
  5.8 0.7 %copy-start.3 = (f32[8]{0:T(128)S(1)}, f32[8]{0:T(128)}, u32[]{:S(2)}) copy-start(f32[8]{0:T(128)} %param.9) | copy-start | bytes 100
  5.8 0.7 %copy-start.4 = (f32[8]{0:T(128)S(1)}, f32[8]{0:T(128)}, u32[]{:S(2)}) copy-start(f32[8]{0:T(128)} %param.11) | copy-start | bytes 100
  5.8 0.7 %copy-start.5 = (f32[16]{0:T(128)S(1)}, f32[16]{0:T(128)}, u32[]{:S(2)}) copy-start(f32[16]{0:T(128)} %param.13) | copy-start | bytes 196
  8.5 1.3 %collective-permute-start.4 = (bf16[3,40,128]{2,1,0:T(8,128)(2,1)S(1)}, bf16[3,40,128]{2,1,0:T(8,128)(2,1)S(1)}, u32[]{:S(2)}, u32[]{:S(2)}) collective-permute-start(bf16[3,40,128]{2,1,0:T(8,128)(2,1)S(1)} %fusion.1.got), channel_id=1, source_target_pairs={{0,1},{1,0},{2,3},{3,2},{4,5},{5,4},{6,7},{7,6},{8,9},{9,8},{10,11... | collective-permute-start | bytes 92168 | tf_op jit(solution)/shard_map/ppermute | solution.py:435
